TPU v7x, 32 devices: a whole 2x2x4 slice. The times are simulated.
32 devices in a mesh: pair: 8 (over z, core), rows: 4 (over y, x).
Axes of the slice: x: 2, y: 2, z: 4, core: 2. Of those that a mesh axis runs over, the one named last changes fastest.
Arguments:
- matrix: float32 [2048, 8192], P(('rows', 'pair')), may hold values from -6 to 6
- plan: int32 [16], replicated, may hold values from 0 to 15, each once
Outputs:
- rotated: float32 [2048, 8192], P('rows', 'pair')
Inputs may be any that keep to these rules, and one draw needn't show every extreme that they name: `plan`: each block number appears once.
All inputs are finite; a program needn't handle non-finite values.
Results may differ from a plain program's by a relative error of at most 0.0003.
Values sent between devices are 32-bit elements; how exact they have to be, the bound alone decides.
No kernel may reach another device: no remote copies, remote signals or barrier semaphores. Data moves between devices by JAX's collectives and lax.ppermute only.
A program may use at most 64 MiB of HBM per device.

v0:
```python
import functools

import jax
import jax.numpy as jnp
from jax import lax
from jax.experimental import pallas as pl
from jax.experimental.pallas import tpu as pltpu
from jax.sharding import PartitionSpec as P

BLK = 512
TILE = 128
SPAN = 256

epsilon = 1e-06
f32 = jnp.float32
bf16 = jnp.bfloat16
VMEM = pl.BlockSpec(memory_space=pltpu.VMEM)
SMEM = pl.BlockSpec(memory_space=pltpu.SMEM)
ANY = pl.BlockSpec(memory_space=pl.ANY)

CHUNKS = ((0, 0, 512), (1, 0, 256), (1, 256, 256))


def shape(dims, dtype=f32):
    return jax.ShapeDtypeStruct(dims, dtype)


def params(mib):
    return pltpu.CompilerParams(vmem_limit_bytes=mib * 1024 * 1024)


def cost(macs, moved):
    return pl.CostEstimate(flops=int(macs) // 64, bytes_accessed=int(moved) // 64, transcendentals=0)


def halves(value):
    top = value.astype(bf16)
    return top, (value - top.astype(f32)).astype(bf16)


def dot(left, right):
    return lax.dot_general(left, right, (((1,), (0,)), ((), ())), preferred_element_type=f32)


def dot_t(left, right):
    return lax.dot_general(left, right, (((0,), (0,)), ((), ())), preferred_element_type=f32)


def three(op, left, right):
    (lh, ll), (rh, rl) = left, right
    return op(lh, rl) + op(ll, rh) + op(lh, rh)


def triangle(first, count):
    return [(first + i, first + j) for i in range(count) for j in range(i + 1)]


ROUNDS = ((0, 1), (2,))


def round_tiles(index):
    return [tile for chunk in ROUNDS[index] for tile in chunk_tiles(chunk)]


def chunk_tiles(index):
    base = [0]
    for _, _, width in CHUNKS:
        base.append(base[-1] + width // TILE)
    lo, hi = base[index], base[index + 1]
    return [(i, j) for i in range(lo, hi) for j in range(lo)] + triangle(lo, hi - lo)


def pick_kernel(plan_ref, matrix, near, own_q, *rest):
    own_s, sems = rest[:-1], rest[-1]
    me = lax.axis_index("pair")
    hops = len(own_s)
    copies = []
    for k in range(hops):
        for other in (1, 0):
            pair = jnp.bitwise_xor(lax.rem(me + 2 * k, 2 * hops), other)
            flip = jnp.where((lax.rem(pair, 2) == 0) & (pair > 0), 1, 0)
            for which in (0, 1):
                block = plan_ref[2 * pair + (flip if which == 0 else 1 - flip)]
                source = matrix.at[:, pl.ds(pl.multiple_of(block * BLK, BLK), BLK)]
                if other:
                    target = near.at[which, k]
                elif which:
                    target = own_q.at[k]
                else:
                    target = own_s[k]
                copies.append(pltpu.make_async_copy(source, target, sems.at[len(copies)]))
                copies[-1].start()
    for copy in copies:
        copy.wait()


def pick(matrix, plan, pairs):
    rows = matrix.shape[0]
    hops = pairs // 2
    outs = [shape((2, hops, rows, BLK)), shape((hops, rows, BLK))] + [shape((rows, BLK))] * hops
    near, own_q, *own_s = pl.pallas_call(
        pick_kernel,
        out_shape=outs,
        in_specs=[SMEM, pl.BlockSpec(memory_space=pltpu.HBM)],
        out_specs=[VMEM] * len(outs),
        scratch_shapes=[pltpu.SemaphoreType.DMA((4 * hops,))],
        compiler_params=params(48),
        name="pick",
    )(plan, matrix)
    return near, own_q, own_s


def merge_kernel(near, own_q, *outs):
    core = lax.rem(lax.axis_index("pair"), 2)
    hops, rows, _ = own_q.shape
    forward, queues = outs[:hops], outs[hops:]
    mine = pl.multiple_of(core * rows, rows)
    theirs = pl.multiple_of((1 - core) * rows, rows)
    for k in range(hops):
        forward[k][...] = near[0, k]
        for c, (_, start, width) in enumerate(CHUNKS[1:]):
            out = queues[c * hops + k]
            out[pl.ds(mine, rows), :] = own_q[k, :, start : start + width]
            out[pl.ds(theirs, rows), :] = near[1, k, :, start : start + width]


def merge(near, own_q):
    hops, rows, _ = own_q.shape
    outs = [shape((rows, BLK))] * hops
    outs += [shape((2 * rows, w)) for _, _, w in CHUNKS[1:] for _ in range(hops)]
    flat = pl.pallas_call(
        merge_kernel,
        out_shape=outs,
        in_specs=[VMEM] * 2,
        out_specs=[VMEM] * len(outs),
        compiler_params=params(16),
        name="merge",
    )(near, own_q)
    return [flat[i : i + hops] for i in range(0, len(flat), hops)]


def paths(groups):
    row = lax.axis_index("rows")
    if groups != 4:
        return [jnp.bitwise_xor(row, d) for d in range(groups)]
    x, y = lax.rem(row, 2), lax.div(row, 2)
    return [x, 1 - x, 2 + y, 3 - y]


def part_shapes(n, groups):
    return [shape((n, TILE // groups, TILE))] * groups


def spread_tiles(packed, outs, groups):
    size = TILE // groups
    for out, k in zip(outs, paths(groups)):
        out[...] = packed[:, pl.ds(pl.multiple_of(k * size, size), size), :]


def gram_kernel(pairs, index, groups, counts, *refs):
    refs = list(refs)
    packed = refs.pop()
    n_prev, n_new = ROUNDS[index][0], len(ROUNDS[index])
    split = [tuple(refs[2 * k : 2 * k + 2]) for k in range(n_prev)]
    del refs[: 2 * n_prev]
    outs = refs[-groups:]
    new = [tuple(refs[2 * k - 2 * n_new - groups :][:2]) for k in range(n_new)]
    me = lax.axis_index("pair")
    core = lax.rem(me, 2)
    hops = pairs // 2
    for (top, low), count in zip(new, counts):
        pieces = refs[:count]
        del refs[:count]
        rows = top.shape[0] // pairs
        for k in range(hops):
            start = lax.rem(me // 2 + hops - k, hops) * (2 * rows)
            if count == hops:
                parts = [(pieces[k], start, 2 * rows)]
            else:
                parts = [(pieces[k], start + core * rows, rows), (pieces[hops + k], start + (1 - core) * rows, rows)]
            for piece, at, size in parts:
                here = pl.ds(pl.multiple_of(at, rows), size)
                top[here, :], low[here, :] = halves(piece[...])
    split += new
    blocks, first = [], 0
    for both in split:
        blocks += [(both, j, first + j) for j in range(0, both[0].shape[1], SPAN)]
        first += both[0].shape[1]
    place = {t: k for k, t in enumerate(round_tiles(index))}
    base = sum(w for _, _, w in CHUNKS[:n_prev])
    for (th, tl), i, row in blocks:
        if row < base:
            continue
        left = (th[:, i : i + SPAN], tl[:, i : i + SPAN])
        for (uh, ul), j, col in blocks:
            if col > row:
                continue
            full = three(dot_t, left, (uh[:, j : j + SPAN], ul[:, j : j + SPAN]))
            for a in range(0, SPAN, TILE):
                for b in range(0, SPAN, TILE):
                    key = ((row + a) // TILE, (col + b) // TILE)
                    if key in place:
                        packed[place[key]] = full[a : a + TILE, b : b + TILE]
    spread_tiles(packed, outs, groups)


def gram(arrays, prev, index, pairs):
    widths = [pieces[0].shape[1] for pieces in arrays]
    rows = arrays[0][0].shape[0] * len(arrays[0])
    n = len(round_tiles(index))
    groups = lax.axis_size("rows")
    flat = [h for both in prev for h in both] + [p for pieces in arrays for p in pieces]
    outs = [shape((rows, w), bf16) for w in widths for _ in (0, 1)] + part_shapes(n, groups)
    out = pl.pallas_call(
        functools.partial(gram_kernel, pairs, index, groups, [len(pieces) for pieces in arrays]),
        out_shape=outs,
        in_specs=[VMEM] * len(flat),
        out_specs=[VMEM] * len(outs),
        scratch_shapes=[pltpu.VMEM((n, TILE, TILE), f32)],
        compiler_params=params(20),
        cost_estimate=cost(10000 * n * TILE * TILE * rows, 8 * rows * sum(widths)),
        name="gram" + str(index),
    )(*flat)
    n_new = len(widths)
    return [(out[2 * k], out[2 * k + 1]) for k in range(n_new)], out[2 * n_new :]


def flip_rows(x, mask):
    return lax.ppermute(x, "rows", [(i, i ^ mask) for i in range(lax.axis_size("rows"))])


def sum_first(parts):
    if len(parts) != 4:
        return [flip_rows(parts[d], d) for d in range(1, len(parts))]
    return [flip_rows(parts[1], 1), flip_rows(parts[3], 2)]


def sum_second(parts, got, gate):
    if len(parts) != 4:
        return [sum(got, parts[0])]
    mine = after([parts[0] + got[0], parts[2] + got[1]], gate)
    return [mine[0] + flip_rows(mine[0], 2), mine[1] + flip_rows(mine[1], 1)]


def sum_spread(done):
    if len(done) == 1:
        return done + [flip_rows(done[0], d) for d in range(1, lax.axis_size("rows"))]
    return [done[0], flip_rows(done[0], 1), done[1], flip_rows(done[1], 2)]


def sum_rows(parts):
    return sum_spread(sum_second(parts, sum_first(parts), []))


def swap_near(x, pairs):
    return lax.ppermute(x, "pair", [(i, i ^ 1) for i in range(pairs)])


def swap_far(x, pairs):
    ends = [(0, 0), (pairs - 1, pairs - 1)]
    return lax.ppermute(x, "pair", ends + [(i, ((i + 1) ^ 1) - 1) for i in range(1, pairs - 1)])


def newton_kernel(tile_lists, whole_lists, n_columns, last, *refs):
    refs = list(refs)

    def take(n):
        got = refs[:n]
        del refs[:n]
        return got

    places = paths(lax.axis_size("rows"))
    groups = [take(len(places)) for _ in tile_lists]
    wholes = take(len(whole_lists))
    columns = [take(2) for _ in range(n_columns)]
    out_s, plain_q, w_hi, w_lo, b_hi, b_lo, f_ref = take(7)
    extra = [] if last else take(5)
    n_hi, n_lo, a_hi, a_lo = take(4) if last else extra[:4]
    tile_ref = refs[0]
    width = n_hi.shape[0]
    count = width // TILE
    row = lax.axis_index("rows")
    x_flip, y_flip = lax.rem(row, 2) == 1, lax.div(row, 2) == 1

    def load(parts, t):
        if len(parts) != 4:
            for part, place in zip(parts, places):
                size = part.shape[1]
                tile_ref[pl.ds(pl.multiple_of(place * size, size), size), :] = part[t]
            return tile_ref[...]
        one, two, three_, four = (part[t] for part in parts)
        rows_ = [jnp.where(x_flip, two, one), jnp.where(x_flip, one, two)]
        rows_ += [jnp.where(y_flip, four, three_), jnp.where(y_flip, three_, four)]
        return jnp.concatenate(rows_, axis=0)

    source = {}
    for tiles, parts in zip(tile_lists, groups):
        for t, key in enumerate(tiles):
            source[key] = functools.partial(load, parts, t)
    for tiles, part in zip(whole_lists, wholes):
        for t, key in enumerate(tiles):
            source[key] = functools.partial(lambda ref, k: ref[k], part, t)

    eye = lax.broadcasted_iota(jnp.int32, (TILE, TILE), 0) == lax.broadcasted_iota(jnp.int32, (TILE, TILE), 1)
    along, down = [], []
    for i in range(count):
        own = jnp.where(eye, source[i, i](), 0.0)
        along.append(jnp.sum(own, axis=0, keepdims=True) + epsilon)
        down.append(jnp.sum(own, axis=1, keepdims=True) + epsilon)
    d_row = jnp.concatenate(along, axis=1)
    s_row = lax.rsqrt(d_row)
    s_col = [lax.rsqrt(v) for v in down]
    square = jnp.zeros((TILE, TILE), f32)
    for (i, j), get in source.items():
        at, to = slice(i * TILE, (i + 1) * TILE), slice(j * TILE, (j + 1) * TILE)
        normed = get() * s_col[i] * s_row[:, to]
        n_hi[at, to], n_lo[at, to] = halves(normed)
        if i == j:
            square = square + normed * normed
        else:
            square = square + 2.0 * (normed * normed)
            n_hi[to, at], n_lo[to, at] = halves(normed.T)
    square = jnp.sum(square, axis=0, keepdims=True)
    spread = jnp.full((1, 1), 1.5, f32) * jnp.sqrt(jnp.sum(square, axis=1, keepdims=True) / width)
    inverse = 1.0 / spread
    factor = 0.0625 * jnp.sqrt(d_row) * lax.rsqrt(spread)

    for i in range(0, width, SPAN):
        band = slice(i, i + SPAN)
        product = three(dot, (n_hi[band, :], n_lo[band, :]), (n_hi[...], n_lo[...]))
        scaled = (n_hi[band, :].astype(f32) + n_lo[band, :].astype(f32)) * inverse
        product = product * (inverse * inverse)
        here = lax.broadcasted_iota(jnp.int32, (SPAN, width), 0) + i == lax.broadcasted_iota(jnp.int32, (SPAN, width), 1)
        weight = jnp.concatenate(s_col[i // TILE : (i + SPAN) // TILE], axis=0)
        a_hi[band, :], a_lo[band, :] = halves((product - 3.0 * scaled + jnp.where(here, 4.0, 0.0)) * weight)
        b_hi[band, :], b_lo[band, :] = halves(product - 6.0 * scaled + jnp.where(here, 5.0, 0.0))

    rows = w_hi.shape[0]

    def wide(k, band):
        return jnp.concatenate([both[k][band, :] for both in columns], axis=1)

    for i in range(0, rows, SPAN):
        band = slice(i, i + SPAN)
        value = three(dot, (wide(0, band), wide(1, band)), (a_hi[...], a_lo[...]))
        w_hi[band, :], w_lo[band, :] = halves(value)

    f_ref[...] = factor
    if last:
        s_at, q_at = ends()
    else:
        s_at, q_at = 0, BLK
        extra[4][...] = d_row
    for i in range(0, rows, SPAN):
        band = slice(i, i + SPAN)
        cols = pl.ds(s_at, BLK)
        value = three(dot, (w_hi[band, :], w_lo[band, :]), (b_hi[:, cols], b_lo[:, cols]))
        plain = wide(0, band).astype(f32) + wide(1, band).astype(f32)
        plain = plain * (16.0 * s_row * factor)
        if last:
            swapped = lax.axis_index("pair") == 0
            left, right, f_left, f_right = plain[:, :BLK], plain[:, BLK:], factor[:, :BLK], factor[:, BLK:]
            out_s[band, :] = value * jnp.where(swapped, f_right, f_left) + jnp.where(swapped, right, left)
            plain_q[band, :] = jnp.where(swapped, left, right)
        else:
            out_s[band, :] = value * factor[:, :BLK] + plain[:, :BLK]
            plain_q[band, :] = plain[:, BLK:]


def ends():
    swapped = lax.axis_index("pair") == 0
    return pl.multiple_of(jnp.where(swapped, BLK, 0), BLK), pl.multiple_of(jnp.where(swapped, 0, BLK), BLK)


def rest_kernel(last, plain_q, w_hi, w_lo, b_hi, b_lo, f_ref, out_q):
    cols = pl.ds(ends()[1] if last else BLK, BLK)
    factor = f_ref[...][:, BLK:]
    if last:
        factor = jnp.where(lax.axis_index("pair") == 0, f_ref[...][:, :BLK], factor)
    for i in range(0, plain_q.shape[0], SPAN):
        band = slice(i, i + SPAN)
        value = three(dot, (w_hi[band, :], w_lo[band, :]), (b_hi[:, cols], b_lo[:, cols]))
        out_q[band, :] = value * factor + plain_q[band, :]


def rest(held, last):
    rows, width = held[1].shape
    return pl.pallas_call(
        functools.partial(rest_kernel, last),
        out_shape=shape((rows, BLK)),
        in_specs=[VMEM] * 6,
        out_specs=VMEM,
        compiler_params=params(12),
        cost_estimate=cost(3000 * rows * width * BLK, 8 * rows * width),
        name="rest",
    )(*held)


def newton(tile_lists, whole_lists, groups, wholes, columns, last):
    rows = columns[0][0].shape[0]
    width = sum(hi.shape[1] for hi, _ in columns)
    flat = [p for parts in groups for p in parts] + list(wholes) + [h for both in columns for h in both]
    square = [shape((width, width), bf16)] * 4
    tall = [shape((rows, width), bf16)] * 2
    outs = [shape((rows, BLK))] * 2 + tall + square[:2] + [shape((1, width))]
    outs += [] if last else square + [shape((1, width))]
    scratch = [pltpu.VMEM((width, width), bf16)] * 4 if last else []
    scratch += [pltpu.VMEM((TILE, TILE), f32)]
    return pl.pallas_call(
        functools.partial(newton_kernel, tile_lists, whole_lists, len(columns), last),
        out_shape=outs,
        in_specs=[VMEM] * len(flat),
        out_specs=[VMEM] * len(outs),
        scratch_shapes=scratch,
        compiler_params=params(28),
        cost_estimate=cost(3 * (width**3 + 1.5 * rows * width**2), 16 * width**2),
        name="newton",
    )(*flat)


def flip_line(row):
    eye = lax.broadcasted_iota(jnp.int32, (TILE, TILE), 0) == lax.broadcasted_iota(jnp.int32, (TILE, TILE), 1)
    parts = [jnp.where(eye, row[:, i : i + TILE], 0.0) for i in range(0, row.shape[1], TILE)]
    return [jnp.sum(part, axis=1, keepdims=True) for part in parts]


def power_kernel(n_hi, n_lo, a_hi, a_lo, b_hi, b_lo, d_ref, p_hi, p_lo, t_hi, t_lo):
    width = n_hi.shape[0]
    d_col = flip_line(d_ref[...])
    for i in range(0, width, SPAN):
        band = slice(i, i + SPAN)
        here = lax.broadcasted_iota(jnp.int32, (SPAN, width), 0) + i == lax.broadcasted_iota(jnp.int32, (SPAN, width), 1)
        root = jnp.sqrt(jnp.concatenate(d_col[i // TILE : (i + SPAN) // TILE], axis=0))
        value = three(dot, (a_hi[band, :], a_lo[band, :]), (b_hi[...], b_lo[...]))
        p_hi[band, :], p_lo[band, :] = halves(value * (0.125 * root) + jnp.where(here, 2.0, 0.0))
    for i in range(0, width, SPAN):
        band = slice(i, i + SPAN)
        value = three(dot, (n_hi[band, :], n_lo[band, :]), (p_hi[...], p_lo[...]))
        t_hi[band, :], t_lo[band, :] = halves(value)


def powers(n_hi, n_lo, a_hi, a_lo, b_hi, b_lo, d_row):
    width = n_hi.shape[0]
    return pl.pallas_call(
        power_kernel,
        out_shape=[shape((width, width), bf16)] * 4,
        in_specs=[VMEM] * 7,
        out_specs=[VMEM] * 4,
        compiler_params=params(24),
        cost_estimate=cost(3 * 2 * width**3, 16 * width**2),
        name="powers",
    )(n_hi, n_lo, a_hi, a_lo, b_hi, b_lo, d_row)


def next_kernel(p_hi, p_lo, t_hi, t_lo, f_ref, s_out, q_out):
    f_row = f_ref[...] * 8.0
    f_col = flip_line(f_row)
    for out, base in ((s_out, 0), (q_out, BLK)):
        place = {t: k for k, t in enumerate(triangle(0, BLK // TILE))}
        for i in range(base, base + BLK, SPAN):
            cols = slice(base, i + SPAN)
            full = three(dot, (p_hi[i : i + SPAN, :], p_lo[i : i + SPAN, :]), (t_hi[:, cols], t_lo[:, cols]))
            for at in range(i, i + SPAN, TILE):
                for j in range(base, at + TILE, TILE):
                    tile = full[at - i : at - i + TILE, j - base : j - base + TILE]
                    tile = tile * f_col[at // TILE] * f_row[:, j : j + TILE]
                    out[place[((at - base) // TILE, (j - base) // TILE)]] = tile


def next_grams(p_hi, p_lo, t_hi, t_lo, f_row):
    width = p_hi.shape[0]
    n = len(triangle(0, BLK // TILE))
    return pl.pallas_call(
        next_kernel,
        out_shape=[shape((n, TILE, TILE))] * 2,
        in_specs=[VMEM] * 5,
        out_specs=[VMEM] * 2,
        compiler_params=params(16),
        cost_estimate=cost(3 * 0.5 * width**3, 8 * width**2),
        name="next_grams",
    )(p_hi, p_lo, t_hi, t_lo, f_row)


def cross_kernel(groups, near, far, near_hi, near_lo, far_hi, far_lo, *rest):
    outs, packed = rest[:-1], rest[-1]
    near_hi[...], near_lo[...] = halves(near[...])
    far_hi[...], far_lo[...] = halves(far[...])
    count = BLK // TILE
    for i in range(0, BLK, SPAN):
        left = (far_hi[:, i : i + SPAN], far_lo[:, i : i + SPAN])
        full = three(dot_t, left, (near_hi[...], near_lo[...]))
        for a in range(0, SPAN, TILE):
            for b in range(0, BLK, TILE):
                packed[(i + a) // TILE * count + b // TILE] = full[a : a + TILE, b : b + TILE]
    spread_tiles(packed, outs, groups)


def cross(near, far):
    rows = near.shape[0]
    n = (BLK // TILE) ** 2
    groups = lax.axis_size("rows")
    outs = [shape((rows, BLK), bf16)] * 4 + part_shapes(n, groups)
    out = pl.pallas_call(
        functools.partial(cross_kernel, groups),
        out_shape=outs,
        in_specs=[VMEM] * 2,
        out_specs=[VMEM] * len(outs),
        scratch_shapes=[pltpu.VMEM((n, TILE, TILE), f32)],
        compiler_params=params(16),
        cost_estimate=cost(3 * rows * BLK * BLK, 16 * rows * BLK),
        name="cross",
    )(near, far)
    return (out[0], out[1]), (out[2], out[3]), out[4:]


def around(x, pairs, hop):
    return lax.ppermute(x, "pair", [(i, (i + 2 * hop) % pairs) for i in range(pairs)])


def after(values, first):
    return lax.optimization_barrier((values, first))[0]


def place_kernel(first, block, kept, out, sem):
    core = lax.rem(lax.axis_index("pair"), 2)
    at = core if first else 1 - core
    half = pl.ds(pl.multiple_of((1 - at) * BLK, BLK), BLK)
    copy = pltpu.make_async_copy(block, out.at[:, half], sem)
    copy.start()
    copy.wait()


def place(block, out):
    first = out is None
    rows = block.shape[0]
    call = pl.pallas_call(
        functools.partial(place_kernel, first),
        out_shape=shape((rows, 2 * BLK)),
        in_specs=[VMEM, SMEM if first else ANY],
        out_specs=ANY,
        scratch_shapes=[pltpu.SemaphoreType.DMA],
        input_output_aliases={} if first else {1: 0},
        compiler_params=params(16),
        name="place",
    )
    return call(block, jnp.zeros((1,), f32) if first else out)


def per_device(matrix, plan):
    pairs = lax.axis_size("pair")
    hops = pairs // 2
    near, own_q, own_s = pick(matrix, plan, pairs)
    near = swap_near(near, pairs)
    s_mine = [own_s[0]] + [around(own_s[k], pairs, k) for k in range(1, hops)]
    forward, *queues = merge(near, own_q)
    s_theirs = [forward[0]] + [around(forward[k], pairs, k) for k in range(1, hops)]
    arrived = [s_mine + s_theirs]
    gate = [s_mine, s_theirs[1]]
    columns, groups = [], []
    done, spread = [], []
    for index, chunks in enumerate(ROUNDS):
        for chunk in chunks:
            if chunk:
                queue = after(queues[chunk - 1], gate)
                arrived.append([queue[0]] + [around(queue[k], pairs, k) for k in range(1, hops)])
        both, parts = gram([arrived[chunk] for chunk in chunks], columns, index, pairs)
        columns += both
        gate = parts
        got = sum_first(parts)
        done = after(sum_second(parts, got, done), spread)
        spread = sum_spread(done)
        groups.append(spread)
    tiles = [round_tiles(k) for k in range(len(ROUNDS))]
    out_s, *held = newton(tiles, [], groups, [], columns, False)
    held, (n_hi, n_lo, a_hi, a_lo, d_row) = held[:6], held[6:]
    far = swap_far(out_s, pairs)
    near = swap_near(rest(held, False), pairs)
    power = powers(n_hi, n_lo, a_hi, a_lo, held[3], held[4], d_row)
    near, far = after((near, far), power)
    near_pair, far_pair, parts = cross(near, far)
    s_gram, q_gram = next_grams(*after(power, parts), held[5])
    far_gram = swap_far(s_gram, pairs)
    near_gram = swap_near(q_gram, pairs)
    summed = sum_rows(parts)
    count = BLK // TILE
    crossing = [(count + i, j) for i in range(count) for j in range(count)]
    out_s, *held = newton(
        [crossing],
        [triangle(0, count), triangle(count, count)],
        [summed],
        [near_gram, far_gram],
        [near_pair, far_pair],
        True,
    )
    far = swap_far(out_s, pairs)
    near = swap_near(rest(held, True), pairs)
    return place(far, place(near, None))


def solution(mesh):
    placed = (P(("rows", "pair"), None), P())
    return jax.shard_map(
        per_device, mesh=mesh, in_specs=placed, out_specs=P("rows", "pair"), check_vma=False
    )
```

profile of v0, /device:TPU:1, one launch (start us, length us, event | category | flops | bytes accessed | tf_op | source)
XLA Modules:
  0.0 182.9 jit_solution(12458501806933253962)
XLA Ops:
  0.0 1.6 copy-done
  3.6 2.7 %collective-permute-start = (f32[64,512]{1,0:T(8,128)S(1)}, f32[64,512]{1,0:T(8,128)S(1)}, u32[]{:S(2)}, u32[]{:S(2)}) collective-permute-start(f32[64,512]{1,0:T(8,128)S(1)} %get-tuple-element.95), channel_id=1, source_target_pairs={{0,8},{4,12},{8,16},{12,20},{16,24},{20,28},{24,0},{28,4},{1,9},{5... | collective-permute-start | bytes 393224 | tf_op jit(solution)/shard_map/ppermute | solution.py:517
  6.3 2.3 %collective-permute-start.1 = (f32[64,512]{1,0:T(8,128)S(1)}, f32[64,512]{1,0:T(8,128)S(1)}, u32[]{:S(2)}, u32[]{:S(2)}) collective-permute-start(f32[64,512]{1,0:T(8,128)S(1)} %get-tuple-element.96), channel_id=1, source_target_pairs={{0,16},{4,20},{8,24},{12,28},{16,0},{20,4},{24,8},{28,12},{1,17},{... | collective-permute-start | bytes 393224 | tf_op jit(solution)/shard_map/ppermute | solution.py:517
  13.4 4.7 %collective-permute-done.1.refs_2_ = f32[64,512]{1,0:T(8,128)S(1)} collective-permute-done((f32[64,512]{1,0:T(8,128)S(1)}, f32[64,512]{1,0:T(8,128)S(1)}, u32[]{:S(2)}, u32[]{:S(2)}) %collective-permute-start.1) | collective-permute-done | bytes 131104 | tf_op jit(solution)/shard_map/ppermute | solution.py:517
  18.2 2.5 %collective-permute-done.4.refs_5_ = f32[64,512]{1,0:T(8,128)S(1)} collective-permute-done((f32[64,512]{1,0:T(8,128)S(1)}, f32[64,512]{1,0:T(8,128)S(1)}, u32[]{:S(2)}, u32[]{:S(2)}) %collective-permute-start.4) | collective-permute-done | bytes 131104 | tf_op jit(solution)/shard_map/ppermute | solution.py:517
  20.7 6.7 %collective-permute-start.7 = (f32[128,256]{1,0:T(8,128)S(1)}, f32[128,256]{1,0:T(8,128)S(1)}, u32[]{:S(2)}, u32[]{:S(2)}) collective-permute-start(f32[128,256]{1,0:T(8,128)S(1)} %get-tuple-element.109), channel_id=1, source_target_pairs={{0,8},{4,12},{8,16},{12,20},{16,24},{20,28},{24,0},{28,4},{1,9},{5... | collective-permute-start | bytes 393224 | tf_op jit(solution)/shard_map/ppermute | solution.py:517
  27.4 1.9 %collective-permute-start.8 = (f32[128,256]{1,0:T(8,128)S(1)}, f32[128,256]{1,0:T(8,128)S(1)}, u32[]{:S(2)}, u32[]{:S(2)}) collective-permute-start(f32[128,256]{1,0:T(8,128)S(1)} %get-tuple-element.110), channel_id=1, source_target_pairs={{0,16},{4,20},{8,24},{12,28},{16,0},{20,4},{24,8},{28,12},{1,17},{... | collective-permute-start | bytes 393224 | tf_op jit(solution)/shard_map/ppermute | solution.py:517
  29.3 2.4 %collective-permute-start.9 = (f32[128,256]{1,0:T(8,128)S(1)}, f32[128,256]{1,0:T(8,128)S(1)}, u32[]{:S(2)}, u32[]{:S(2)}) collective-permute-start(f32[128,256]{1,0:T(8,128)S(1)} %get-tuple-element.111), channel_id=1, source_target_pairs={{0,24},{4,28},{8,0},{12,4},{16,8},{20,12},{24,16},{28,20},{1,25},{... | collective-permute-start | bytes 393224 | tf_op jit(solution)/shard_map/ppermute | solution.py:517
  32.0 8.4 %collective-permute-done.8.refs_10_ = f32[128,256]{1,0:T(8,128)S(1)} collective-permute-done((f32[128,256]{1,0:T(8,128)S(1)}, f32[128,256]{1,0:T(8,128)S(1)}, u32[]{:S(2)}, u32[]{:S(2)}) %collective-permute-start.8) | collective-permute-done | bytes 131104 | tf_op jit(solution)/shard_map/ppermute | solution.py:517
  40.5 1.9 %gram0.1 = (bf16[512,512]{1,0:T(8,128)(2,1)S(1)}, bf16[512,512]{1,0:T(8,128)(2,1)S(1)}, bf16[512,256]{1,0:T(8,128)(2,1)S(1)}, bf16[512,256]{1,0:T(8,128)(2,1)S(1...) custom-call(f32[64,512]{1,0:T(8,128)S(1)} %get-tuple-element.94.refs, ...), custom_call_target="tpu_custom_call" | custom-call | flops 27525120000 | bytes 49152 | tf_op jit(solution)/shard_map/gram0/pallas_call | solution.py:214
  44.9 3.1 %collective-permute-start.16 = (f32[128,256]{1,0:T(8,128)S(1)}, f32[128,256]{1,0:T(8,128)S(1)}, u32[]{:S(2)}, u32[]{:S(2)}) collective-permute-start(f32[128,256]{1,0:T(8,128)S(1)} %get-tuple-element.129), channel_id=1, source_target_pairs={{0,8},{4,12},{8,16},{12,20},{16,24},{20,28},{24,0},{28,4},{1,9},{5... | collective-permute-start | bytes 393224 | tf_op jit(solution)/shard_map/ppermute | solution.py:517
  48.5 1.6 collective-permute-start.18
  52.4 1.3 collective-permute-start.12
  54.2 4.0 %collective-permute-done.17.refs_6_ = f32[128,256]{1,0:T(8,128)S(1)} collective-permute-done((f32[128,256]{1,0:T(8,128)S(1)}, f32[128,256]{1,0:T(8,128)S(1)}, u32[]{:S(2)}, u32[]{:S(2)}) %collective-permute-start.17) | collective-permute-done | bytes 131104 | tf_op jit(solution)/shard_map/ppermute | solution.py:517
  62.6 4.9 %collective-permute-done.19 = f32[15,32,128]{2,1,0:T(8,128)S(1)} collective-permute-done((f32[15,32,128]{2,1,0:T(8,128)S(1)}, f32[15,32,128]{2,1,0:T(8,128)S(1)}, u32[]{:S(2)}, u32[]{:S(2)}) %collective-permute-start.19) | collective-permute-done | bytes 245792 | tf_op jit(solution)/shard_map/ppermute | solution.py:229
  68.5 9.9 %collective-permute-done.21 = f32[15,32,128]{2,1,0:T(8,128)S(1)} collective-permute-done((f32[15,32,128]{2,1,0:T(8,128)S(1)}, f32[15,32,128]{2,1,0:T(8,128)S(1)}, u32[]{:S(2)}, u32[]{:S(2)}) %collective-permute-start.21) | collective-permute-done | bytes 245792 | tf_op jit(solution)/shard_map/ppermute | solution.py:229
  78.5 1.7 collective-permute-done.22
  80.9 4.9 %collective-permute-done.23.refs_5_ = f32[15,32,128]{2,1,0:T(8,128)S(1)} collective-permute-done((f32[15,32,128]{2,1,0:T(8,128)S(1)}, f32[15,32,128]{2,1,0:T(8,128)S(1)}, u32[]{:S(2)}, u32[]{:S(2)}) %collective-permute-start.23) | collective-permute-done | bytes 245792 | tf_op jit(solution)/shard_map/ppermute | solution.py:229
  85.9 14.8 %newton.2 = (f32[512,512]{1,0:T(8,128)S(1)}, f32[512,512]{1,0:T(8,128)S(1)}, bf16[512,1024]{1,0:T(8,128)(2,1)S(1)}, bf16[512,1024]{1,0:T(8,128)(2,1)S(1)}, bf16[...) custom-call(f32[21,32,128]{2,1,0:T(8,128)S(1)} %add.38.refs_0_, ...), custom_call_target="tpu_custom_call" | custom-call | flops 88080384 | bytes 262144 | tf_op jit(solution)/shard_map/newton/pallas_call | solution.py:409
  100.7 1.9 %rest.2 = f32[512,512]{1,0:T(8,128)S(1)} custom-call(f32[512,512]{1,0:T(8,128)S(1)} %get-tuple-element.142.plain_q, bf16[512,1024]{1,0:T(8,128)(2,1)S(1)} %get-tuple-element.143.w_hi, bf16[512,1024]{1,0:T(8,128)(2,1)S(1)} %get-tuple-element.144.w_lo, bf16[1024,1024]{1,0:T(8,128)(2,1)S(1)} %get-tuple-element.145.b_hi, ...), custom_call_target="tpu_custom_call" | custom-call | flops 12582912000 | bytes 65536 | tf_op jit(solution)/shard_map/rest/pallas_call | solution.py:388
  102.5 3.3 %collective-permute-start.25 = (f32[512,512]{1,0:T(8,128)S(1)}, f32[512,512]{1,0:T(8,128)S(1)}, u32[]{:S(2)}, u32[]{:S(2)}) collective-permute-start(f32[512,512]{1,0:T(8,128)S(1)} %rest.2), channel_id=1, source_target_pairs={{0,4},{4,0},{8,12},{12,8},{16,20},{20,16},{24,28},{28,24},{1,5},{5... | collective-permute-start | bytes 3145736 | tf_op jit(solution)/shard_map/ppermute | solution.py:256
  105.8 4.9 %collective-permute-start.26 = (f32[512,512]{1,0:T(8,128)S(1)}, f32[512,512]{1,0:T(8,128)S(1)}, u32[]{:S(2)}, u32[]{:S(2)}) collective-permute-start(f32[512,512]{1,0:T(8,128)S(1)} %get-tuple-element.148), channel_id=1, source_target_pairs={{0,0},{28,28},{4,8},{8,4},{12,16},{16,12},{20,24},{24,20},{1,1},{2... | collective-permute-start | bytes 3145736 | tf_op jit(solution)/shard_map/ppermute | solution.py:261
  110.8 13.7 %powers.1 = (bf16[1024,1024]{1,0:T(8,128)(2,1)S(1)}, bf16[1024,1024]{1,0:T(8,128)(2,1)S(1)}, bf16[1024,1024]{1,0:T(8,128)(2,1)S(1)}, bf16[1024,1024]{1,0:T(8,128)(2,1)S(1)}) custom-call(bf16[1024,1024]{1,0:T(8,128)(2,1)S(1)} %get-tuple-element.149.n_hi, bf16[1024,1024]{1,0:T(8,128)(2,1)S(1)} %get-tuple-element.150.n_lo, ...), custom_call_target="tpu_custom_call" | custom-call | flops 100663296 | bytes 262144 | tf_op jit(solution)/shard_map/powers/pallas_call | solution.py:444
  127.3 2.8 %next_grams.1 = (f32[10,128,128]{2,1,0:T(8,128)S(1)}, f32[10,128,128]{2,1,0:T(8,128)S(1)}) custom-call(bf16[1024,1024]{1,0:T(8,128)(2,1)S(1)} %get-tuple-element.166.p_hi, bf16[1024,1024]{1,0:T(8,128)(2,1)S(1)} %get-tuple-element.167.p_lo, bf16[1024,1024]{1,0:T(8,128)(2,1)S(1)} %get-tuple-element.168.t_hi, bf16[1024,1024]{1,0:T(8,128)(2,1)S(1)} %get-tuple-element.169.t_lo, ...), custom_call_target="tpu_custom_call" | custom-call | flops 25165824 | bytes 131072 | tf_op jit(solution)/shard_map/next_grams/pallas_call | solution.py:473
  130.2 3.0 %collective-permute-start.34 = (f32[10,128,128]{2,1,0:T(8,128)S(1)}, f32[10,128,128]{2,1,0:T(8,128)S(1)}, u32[]{:S(2)}, u32[]{:S(2)}) collective-permute-start(f32[10,128,128]{2,1,0:T(8,128)S(1)} %get-tuple-element.171), channel_id=1, source_target_pairs={{0,0},{28,28},{4,8},{8,4},{12,16},{16,12},{20,24},{24,20},{1,1},{2... | collective-permute-start | bytes 1966088 | tf_op jit(solution)/shard_map/ppermute | solution.py:261
  134.8 5.6 %collective-permute-done.29 = f32[16,32,128]{2,1,0:T(8,128)S(1)} collective-permute-done((f32[16,32,128]{2,1,0:T(8,128)S(1)}, f32[16,32,128]{2,1,0:T(8,128)S(1)}, u32[]{:S(2)}, u32[]{:S(2)}) %collective-permute-start.29) | collective-permute-done | bytes 262176 | tf_op jit(solution)/shard_map/ppermute | solution.py:229
  142.1 6.2 %collective-permute-done.30.refs_1_ = f32[16,32,128]{2,1,0:T(8,128)S(1)} collective-permute-done((f32[16,32,128]{2,1,0:T(8,128)S(1)}, f32[16,32,128]{2,1,0:T(8,128)S(1)}, u32[]{:S(2)}, u32[]{:S(2)}) %collective-permute-start.30) | collective-permute-done | bytes 262176 | tf_op jit(solution)/shard_map/ppermute | solution.py:229
  148.3 1.4 collective-permute-done.32.refs_3_
  149.7 13.4 %newton.3 = (f32[512,512]{1,0:T(8,128)S(1)}, f32[512,512]{1,0:T(8,128)S(1)}, bf16[512,1024]{1,0:T(8,128)(2,1)S(1)}, bf16[512,1024]{1,0:T(8,128)(2,1)S(1)}, bf16[...) custom-call(f32[16,32,128]{2,1,0:T(8,128)S(1)} %add.46.refs_0_, ...), custom_call_target="tpu_custom_call" | custom-call | flops 88080384 | bytes 262144 | tf_op jit(solution)/shard_map/newton/pallas_call | solution.py:409
  163.1 1.8 %rest.3 = f32[512,512]{1,0:T(8,128)S(1)} custom-call(f32[512,512]{1,0:T(8,128)S(1)} %get-tuple-element.177.plain_q, bf16[512,1024]{1,0:T(8,128)(2,1)S(1)} %get-tuple-element.178.w_hi, bf16[512,1024]{1,0:T(8,128)(2,1)S(1)} %get-tuple-element.179.w_lo, bf16[1024,1024]{1,0:T(8,128)(2,1)S(1)} %get-tuple-element.180.b_hi, ...), custom_call_target="tpu_custom_call" | custom-call | flops 12582912000 | bytes 65536 | tf_op jit(solution)/shard_map/rest/pallas_call | solution.py:388
  165.6 2.7 %collective-permute-start.35 = (f32[512,512]{1,0:T(8,128)S(1)}, f32[512,512]{1,0:T(8,128)S(1)}, u32[]{:S(2)}, u32[]{:S(2)}) collective-permute-start(f32[512,512]{1,0:T(8,128)S(1)} %get-tuple-element.176), channel_id=1, source_target_pairs={{0,0},{28,28},{4,8},{8,4},{12,16},{16,12},{20,24},{24,20},{1,1},{2... | collective-permute-start | bytes 3145736 | tf_op jit(solution)/shard_map/ppermute | solution.py:261
  169.3 12.4 %collective-permute-done.35.block = f32[512,512]{1,0:T(8,128)S(1)} collective-permute-done((f32[512,512]{1,0:T(8,128)S(1)}, f32[512,512]{1,0:T(8,128)S(1)}, u32[]{:S(2)}, u32[]{:S(2)}) %collective-permute-start.35) | collective-permute-done | bytes 1048608 | tf_op jit(solution)/shard_map/ppermute | solution.py:261
  (71 shorter events, 27.9 us)
Async XLA Ops:
  3.6 8.6 %collective-permute-start = (f32[64,512]{1,0:T(8,128)S(1)}, f32[64,512]{1,0:T(8,128)S(1)}, u32[]{:S(2)}, u32[]{:S(2)}) collective-permute-start(f32[64,512]{1,0:T(8,128)S(1)} %get-tuple-element.95), channel_id=1, source_target_pairs={{0,8},{4,12},{8,16},{12,20},{16,24},{20,28},{24,0},{28,4},{1,9},{5... | collective-permute-start | bytes 393224 | tf_op jit(solution)/shard_map/ppermute | solution.py:517
  6.3 11.8 %collective-permute-start.1 = (f32[64,512]{1,0:T(8,128)S(1)}, f32[64,512]{1,0:T(8,128)S(1)}, u32[]{:S(2)}, u32[]{:S(2)}) collective-permute-start(f32[64,512]{1,0:T(8,128)S(1)} %get-tuple-element.96), channel_id=1, source_target_pairs={{0,16},{4,20},{8,24},{12,28},{16,0},{20,4},{24,8},{28,12},{1,17},{... | collective-permute-start | bytes 393224 | tf_op jit(solution)/shard_map/ppermute | solution.py:517
  8.6 9.5 %collective-permute-start.2 = (f32[64,512]{1,0:T(8,128)S(1)}, f32[64,512]{1,0:T(8,128)S(1)}, u32[]{:S(2)}, u32[]{:S(2)}) collective-permute-start(f32[64,512]{1,0:T(8,128)S(1)} %get-tuple-element.97), channel_id=1, source_target_pairs={{0,24},{4,28},{8,0},{12,4},{16,8},{20,12},{24,16},{28,20},{1,25},{... | collective-permute-start | bytes 393224 | tf_op jit(solution)/shard_map/ppermute | solution.py:517
  9.8 10.8 %collective-permute-start.4 = (f32[64,512]{1,0:T(8,128)S(1)}, f32[64,512]{1,0:T(8,128)S(1)}, u32[]{:S(2)}, u32[]{:S(2)}) collective-permute-start(f32[64,512]{1,0:T(8,128)S(1)} %get-tuple-element.101), channel_id=1, source_target_pairs={{0,8},{4,12},{8,16},{12,20},{16,24},{20,28},{24,0},{28,4},{1,9},{5... | collective-permute-start | bytes 393224 | tf_op jit(solution)/shard_map/ppermute | solution.py:517
  10.3 21.8 %collective-permute-start.5 = (f32[64,512]{1,0:T(8,128)S(1)}, f32[64,512]{1,0:T(8,128)S(1)}, u32[]{:S(2)}, u32[]{:S(2)}) collective-permute-start(f32[64,512]{1,0:T(8,128)S(1)} %get-tuple-element.102), channel_id=1, source_target_pairs={{0,16},{4,20},{8,24},{12,28},{16,0},{20,4},{24,8},{28,12},{1,17},{... | collective-permute-start | bytes 393224 | tf_op jit(solution)/shard_map/ppermute | solution.py:517
  12.2 19.8 %collective-permute-start.6 = (f32[64,512]{1,0:T(8,128)S(1)}, f32[64,512]{1,0:T(8,128)S(1)}, u32[]{:S(2)}, u32[]{:S(2)}) collective-permute-start(f32[64,512]{1,0:T(8,128)S(1)} %get-tuple-element.103), channel_id=1, source_target_pairs={{0,24},{4,28},{8,0},{12,4},{16,8},{20,12},{24,16},{28,20},{1,25},{... | collective-permute-start | bytes 393224 | tf_op jit(solution)/shard_map/ppermute | solution.py:517
  20.7 11.4 %collective-permute-start.7 = (f32[128,256]{1,0:T(8,128)S(1)}, f32[128,256]{1,0:T(8,128)S(1)}, u32[]{:S(2)}, u32[]{:S(2)}) collective-permute-start(f32[128,256]{1,0:T(8,128)S(1)} %get-tuple-element.109), channel_id=1, source_target_pairs={{0,8},{4,12},{8,16},{12,20},{16,24},{20,28},{24,0},{28,4},{1,9},{5... | collective-permute-start | bytes 393224 | tf_op jit(solution)/shard_map/ppermute | solution.py:517
  27.4 13.1 %collective-permute-start.8 = (f32[128,256]{1,0:T(8,128)S(1)}, f32[128,256]{1,0:T(8,128)S(1)}, u32[]{:S(2)}, u32[]{:S(2)}) collective-permute-start(f32[128,256]{1,0:T(8,128)S(1)} %get-tuple-element.110), channel_id=1, source_target_pairs={{0,16},{4,20},{8,24},{12,28},{16,0},{20,4},{24,8},{28,12},{1,17},{... | collective-permute-start | bytes 393224 | tf_op jit(solution)/shard_map/ppermute | solution.py:517
  29.3 11.2 %collective-permute-start.9 = (f32[128,256]{1,0:T(8,128)S(1)}, f32[128,256]{1,0:T(8,128)S(1)}, u32[]{:S(2)}, u32[]{:S(2)}) collective-permute-start(f32[128,256]{1,0:T(8,128)S(1)} %get-tuple-element.111), channel_id=1, source_target_pairs={{0,24},{4,28},{8,0},{12,4},{16,8},{20,12},{24,16},{28,20},{1,25},{... | collective-permute-start | bytes 393224 | tf_op jit(solution)/shard_map/ppermute | solution.py:517
  42.3 9.1 %collective-permute-start.10 = (f32[21,32,128]{2,1,0:T(8,128)S(1)}, f32[21,32,128]{2,1,0:T(8,128)S(1)}, u32[]{:S(2)}, u32[]{:S(2)}) collective-permute-start(f32[21,32,128]{2,1,0:T(8,128)S(1)} %get-tuple-element.113), channel_id=1, source_target_pairs={{0,1},{1,0},{2,3},{3,2},{4,5},{5,4},{6,7},{7,6},{8,9},{9,8},{10,11... | collective-permute-start | bytes 1032200 | tf_op jit(solution)/shard_map/ppermute | solution.py:229
  43.6 8.8 %collective-permute-start.11 = (f32[21,32,128]{2,1,0:T(8,128)S(1)}, f32[21,32,128]{2,1,0:T(8,128)S(1)}, u32[]{:S(2)}, u32[]{:S(2)}) collective-permute-start(f32[21,32,128]{2,1,0:T(8,128)S(1)} %get-tuple-element.115), channel_id=1, source_target_pairs={{0,2},{1,3},{2,0},{3,1},{4,6},{5,7},{6,4},{7,5},{8,10},{9,11},{10,... | collective-permute-start | bytes 1032200 | tf_op jit(solution)/shard_map/ppermute | solution.py:229
  44.9 9.3 %collective-permute-start.16 = (f32[128,256]{1,0:T(8,128)S(1)}, f32[128,256]{1,0:T(8,128)S(1)}, u32[]{:S(2)}, u32[]{:S(2)}) collective-permute-start(f32[128,256]{1,0:T(8,128)S(1)} %get-tuple-element.129), channel_id=1, source_target_pairs={{0,8},{4,12},{8,16},{12,20},{16,24},{20,28},{24,0},{28,4},{1,9},{5... | collective-permute-start | bytes 393224 | tf_op jit(solution)/shard_map/ppermute | solution.py:517
  47.9 10.2 %collective-permute-start.17 = (f32[128,256]{1,0:T(8,128)S(1)}, f32[128,256]{1,0:T(8,128)S(1)}, u32[]{:S(2)}, u32[]{:S(2)}) collective-permute-start(f32[128,256]{1,0:T(8,128)S(1)} %get-tuple-element.130), channel_id=1, source_target_pairs={{0,16},{4,20},{8,24},{12,28},{16,0},{20,4},{24,8},{28,12},{1,17},{... | collective-permute-start | bytes 393224 | tf_op jit(solution)/shard_map/ppermute | solution.py:517
  48.5 9.7 %collective-permute-start.18 = (f32[128,256]{1,0:T(8,128)S(1)}, f32[128,256]{1,0:T(8,128)S(1)}, u32[]{:S(2)}, u32[]{:S(2)}) collective-permute-start(f32[128,256]{1,0:T(8,128)S(1)} %get-tuple-element.131), channel_id=1, source_target_pairs={{0,24},{4,28},{8,0},{12,4},{16,8},{20,12},{24,16},{28,20},{1,25},{... | collective-permute-start | bytes 393224 | tf_op jit(solution)/shard_map/ppermute | solution.py:517
  52.4 7.9 %collective-permute-start.12 = (f32[21,32,128]{2,1,0:T(8,128)S(1)}, f32[21,32,128]{2,1,0:T(8,128)S(1)}, u32[]{:S(2)}, u32[]{:S(2)}) collective-permute-start(f32[21,32,128]{2,1,0:T(8,128)S(1)} %add.36), channel_id=1, source_target_pairs={{0,2},{1,3},{2,0},{3,1},{4,6},{5,7},{6,4},{7,5},{8,10},{9,11},{10,... | collective-permute-start | bytes 1032200 | tf_op jit(solution)/shard_map/ppermute | solution.py:229
  53.8 7.6 %collective-permute-start.13 = (f32[21,32,128]{2,1,0:T(8,128)S(1)}, f32[21,32,128]{2,1,0:T(8,128)S(1)}, u32[]{:S(2)}, u32[]{:S(2)}) collective-permute-start(f32[21,32,128]{2,1,0:T(8,128)S(1)} %add.37), channel_id=1, source_target_pairs={{0,1},{1,0},{2,3},{3,2},{4,5},{5,4},{6,7},{7,6},{8,9},{9,8},{10,11... | collective-permute-start | bytes 1032200 | tf_op jit(solution)/shard_map/ppermute | solution.py:229
  59.4 8.1 %collective-permute-start.19 = (f32[15,32,128]{2,1,0:T(8,128)S(1)}, f32[15,32,128]{2,1,0:T(8,128)S(1)}, u32[]{:S(2)}, u32[]{:S(2)}) collective-permute-start(f32[15,32,128]{2,1,0:T(8,128)S(1)} %get-tuple-element.133), channel_id=1, source_target_pairs={{0,1},{1,0},{2,3},{3,2},{4,5},{5,4},{6,7},{7,6},{8,9},{9,8},{10,11... | collective-permute-start | bytes 737288 | tf_op jit(solution)/shard_map/ppermute | solution.py:229
  59.7 7.8 %collective-permute-start.20 = (f32[15,32,128]{2,1,0:T(8,128)S(1)}, f32[15,32,128]{2,1,0:T(8,128)S(1)}, u32[]{:S(2)}, u32[]{:S(2)}) collective-permute-start(f32[15,32,128]{2,1,0:T(8,128)S(1)} %get-tuple-element.135), channel_id=1, source_target_pairs={{0,2},{1,3},{2,0},{3,1},{4,6},{5,7},{6,4},{7,5},{8,10},{9,11},{10,... | collective-permute-start | bytes 737288 | tf_op jit(solution)/shard_map/ppermute | solution.py:229
  61.4 18.8 %collective-permute-start.14 = (f32[21,32,128]{2,1,0:T(8,128)S(1)}, f32[21,32,128]{2,1,0:T(8,128)S(1)}, u32[]{:S(2)}, u32[]{:S(2)}) collective-permute-start(f32[21,32,128]{2,1,0:T(8,128)S(1)} %add.38.refs_0_), channel_id=1, source_target_pairs={{0,1},{1,0},{2,3},{3,2},{4,5},{5,4},{6,7},{7,6},{8,9},{9,8},{10,11... | collective-permute-start | bytes 1032200 | tf_op jit(solution)/shard_map/ppermute | solution.py:229
  62.0 18.3 %collective-permute-start.15 = (f32[21,32,128]{2,1,0:T(8,128)S(1)}, f32[21,32,128]{2,1,0:T(8,128)S(1)}, u32[]{:S(2)}, u32[]{:S(2)}) collective-permute-start(f32[21,32,128]{2,1,0:T(8,128)S(1)} %add.39.refs_2_), channel_id=1, source_target_pairs={{0,2},{1,3},{2,0},{3,1},{4,6},{5,7},{6,4},{7,5},{8,10},{9,11},{10,... | collective-permute-start | bytes 1032200 | tf_op jit(solution)/shard_map/ppermute | solution.py:229
  67.6 10.8 %collective-permute-start.21 = (f32[15,32,128]{2,1,0:T(8,128)S(1)}, f32[15,32,128]{2,1,0:T(8,128)S(1)}, u32[]{:S(2)}, u32[]{:S(2)}) collective-permute-start(f32[15,32,128]{2,1,0:T(8,128)S(1)} %add.40), channel_id=1, source_target_pairs={{0,2},{1,3},{2,0},{3,1},{4,6},{5,7},{6,4},{7,5},{8,10},{9,11},{10,... | collective-permute-start | bytes 737288 | tf_op jit(solution)/shard_map/ppermute | solution.py:229
  68.1 12.1 %collective-permute-start.22 = (f32[15,32,128]{2,1,0:T(8,128)S(1)}, f32[15,32,128]{2,1,0:T(8,128)S(1)}, u32[]{:S(2)}, u32[]{:S(2)}) collective-permute-start(f32[15,32,128]{2,1,0:T(8,128)S(1)} %add.41), channel_id=1, source_target_pairs={{0,1},{1,0},{2,3},{3,2},{4,5},{5,4},{6,7},{7,6},{8,9},{9,8},{10,11... | collective-permute-start | bytes 737288 | tf_op jit(solution)/shard_map/ppermute | solution.py:229
  102.5 21.9 %collective-permute-start.25 = (f32[512,512]{1,0:T(8,128)S(1)}, f32[512,512]{1,0:T(8,128)S(1)}, u32[]{:S(2)}, u32[]{:S(2)}) collective-permute-start(f32[512,512]{1,0:T(8,128)S(1)} %rest.2), channel_id=1, source_target_pairs={{0,4},{4,0},{8,12},{12,8},{16,20},{20,16},{24,28},{28,24},{1,5},{5... | collective-permute-start | bytes 3145736 | tf_op jit(solution)/shard_map/ppermute | solution.py:256
  105.8 18.6 %collective-permute-start.26 = (f32[512,512]{1,0:T(8,128)S(1)}, f32[512,512]{1,0:T(8,128)S(1)}, u32[]{:S(2)}, u32[]{:S(2)}) collective-permute-start(f32[512,512]{1,0:T(8,128)S(1)} %get-tuple-element.148), channel_id=1, source_target_pairs={{0,0},{28,28},{4,8},{8,4},{12,16},{16,12},{20,24},{24,20},{1,1},{2... | collective-permute-start | bytes 3145736 | tf_op jit(solution)/shard_map/ppermute | solution.py:261
  125.7 7.4 %collective-permute-start.27 = (f32[16,32,128]{2,1,0:T(8,128)S(1)}, f32[16,32,128]{2,1,0:T(8,128)S(1)}, u32[]{:S(2)}, u32[]{:S(2)}) collective-permute-start(f32[16,32,128]{2,1,0:T(8,128)S(1)} %get-tuple-element.161), channel_id=1, source_target_pairs={{0,1},{1,0},{2,3},{3,2},{4,5},{5,4},{6,7},{7,6},{8,9},{9,8},{10,11... | collective-permute-start | bytes 786440 | tf_op jit(solution)/shard_map/ppermute | solution.py:229
  130.1 11.8 %collective-permute-start.33 = (f32[10,128,128]{2,1,0:T(8,128)S(1)}, f32[10,128,128]{2,1,0:T(8,128)S(1)}, u32[]{:S(2)}, u32[]{:S(2)}) collective-permute-start(f32[10,128,128]{2,1,0:T(8,128)S(1)} %get-tuple-element.170), channel_id=1, source_target_pairs={{0,4},{4,0},{8,12},{12,8},{16,20},{20,16},{24,28},{28,24},{1,5},{5... | collective-permute-start | bytes 1966088 | tf_op jit(solution)/shard_map/ppermute | solution.py:256
  130.2 11.9 %collective-permute-start.34 = (f32[10,128,128]{2,1,0:T(8,128)S(1)}, f32[10,128,128]{2,1,0:T(8,128)S(1)}, u32[]{:S(2)}, u32[]{:S(2)}) collective-permute-start(f32[10,128,128]{2,1,0:T(8,128)S(1)} %get-tuple-element.171), channel_id=1, source_target_pairs={{0,0},{28,28},{4,8},{8,4},{12,16},{16,12},{20,24},{24,20},{1,1},{2... | collective-permute-start | bytes 1966088 | tf_op jit(solution)/shard_map/ppermute | solution.py:261
  133.3 7.1 %collective-permute-start.29 = (f32[16,32,128]{2,1,0:T(8,128)S(1)}, f32[16,32,128]{2,1,0:T(8,128)S(1)}, u32[]{:S(2)}, u32[]{:S(2)}) collective-permute-start(f32[16,32,128]{2,1,0:T(8,128)S(1)} %add.44), channel_id=1, source_target_pairs={{0,2},{1,3},{2,0},{3,1},{4,6},{5,7},{6,4},{7,5},{8,10},{9,11},{10,... | collective-permute-start | bytes 786440 | tf_op jit(solution)/shard_map/ppermute | solution.py:229
  134.4 7.0 %collective-permute-start.31 = (f32[16,32,128]{2,1,0:T(8,128)S(1)}, f32[16,32,128]{2,1,0:T(8,128)S(1)}, u32[]{:S(2)}, u32[]{:S(2)}) collective-permute-start(f32[16,32,128]{2,1,0:T(8,128)S(1)} %add.45), channel_id=1, source_target_pairs={{0,1},{1,0},{2,3},{3,2},{4,5},{5,4},{6,7},{7,6},{8,9},{9,8},{10,11... | collective-permute-start | bytes 786440 | tf_op jit(solution)/shard_map/ppermute | solution.py:229
  140.4 7.9 %collective-permute-start.30 = (f32[16,32,128]{2,1,0:T(8,128)S(1)}, f32[16,32,128]{2,1,0:T(8,128)S(1)}, u32[]{:S(2)}, u32[]{:S(2)}) collective-permute-start(f32[16,32,128]{2,1,0:T(8,128)S(1)} %add.46.refs_0_), channel_id=1, source_target_pairs={{0,1},{1,0},{2,3},{3,2},{4,5},{5,4},{6,7},{7,6},{8,9},{9,8},{10,11... | collective-permute-start | bytes 786440 | tf_op jit(solution)/shard_map/ppermute | solution.py:229
  141.4 8.3 %collective-permute-start.32 = (f32[16,32,128]{2,1,0:T(8,128)S(1)}, f32[16,32,128]{2,1,0:T(8,128)S(1)}, u32[]{:S(2)}, u32[]{:S(2)}) collective-permute-start(f32[16,32,128]{2,1,0:T(8,128)S(1)} %add.47.refs_2_), channel_id=1, source_target_pairs={{0,2},{1,3},{2,0},{3,1},{4,6},{5,7},{6,4},{7,5},{8,10},{9,11},{10,... | collective-permute-start | bytes 786440 | tf_op jit(solution)/shard_map/ppermute | solution.py:229
  165.6 16.1 %collective-permute-start.35 = (f32[512,512]{1,0:T(8,128)S(1)}, f32[512,512]{1,0:T(8,128)S(1)}, u32[]{:S(2)}, u32[]{:S(2)}) collective-permute-start(f32[512,512]{1,0:T(8,128)S(1)} %get-tuple-element.176), channel_id=1, source_target_pairs={{0,0},{28,28},{4,8},{8,4},{12,16},{16,12},{20,24},{24,20},{1,1},{2... | collective-permute-start | bytes 3145736 | tf_op jit(solution)/shard_map/ppermute | solution.py:261
  (7 other events, 29.0 us)
where the time goes:
time: 186 us; the launch traced here: 183 us
  waiting for transfers between devices  72.7 us (39%)
  Pallas kernels  56 us (30%)
  starting transfers between devices  51 us (27%)
  local copies, waits for them, and re-layouts  2.25 us (1%)
    ppermute x18, waiting for transfers between devices, flip_rows(): lax.ppermute(x, 'rows', [(i, i ^ mask) for i in range(lax.axis_size('rows...  38.9 us
    pallas_call x2, Pallas kernels, newton(): pl.pallas_call(functools.partial(newton_kernel, tile_lists, whole_lists,...  28.2 us
    ppermute x12, starting transfers between devices, around(): lax.ppermute(x, 'pair', [(i, (i + 2 * hop) % pairs) for i in range(pairs)])  24.9 us
    ppermute x12, waiting for transfers between devices, around(): lax.ppermute(x, 'pair', [(i, (i + 2 * hop) % pairs) for i in range(pairs)])  21.2 us
    pallas_call x1, Pallas kernels, powers(): pl.pallas_call(power_kernel, out_shape=[shape((width, width), bf16)] * 4,...  13.7 us
    ppermute x3, waiting for transfers between devices, swap_far(): lax.ppermute(x, 'pair', ends + [(i, (i + 1 ^ 1) - 1) for i in range(1, pa...  12.6 us
    ppermute x18, starting transfers between devices, flip_rows(): lax.ppermute(x, 'rows', [(i, i ^ mask) for i in range(lax.axis_size('rows...  11.4 us
    ppermute x3, starting transfers between devices, swap_far(): lax.ppermute(x, 'pair', ends + [(i, (i + 1 ^ 1) - 1) for i in range(1, pa...  10.6 us
  transfers between devices with their start and end apart: 37, of which 21 were waited for; matrix products, arithmetic and copies ran while one was open for 0% of the time, Pallas kernels for 10%

commit v1 on v0

--- a/solution.py
+++ b/solution.py
@@ -261,167 +261,183 @@
     return lax.ppermute(x, "pair", ends + [(i, ((i + 1) ^ 1) - 1) for i in range(1, pairs - 1)])
 
 
-def newton_kernel(tile_lists, whole_lists, n_columns, last, *refs):
-    refs = list(refs)
-
-    def take(n):
-        got = refs[:n]
-        del refs[:n]
-        return got
-
-    places = paths(lax.axis_size("rows"))
-    groups = [take(len(places)) for _ in tile_lists]
-    wholes = take(len(whole_lists))
-    columns = [take(2) for _ in range(n_columns)]
-    out_s, plain_q, w_hi, w_lo, b_hi, b_lo, f_ref = take(7)
-    extra = [] if last else take(5)
-    n_hi, n_lo, a_hi, a_lo = take(4) if last else extra[:4]
-    tile_ref = refs[0]
-    width = n_hi.shape[0]
-    count = width // TILE
+def load_tile(parts, t, tile_ref):
+    groups = len(parts)
+    if groups == 1:
+        return parts[0][t]
+    if groups != 4:
+        for part, place in zip(parts, paths(groups)):
+            size = part.shape[1]
+            tile_ref[pl.ds(pl.multiple_of(place * size, size), size), :] = part[t]
+        return tile_ref[...]
     row = lax.axis_index("rows")
     x_flip, y_flip = lax.rem(row, 2) == 1, lax.div(row, 2) == 1
-
-    def load(parts, t):
-        if len(parts) != 4:
-            for part, place in zip(parts, places):
-                size = part.shape[1]
-                tile_ref[pl.ds(pl.multiple_of(place * size, size), size), :] = part[t]
-            return tile_ref[...]
-        one, two, three_, four = (part[t] for part in parts)
-        rows_ = [jnp.where(x_flip, two, one), jnp.where(x_flip, one, two)]
-        rows_ += [jnp.where(y_flip, four, three_), jnp.where(y_flip, three_, four)]
-        return jnp.concatenate(rows_, axis=0)
-
-    source = {}
-    for tiles, parts in zip(tile_lists, groups):
-        for t, key in enumerate(tiles):
-            source[key] = functools.partial(load, parts, t)
-    for tiles, part in zip(whole_lists, wholes):
-        for t, key in enumerate(tiles):
-            source[key] = functools.partial(lambda ref, k: ref[k], part, t)
-
+    a, b, c, d = (part[t] for part in parts)
+    pieces = [jnp.where(x_flip, b, a), jnp.where(x_flip, a, b), jnp.where(y_flip, d, c), jnp.where(y_flip, c, d)]
+    return jnp.concatenate(pieces, axis=0)
+
+
+def diagonal_of(value):
     eye = lax.broadcasted_iota(jnp.int32, (TILE, TILE), 0) == lax.broadcasted_iota(jnp.int32, (TILE, TILE), 1)
-    along, down = [], []
-    for i in range(count):
-        own = jnp.where(eye, source[i, i](), 0.0)
-        along.append(jnp.sum(own, axis=0, keepdims=True) + epsilon)
-        down.append(jnp.sum(own, axis=1, keepdims=True) + epsilon)
-    d_row = jnp.concatenate(along, axis=1)
-    s_row = lax.rsqrt(d_row)
-    s_col = [lax.rsqrt(v) for v in down]
+    return jnp.sum(jnp.where(eye, value, 0.0), axis=0, keepdims=True) + epsilon
+
+
+def flip_line(row):
+    eye = lax.broadcasted_iota(jnp.int32, (TILE, TILE), 0) == lax.broadcasted_iota(jnp.int32, (TILE, TILE), 1)
+    parts = [jnp.where(eye, row[:, i : i + TILE], 0.0) for i in range(0, row.shape[1], TILE)]
+    return [jnp.sum(part, axis=1, keepdims=True) for part in parts]
+
+
+def normalize_tiles(tiles, parts, tile_ref, s_row, s_col, n_hi, n_lo):
     square = jnp.zeros((TILE, TILE), f32)
-    for (i, j), get in source.items():
+    for t, (i, j) in enumerate(tiles):
         at, to = slice(i * TILE, (i + 1) * TILE), slice(j * TILE, (j + 1) * TILE)
-        normed = get() * s_col[i] * s_row[:, to]
+        normed = load_tile(parts, t, tile_ref) * s_col[i] * s_row[:, to]
         n_hi[at, to], n_lo[at, to] = halves(normed)
         if i == j:
             square = square + normed * normed
         else:
             square = square + 2.0 * (normed * normed)
             n_hi[to, at], n_lo[to, at] = halves(normed.T)
-    square = jnp.sum(square, axis=0, keepdims=True)
+    return jnp.sum(square, axis=0, keepdims=True)
+
+
+def early_kernel(tiles, n_parts, *refs):
+    parts, (n_hi, n_lo, own, d_ref, square_ref, tile_ref) = refs[:n_parts], refs[n_parts:]
+    width = n_hi.shape[0]
+    place = {key: t for t, key in enumerate(tiles)}
+    d_row = jnp.concatenate(
+        [diagonal_of(load_tile(parts, place[i, i], tile_ref)) for i in range(width // TILE)], axis=1
+    )
+    d_ref[...] = d_row
+    s_row = lax.rsqrt(d_row)
+    square_ref[...] = normalize_tiles(tiles, parts, tile_ref, s_row, flip_line(s_row), n_hi, n_lo)
+    for i in range(0, width, SPAN):
+        band = slice(i, i + SPAN)
+        own[band, :] = three(dot, (n_hi[band, :], n_lo[band, :]), (n_hi[...], n_lo[...]))
+
+
+def early(tiles, parts, width):
+    return pl.pallas_call(
+        functools.partial(early_kernel, tiles, len(parts)),
+        out_shape=[shape((width, width), bf16)] * 2 + [shape((width, width)), shape((1, width)), shape((1, TILE))],
+        in_specs=[VMEM] * len(parts),
+        out_specs=[VMEM] * 5,
+        scratch_shapes=[pltpu.VMEM((TILE, TILE), f32)],
+        compiler_params=params(16),
+        cost_estimate=cost(100 * width**3, 8 * width**2),
+        name="early",
+    )(*parts)
+
+
+def columns_band(columns, band):
+    high = jnp.concatenate([hi[band, :] for hi, _ in columns], axis=1)
+    low = jnp.concatenate([lo[band, :] for _, lo in columns], axis=1)
+    return high, low
+
+
+def ends(last):
+    if not last:
+        return 0, BLK
+    swapped = lax.axis_index("pair") == 0
+    return pl.multiple_of(jnp.where(swapped, BLK, 0), BLK), pl.multiple_of(jnp.where(swapped, 0, BLK), BLK)
+
+
+def newton_kernel(tiles, n_parts, blocks, n_columns, last, *refs):
+    refs = list(refs)
+
+    def take(n):
+        got = refs[:n]
+        del refs[:n]
+        return got
+
+    parts = take(n_parts)
+    known = [take(5) for _ in blocks]
+    columns = [take(2) for _ in range(n_columns)]
+    out_s, out_q = take(2)
+    if last:
+        tile_ref = take(1)[0]
+    n_hi, n_lo, a_hi, a_lo, b_hi, b_lo = take(6)
+    if not last:
+        d_out, f_out, tile_ref = refs
+    width = n_hi.shape[0]
+    place = {key: t for t, key in enumerate(tiles)}
+
+    d_parts = [block[3][...] for block in known]
+    for i in range(blocks[-1][1] // TILE, width // TILE):
+        d_parts.append(diagonal_of(load_tile(parts, place[i, i], tile_ref)))
+    d_row = jnp.concatenate(d_parts, axis=1)
+    s_row = lax.rsqrt(d_row)
+    square = normalize_tiles(tiles, parts, tile_ref, s_row, flip_line(s_row), n_hi, n_lo)
+    for (lo, hi), block in zip(blocks, known):
+        n_hi[lo:hi, lo:hi] = block[0][...]
+        n_lo[lo:hi, lo:hi] = block[1][...]
+        square = square + block[4][...]
     spread = jnp.full((1, 1), 1.5, f32) * jnp.sqrt(jnp.sum(square, axis=1, keepdims=True) / width)
     inverse = 1.0 / spread
     factor = 0.0625 * jnp.sqrt(d_row) * lax.rsqrt(spread)
+    scale = 16.0 * s_row * factor
+    s_col = flip_line(s_row)
+    if not last:
+        d_out[...] = d_row
+        f_out[...] = factor
 
     for i in range(0, width, SPAN):
         band = slice(i, i + SPAN)
-        product = three(dot, (n_hi[band, :], n_lo[band, :]), (n_hi[...], n_lo[...]))
+        inside = [k for k, (lo, hi) in enumerate(blocks) if lo <= i < hi]
+        if inside:
+            lo, hi = blocks[inside[0]]
+            rest_ = slice(hi, width) if lo == 0 else slice(0, lo)
+            own = three(dot, (n_hi[band, rest_], n_lo[band, rest_]), (n_hi[rest_, lo:hi], n_lo[rest_, lo:hi]))
+            own = own + known[inside[0]][2][i - lo : i - lo + SPAN, :]
+            other = three(dot, (n_hi[band, :], n_lo[band, :]), (n_hi[:, rest_], n_lo[:, rest_]))
+            product = jnp.concatenate([own, other] if lo == 0 else [other, own], axis=1)
+        else:
+            product = three(dot, (n_hi[band, :], n_lo[band, :]), (n_hi[...], n_lo[...]))
         scaled = (n_hi[band, :].astype(f32) + n_lo[band, :].astype(f32)) * inverse
         product = product * (inverse * inverse)
         here = lax.broadcasted_iota(jnp.int32, (SPAN, width), 0) + i == lax.broadcasted_iota(jnp.int32, (SPAN, width), 1)
         weight = jnp.concatenate(s_col[i // TILE : (i + SPAN) // TILE], axis=0)
         a_hi[band, :], a_lo[band, :] = halves((product - 3.0 * scaled + jnp.where(here, 4.0, 0.0)) * weight)
         b_hi[band, :], b_lo[band, :] = halves(product - 6.0 * scaled + jnp.where(here, 5.0, 0.0))
-
-    rows = w_hi.shape[0]
-
-    def wide(k, band):
-        return jnp.concatenate([both[k][band, :] for both in columns], axis=1)
-
-    for i in range(0, rows, SPAN):
+    swapped = lax.axis_index("pair") == 0
+    s_at, q_at = ends(last)
+    for i in range(0, out_s.shape[0], SPAN):
         band = slice(i, i + SPAN)
-        value = three(dot, (wide(0, band), wide(1, band)), (a_hi[...], a_lo[...]))
-        w_hi[band, :], w_lo[band, :] = halves(value)
-
-    f_ref[...] = factor
-    if last:
-        s_at, q_at = ends()
-    else:
-        s_at, q_at = 0, BLK
-        extra[4][...] = d_row
-    for i in range(0, rows, SPAN):
-        band = slice(i, i + SPAN)
-        cols = pl.ds(s_at, BLK)
-        value = three(dot, (w_hi[band, :], w_lo[band, :]), (b_hi[:, cols], b_lo[:, cols]))
-        plain = wide(0, band).astype(f32) + wide(1, band).astype(f32)
-        plain = plain * (16.0 * s_row * factor)
+        high, low = columns_band(columns, band)
+        w = halves(three(dot, (high, low), (a_hi[...], a_lo[...])))
+        plain = (high.astype(f32) + low.astype(f32)) * scale
+        near_cols, far_cols = pl.ds(q_at, BLK), pl.ds(s_at, BLK)
+        s_value = three(dot, w, (b_hi[:, far_cols], b_lo[:, far_cols]))
+        q_value = three(dot, w, (b_hi[:, near_cols], b_lo[:, near_cols]))
+        left, right, f_left, f_right = plain[:, :BLK], plain[:, BLK:], factor[:, :BLK], factor[:, BLK:]
         if last:
-            swapped = lax.axis_index("pair") == 0
-            left, right, f_left, f_right = plain[:, :BLK], plain[:, BLK:], factor[:, :BLK], factor[:, BLK:]
-            out_s[band, :] = value * jnp.where(swapped, f_right, f_left) + jnp.where(swapped, right, left)
-            plain_q[band, :] = jnp.where(swapped, left, right)
-        else:
-            out_s[band, :] = value * factor[:, :BLK] + plain[:, :BLK]
-            plain_q[band, :] = plain[:, BLK:]
-
-
-def ends():
-    swapped = lax.axis_index("pair") == 0
-    return pl.multiple_of(jnp.where(swapped, BLK, 0), BLK), pl.multiple_of(jnp.where(swapped, 0, BLK), BLK)
-
-
-def rest_kernel(last, plain_q, w_hi, w_lo, b_hi, b_lo, f_ref, out_q):
-    cols = pl.ds(ends()[1] if last else BLK, BLK)
-    factor = f_ref[...][:, BLK:]
-    if last:
-        factor = jnp.where(lax.axis_index("pair") == 0, f_ref[...][:, :BLK], factor)
-    for i in range(0, plain_q.shape[0], SPAN):
-        band = slice(i, i + SPAN)
-        value = three(dot, (w_hi[band, :], w_lo[band, :]), (b_hi[:, cols], b_lo[:, cols]))
-        out_q[band, :] = value * factor + plain_q[band, :]
-
-
-def rest(held, last):
-    rows, width = held[1].shape
-    return pl.pallas_call(
-        functools.partial(rest_kernel, last),
-        out_shape=shape((rows, BLK)),
-        in_specs=[VMEM] * 6,
-        out_specs=VMEM,
-        compiler_params=params(12),
-        cost_estimate=cost(3000 * rows * width * BLK, 8 * rows * width),
-        name="rest",
-    )(*held)
-
-
-def newton(tile_lists, whole_lists, groups, wholes, columns, last):
+            left, right = jnp.where(swapped, right, left), jnp.where(swapped, left, right)
+            f_left, f_right = jnp.where(swapped, f_right, f_left), jnp.where(swapped, f_left, f_right)
+        out_s[band, :] = s_value * f_left + left
+        out_q[band, :] = q_value * f_right + right
+
+
+def newton(tiles, parts, blocks, known, columns, last):
     rows = columns[0][0].shape[0]
     width = sum(hi.shape[1] for hi, _ in columns)
-    flat = [p for parts in groups for p in parts] + list(wholes) + [h for both in columns for h in both]
-    square = [shape((width, width), bf16)] * 4
-    tall = [shape((rows, width), bf16)] * 2
-    outs = [shape((rows, BLK))] * 2 + tall + square[:2] + [shape((1, width))]
-    outs += [] if last else square + [shape((1, width))]
-    scratch = [pltpu.VMEM((width, width), bf16)] * 4 if last else []
-    scratch += [pltpu.VMEM((TILE, TILE), f32)]
+    flat = list(parts) + [v for block in known for v in block] + [h for both in columns for h in both]
+    outs = [shape((rows, BLK))] * 2
+    scratch = [pltpu.VMEM((TILE, TILE), f32)]
+    if last:
+        scratch += [pltpu.VMEM((width, width), bf16)] * 6
+    else:
+        outs += [shape((width, width), bf16)] * 6 + [shape((1, width))] * 2
     return pl.pallas_call(
-        functools.partial(newton_kernel, tile_lists, whole_lists, len(columns), last),
+        functools.partial(newton_kernel, tiles, len(parts), blocks, len(columns), last),
         out_shape=outs,
         in_specs=[VMEM] * len(flat),
         out_specs=[VMEM] * len(outs),
         scratch_shapes=scratch,
         compiler_params=params(28),
-        cost_estimate=cost(3 * (width**3 + 1.5 * rows * width**2), 16 * width**2),
+        cost_estimate=cost(3 * (width**3 + 2 * rows * width**2), 16 * width**2),
         name="newton",
     )(*flat)
-
-
-def flip_line(row):
-    eye = lax.broadcasted_iota(jnp.int32, (TILE, TILE), 0) == lax.broadcasted_iota(jnp.int32, (TILE, TILE), 1)
-    parts = [jnp.where(eye, row[:, i : i + TILE], 0.0) for i in range(0, row.shape[1], TILE)]
-    return [jnp.sum(part, axis=1, keepdims=True) for part in parts]
 
 
 def power_kernel(n_hi, n_lo, a_hi, a_lo, b_hi, b_lo, d_ref, p_hi, p_lo, t_hi, t_lo):
@@ -521,20 +537,19 @@
     return lax.optimization_barrier((values, first))[0]
 
 
-def place_kernel(first, block, kept, out, sem):
+def place_kernel(near, start, block, kept, out, sem):
     core = lax.rem(lax.axis_index("pair"), 2)
-    at = core if first else 1 - core
-    half = pl.ds(pl.multiple_of((1 - at) * BLK, BLK), BLK)
-    copy = pltpu.make_async_copy(block, out.at[:, half], sem)
+    at = 1 - core if near else core
+    cols = pl.ds(pl.multiple_of(at * BLK, BLK), BLK)
+    copy = pltpu.make_async_copy(block, out.at[start : start + block.shape[0], cols], sem)
     copy.start()
     copy.wait()
 
 
-def place(block, out):
+def place(block, start, out, rows):
     first = out is None
-    rows = block.shape[0]
     call = pl.pallas_call(
-        functools.partial(place_kernel, first),
+        functools.partial(place_kernel, first, start),
         out_shape=shape((rows, 2 * BLK)),
         in_specs=[VMEM, SMEM if first else ANY],
         out_specs=ANY,
@@ -570,31 +585,24 @@
         done = after(sum_second(parts, got, done), spread)
         spread = sum_spread(done)
         groups.append(spread)
-    tiles = [round_tiles(k) for k in range(len(ROUNDS))]
-    out_s, *held = newton(tiles, [], groups, [], columns, False)
-    held, (n_hi, n_lo, a_hi, a_lo, d_row) = held[:6], held[6:]
-    far = swap_far(out_s, pairs)
-    near = swap_near(rest(held, False), pairs)
-    power = powers(n_hi, n_lo, a_hi, a_lo, held[3], held[4], d_row)
+    edge = sum(CHUNKS[k][2] for k in ROUNDS[0])
+    known = early(round_tiles(0), groups[0], edge)
+    out_s, out_q, *squares, d_row, f_row = newton(round_tiles(1), groups[1], [(0, edge)], [known], columns, False)
+    far, near = swap_far(out_s, pairs), swap_near(out_q, pairs)
+    power = powers(*squares, d_row)
     near, far = after((near, far), power)
     near_pair, far_pair, parts = cross(near, far)
-    s_gram, q_gram = next_grams(*after(power, parts), held[5])
+    s_gram, q_gram = next_grams(*after(power, parts), f_row)
     far_gram = swap_far(s_gram, pairs)
     near_gram = swap_near(q_gram, pairs)
     summed = sum_rows(parts)
     count = BLK // TILE
+    known = [early(triangle(0, count), [tiles], BLK) for tiles in (near_gram, far_gram)]
     crossing = [(count + i, j) for i in range(count) for j in range(count)]
-    out_s, *held = newton(
-        [crossing],
-        [triangle(0, count), triangle(count, count)],
-        [summed],
-        [near_gram, far_gram],
-        [near_pair, far_pair],
-        True,
-    )
-    far = swap_far(out_s, pairs)
-    near = swap_near(rest(held, True), pairs)
-    return place(far, place(near, None))
+    columns = [near_pair, far_pair]
+    out_s, out_q = newton(crossing, summed, [(0, BLK), (BLK, 2 * BLK)], known, columns, True)
+    far, near = swap_far(out_s, pairs), swap_near(out_q, pairs)
+    return place(far, 0, place(near, 0, None, near.shape[0]), near.shape[0])
 
 
 def solution(mesh):

time: 186 us -> 184 us (0.989)
  waiting for transfers between devices: 72.7 us -> 64 us
  Pallas kernels: 56 us -> 59.9 us
  starting transfers between devices: 51 us -> 53.4 us
    ppermute x18, waiting for transfers between devices: 38.9 us -> 30.3 us  [flip_rows(): lax.ppermute(x, 'rows', [(i, i ^ mask) for i in range(lax.axis_size('rows...]
    pallas_call x4 -> x5, Pallas kernels: 31.9 us -> 35.8 us  [the longest x2 29.4 us: newton(): pl.pallas_call(functools.partial(newton_kernel, tiles, len(parts), blocks...]
    ppermute x4, starting transfers between devices: 4.13 us -> 6.07 us  [swap_near(): return lax.ppermute(x, 'pair', [(i, i ^ 1) for i in range(pairs)])]
  transfers between devices with their start and end apart: 37 -> 37, of which waited for: 21 -> 20; matrix products, arithmetic and copies ran while one was open for 0% -> 0% of each run, Pallas kernels for 10% -> 14%
where the time goes in v1:
time: 184 us; the launch traced here: 180 us
  waiting for transfers between devices  64 us (35%)
  Pallas kernels  59.9 us (33%)
  starting transfers between devices  53.4 us (29%)
  local copies, waits for them, and re-layouts  2.25 us (1%)
    ppermute x18, waiting for transfers between devices, flip_rows(): lax.ppermute(x, 'rows', [(i, i ^ mask) for i in range(lax.axis_size('rows...  30.3 us
    pallas_call x2, Pallas kernels, newton(): pl.pallas_call(functools.partial(newton_kernel, tiles, len(parts), blocks...  29.4 us
    ppermute x12, starting transfers between devices, around(): lax.ppermute(x, 'pair', [(i, (i + 2 * hop) % pairs) for i in range(pairs)])  25 us
    ppermute x12, waiting for transfers between devices, around(): lax.ppermute(x, 'pair', [(i, (i + 2 * hop) % pairs) for i in range(pairs)])  21.2 us
    pallas_call x1, Pallas kernels, powers(): pl.pallas_call(power_kernel, out_shape=[shape((width, width), bf16)] * 4,...  13.7 us
    ppermute x3, waiting for transfers between devices, swap_far(): lax.ppermute(x, 'pair', ends + [(i, (i + 1 ^ 1) - 1) for i in range(1, pa...  12.4 us
    ppermute x18, starting transfers between devices, flip_rows(): lax.ppermute(x, 'rows', [(i, i ^ mask) for i in range(lax.axis_size('rows...  11.7 us
    ppermute x3, starting transfers between devices, swap_far(): lax.ppermute(x, 'pair', ends + [(i, (i + 1 ^ 1) - 1) for i in range(1, pa...  10.7 us
  transfers between devices with their start and end apart: 37, of which 20 were waited for; matrix products, arithmetic and copies ran while one was open for 0% of the time, Pallas kernels for 14%

profile of v1, /device:TPU:1, one launch (start us, length us, event | category | flops | bytes accessed | tf_op | source)
XLA Modules:
  0.0 180.5 jit_solution(5000225398701458807)
XLA Ops:
  0.0 1.6 copy-done
  3.6 2.7 %collective-permute-start = (f32[64,512]{1,0:T(8,128)S(1)}, f32[64,512]{1,0:T(8,128)S(1)}, u32[]{:S(2)}, u32[]{:S(2)}) collective-permute-start(f32[64,512]{1,0:T(8,128)S(1)} %get-tuple-element.103), channel_id=1, source_target_pairs={{0,8},{4,12},{8,16},{12,20},{16,24},{20,28},{24,0},{28,4},{1,9},{5... | collective-permute-start | bytes 393224 | tf_op jit(solution)/shard_map/ppermute | solution.py:533
  6.3 2.3 %collective-permute-start.1 = (f32[64,512]{1,0:T(8,128)S(1)}, f32[64,512]{1,0:T(8,128)S(1)}, u32[]{:S(2)}, u32[]{:S(2)}) collective-permute-start(f32[64,512]{1,0:T(8,128)S(1)} %get-tuple-element.104), channel_id=1, source_target_pairs={{0,16},{4,20},{8,24},{12,28},{16,0},{20,4},{24,8},{28,12},{1,17},{... | collective-permute-start | bytes 393224 | tf_op jit(solution)/shard_map/ppermute | solution.py:533
  13.4 4.7 %collective-permute-done.1.refs_2_ = f32[64,512]{1,0:T(8,128)S(1)} collective-permute-done((f32[64,512]{1,0:T(8,128)S(1)}, f32[64,512]{1,0:T(8,128)S(1)}, u32[]{:S(2)}, u32[]{:S(2)}) %collective-permute-start.1) | collective-permute-done | bytes 131104 | tf_op jit(solution)/shard_map/ppermute | solution.py:533
  18.2 2.5 %collective-permute-done.4.refs_5_ = f32[64,512]{1,0:T(8,128)S(1)} collective-permute-done((f32[64,512]{1,0:T(8,128)S(1)}, f32[64,512]{1,0:T(8,128)S(1)}, u32[]{:S(2)}, u32[]{:S(2)}) %collective-permute-start.4) | collective-permute-done | bytes 131104 | tf_op jit(solution)/shard_map/ppermute | solution.py:533
  20.7 6.7 %collective-permute-start.7 = (f32[128,256]{1,0:T(8,128)S(1)}, f32[128,256]{1,0:T(8,128)S(1)}, u32[]{:S(2)}, u32[]{:S(2)}) collective-permute-start(f32[128,256]{1,0:T(8,128)S(1)} %get-tuple-element.117), channel_id=1, source_target_pairs={{0,8},{4,12},{8,16},{12,20},{16,24},{20,28},{24,0},{28,4},{1,9},{5... | collective-permute-start | bytes 393224 | tf_op jit(solution)/shard_map/ppermute | solution.py:533
  27.4 1.9 %collective-permute-start.8 = (f32[128,256]{1,0:T(8,128)S(1)}, f32[128,256]{1,0:T(8,128)S(1)}, u32[]{:S(2)}, u32[]{:S(2)}) collective-permute-start(f32[128,256]{1,0:T(8,128)S(1)} %get-tuple-element.118), channel_id=1, source_target_pairs={{0,16},{4,20},{8,24},{12,28},{16,0},{20,4},{24,8},{28,12},{1,17},{... | collective-permute-start | bytes 393224 | tf_op jit(solution)/shard_map/ppermute | solution.py:533
  29.3 2.4 %collective-permute-start.9 = (f32[128,256]{1,0:T(8,128)S(1)}, f32[128,256]{1,0:T(8,128)S(1)}, u32[]{:S(2)}, u32[]{:S(2)}) collective-permute-start(f32[128,256]{1,0:T(8,128)S(1)} %get-tuple-element.119), channel_id=1, source_target_pairs={{0,24},{4,28},{8,0},{12,4},{16,8},{20,12},{24,16},{28,20},{1,25},{... | collective-permute-start | bytes 393224 | tf_op jit(solution)/shard_map/ppermute | solution.py:533
  32.0 8.4 %collective-permute-done.8.refs_10_ = f32[128,256]{1,0:T(8,128)S(1)} collective-permute-done((f32[128,256]{1,0:T(8,128)S(1)}, f32[128,256]{1,0:T(8,128)S(1)}, u32[]{:S(2)}, u32[]{:S(2)}) %collective-permute-start.8) | collective-permute-done | bytes 131104 | tf_op jit(solution)/shard_map/ppermute | solution.py:533
  40.5 1.9 %gram0.1 = (bf16[512,512]{1,0:T(8,128)(2,1)S(1)}, bf16[512,512]{1,0:T(8,128)(2,1)S(1)}, bf16[512,256]{1,0:T(8,128)(2,1)S(1)}, bf16[512,256]{1,0:T(8,128)(2,1)S(1...) custom-call(f32[64,512]{1,0:T(8,128)S(1)} %get-tuple-element.102.ref, ...), custom_call_target="tpu_custom_call" | custom-call | flops 27525120000 | bytes 49152 | tf_op jit(solution)/shard_map/gram0/pallas_call | solution.py:214
  42.3 1.3 collective-permute-start.15
  44.9 3.1 %collective-permute-start.10 = (f32[128,256]{1,0:T(8,128)S(1)}, f32[128,256]{1,0:T(8,128)S(1)}, u32[]{:S(2)}, u32[]{:S(2)}) collective-permute-start(f32[128,256]{1,0:T(8,128)S(1)} %get-tuple-element.133), channel_id=1, source_target_pairs={{0,8},{4,12},{8,16},{12,20},{16,24},{20,28},{24,0},{28,4},{1,9},{5... | collective-permute-start | bytes 393224 | tf_op jit(solution)/shard_map/ppermute | solution.py:533
  48.5 1.7 collective-permute-start.12
  54.1 4.1 %collective-permute-done.11.refs_6_ = f32[128,256]{1,0:T(8,128)S(1)} collective-permute-done((f32[128,256]{1,0:T(8,128)S(1)}, f32[128,256]{1,0:T(8,128)S(1)}, u32[]{:S(2)}, u32[]{:S(2)}) %collective-permute-start.11) | collective-permute-done | bytes 131104 | tf_op jit(solution)/shard_map/ppermute | solution.py:533
  62.6 4.9 %collective-permute-done.13 = f32[15,32,128]{2,1,0:T(8,128)S(1)} collective-permute-done((f32[15,32,128]{2,1,0:T(8,128)S(1)}, f32[15,32,128]{2,1,0:T(8,128)S(1)}, u32[]{:S(2)}, u32[]{:S(2)}) %collective-permute-start.13) | collective-permute-done | bytes 245792 | tf_op jit(solution)/shard_map/ppermute | solution.py:229
  68.4 10.1 %collective-permute-done.19 = f32[15,32,128]{2,1,0:T(8,128)S(1)} collective-permute-done((f32[15,32,128]{2,1,0:T(8,128)S(1)}, f32[15,32,128]{2,1,0:T(8,128)S(1)}, u32[]{:S(2)}, u32[]{:S(2)}) %collective-permute-start.19) | collective-permute-done | bytes 245792 | tf_op jit(solution)/shard_map/ppermute | solution.py:229
  78.5 1.7 collective-permute-done.20
  80.9 3.6 %early.3 = (bf16[768,768]{1,0:T(8,128)(2,1)S(1)}, bf16[768,768]{1,0:T(8,128)(2,1)S(1)}, f32[768,768]{1,0:T(8,128)S(1)}, f32[1,768]{1,0:T(1,128)S(1)}, f32[1,128]{1,0:T(1,128)S(1)}) custom-call(f32[21,32,128]{2,1,0:T(8,128)S(1)} %add.40.refs_0_, f32[21,32,128]{2,1,0:T(8,128)S(1)} %collective-permute-done.21.refs_1_, f32[21,32,128]{2,1,0:T(8,128)S(1)} %add.41.refs_2_, ...), custom_call_target="tpu_custom_call" | custom-call | flops 707788800 | bytes 73728 | tf_op jit(solution)/shard_map/early/pallas_call | solution.py:321
  85.9 16.0 %newton.2 = (f32[512,512]{1,0:T(8,128)S(1)}, f32[512,512]{1,0:T(8,128)S(1)}, bf16[1024,1024]{1,0:T(8,128)(2,1)S(1)}, bf16[1024,1024]{1,0:T(8,128)(2,1)S(1)}, bf1...) custom-call(f32[15,32,128]{2,1,0:T(8,128)S(1)} %add.42.refs_0_, ...), custom_call_target="tpu_custom_call" | custom-call | flops 100663296 | bytes 262144 | tf_op jit(solution)/shard_map/newton/pallas_call | solution.py:431
  101.9 3.3 %collective-permute-start.25 = (f32[512,512]{1,0:T(8,128)S(1)}, f32[512,512]{1,0:T(8,128)S(1)}, u32[]{:S(2)}, u32[]{:S(2)}) collective-permute-start(f32[512,512]{1,0:T(8,128)S(1)} %get-tuple-element.155), channel_id=1, source_target_pairs={{0,4},{4,0},{8,12},{12,8},{16,20},{20,16},{24,28},{28,24},{1,5},{5... | collective-permute-start | bytes 3145736 | tf_op jit(solution)/shard_map/ppermute | solution.py:256
  105.1 5.0 %collective-permute-start.26 = (f32[512,512]{1,0:T(8,128)S(1)}, f32[512,512]{1,0:T(8,128)S(1)}, u32[]{:S(2)}, u32[]{:S(2)}) collective-permute-start(f32[512,512]{1,0:T(8,128)S(1)} %get-tuple-element.156), channel_id=1, source_target_pairs={{0,0},{28,28},{4,8},{8,4},{12,16},{16,12},{20,24},{24,20},{1,1},{2... | collective-permute-start | bytes 3145736 | tf_op jit(solution)/shard_map/ppermute | solution.py:261
  110.1 13.7 %powers.1 = (bf16[1024,1024]{1,0:T(8,128)(2,1)S(1)}, bf16[1024,1024]{1,0:T(8,128)(2,1)S(1)}, bf16[1024,1024]{1,0:T(8,128)(2,1)S(1)}, bf16[1024,1024]{1,0:T(8,128)(2,1)S(1)}) custom-call(bf16[1024,1024]{1,0:T(8,128)(2,1)S(1)} %get-tuple-element.157.n_hi, bf16[1024,1024]{1,0:T(8,128)(2,1)S(1)} %get-tuple-element.158.n_lo, ...), custom_call_target="tpu_custom_call" | custom-call | flops 100663296 | bytes 262144 | tf_op jit(solution)/shard_map/powers/pallas_call | solution.py:460
  126.7 2.8 %next_grams.1 = (f32[10,128,128]{2,1,0:T(8,128)S(1)}, f32[10,128,128]{2,1,0:T(8,128)S(1)}) custom-call(bf16[1024,1024]{1,0:T(8,128)(2,1)S(1)} %get-tuple-element.176.p_hi, bf16[1024,1024]{1,0:T(8,128)(2,1)S(1)} %get-tuple-element.177.p_lo, bf16[1024,1024]{1,0:T(8,128)(2,1)S(1)} %get-tuple-element.178.t_hi, bf16[1024,1024]{1,0:T(8,128)(2,1)S(1)} %get-tuple-element.179.t_lo, ...), custom_call_target="tpu_custom_call" | custom-call | flops 25165824 | bytes 131072 | tf_op jit(solution)/shard_map/next_grams/pallas_call | solution.py:489
  129.5 3.0 %collective-permute-start.34 = (f32[10,128,128]{2,1,0:T(8,128)S(1)}, f32[10,128,128]{2,1,0:T(8,128)S(1)}, u32[]{:S(2)}, u32[]{:S(2)}) collective-permute-start(f32[10,128,128]{2,1,0:T(8,128)S(1)} %get-tuple-element.187), channel_id=1, source_target_pairs={{0,0},{28,28},{4,8},{8,4},{12,16},{16,12},{20,24},{24,20},{1,1},{2... | collective-permute-start | bytes 1966088 | tf_op jit(solution)/shard_map/ppermute | solution.py:261
  134.2 5.9 %collective-permute-done.29 = f32[16,32,128]{2,1,0:T(8,128)S(1)} collective-permute-done((f32[16,32,128]{2,1,0:T(8,128)S(1)}, f32[16,32,128]{2,1,0:T(8,128)S(1)}, u32[]{:S(2)}, u32[]{:S(2)}) %collective-permute-start.29) | collective-permute-done | bytes 262176 | tf_op jit(solution)/shard_map/ppermute | solution.py:229
  141.8 1.4 early.5
  143.2 1.4 early.4
  144.6 2.1 %collective-permute-done.30.refs_1_ = f32[16,32,128]{2,1,0:T(8,128)S(1)} collective-permute-done((f32[16,32,128]{2,1,0:T(8,128)S(1)}, f32[16,32,128]{2,1,0:T(8,128)S(1)}, u32[]{:S(2)}, u32[]{:S(2)}) %collective-permute-start.30) | collective-permute-done | bytes 262176 | tf_op jit(solution)/shard_map/ppermute | solution.py:229
  147.1 13.4 %newton.3 = (f32[512,512]{1,0:T(8,128)S(1)}, f32[512,512]{1,0:T(8,128)S(1)}) custom-call(f32[16,32,128]{2,1,0:T(8,128)S(1)} %add.46.refs_0_, f32[16,32,128]{2,1,0:T(8,128)S(1)} %collective-permute-done.30.refs_1_, f32[16,32,128]{2,1,0:T(8,128)S(1)} %add.47.refs_2_, f32[16,32,128]{2,1,0:T(8,128)S(1)} %collective-permute-done.32.refs_3_, ...), custom_call_target="tpu_custom_call" | custom-call | flops 100663296 | bytes 262144 | tf_op jit(solution)/shard_map/newton/pallas_call | solution.py:431
  160.6 2.6 %collective-permute-start.36 = (f32[512,512]{1,0:T(8,128)S(1)}, f32[512,512]{1,0:T(8,128)S(1)}, u32[]{:S(2)}, u32[]{:S(2)}) collective-permute-start(f32[512,512]{1,0:T(8,128)S(1)} %get-tuple-element.198), channel_id=1, source_target_pairs={{0,4},{4,0},{8,12},{12,8},{16,20},{20,16},{24,28},{28,24},{1,5},{5... | collective-permute-start | bytes 3145736 | tf_op jit(solution)/shard_map/ppermute | solution.py:256
  163.2 2.7 %collective-permute-start.35 = (f32[512,512]{1,0:T(8,128)S(1)}, f32[512,512]{1,0:T(8,128)S(1)}, u32[]{:S(2)}, u32[]{:S(2)}) collective-permute-start(f32[512,512]{1,0:T(8,128)S(1)} %get-tuple-element.197), channel_id=1, source_target_pairs={{0,0},{28,28},{4,8},{8,4},{12,16},{16,12},{20,24},{24,20},{1,1},{2... | collective-permute-start | bytes 3145736 | tf_op jit(solution)/shard_map/ppermute | solution.py:261
  166.9 12.4 %collective-permute-done.35.block = f32[512,512]{1,0:T(8,128)S(1)} collective-permute-done((f32[512,512]{1,0:T(8,128)S(1)}, f32[512,512]{1,0:T(8,128)S(1)}, u32[]{:S(2)}, u32[]{:S(2)}) %collective-permute-start.35) | collective-permute-done | bytes 1048608 | tf_op jit(solution)/shard_map/ppermute | solution.py:261
  (72 shorter events, 28.7 us)
Async XLA Ops:
  3.6 8.6 %collective-permute-start = (f32[64,512]{1,0:T(8,128)S(1)}, f32[64,512]{1,0:T(8,128)S(1)}, u32[]{:S(2)}, u32[]{:S(2)}) collective-permute-start(f32[64,512]{1,0:T(8,128)S(1)} %get-tuple-element.103), channel_id=1, source_target_pairs={{0,8},{4,12},{8,16},{12,20},{16,24},{20,28},{24,0},{28,4},{1,9},{5... | collective-permute-start | bytes 393224 | tf_op jit(solution)/shard_map/ppermute | solution.py:533
  6.3 11.8 %collective-permute-start.1 = (f32[64,512]{1,0:T(8,128)S(1)}, f32[64,512]{1,0:T(8,128)S(1)}, u32[]{:S(2)}, u32[]{:S(2)}) collective-permute-start(f32[64,512]{1,0:T(8,128)S(1)} %get-tuple-element.104), channel_id=1, source_target_pairs={{0,16},{4,20},{8,24},{12,28},{16,0},{20,4},{24,8},{28,12},{1,17},{... | collective-permute-start | bytes 393224 | tf_op jit(solution)/shard_map/ppermute | solution.py:533
  8.6 9.5 %collective-permute-start.2 = (f32[64,512]{1,0:T(8,128)S(1)}, f32[64,512]{1,0:T(8,128)S(1)}, u32[]{:S(2)}, u32[]{:S(2)}) collective-permute-start(f32[64,512]{1,0:T(8,128)S(1)} %get-tuple-element.105), channel_id=1, source_target_pairs={{0,24},{4,28},{8,0},{12,4},{16,8},{20,12},{24,16},{28,20},{1,25},{... | collective-permute-start | bytes 393224 | tf_op jit(solution)/shard_map/ppermute | solution.py:533
  9.8 10.8 %collective-permute-start.4 = (f32[64,512]{1,0:T(8,128)S(1)}, f32[64,512]{1,0:T(8,128)S(1)}, u32[]{:S(2)}, u32[]{:S(2)}) collective-permute-start(f32[64,512]{1,0:T(8,128)S(1)} %get-tuple-element.109), channel_id=1, source_target_pairs={{0,8},{4,12},{8,16},{12,20},{16,24},{20,28},{24,0},{28,4},{1,9},{5... | collective-permute-start | bytes 393224 | tf_op jit(solution)/shard_map/ppermute | solution.py:533
  10.3 21.8 %collective-permute-start.5 = (f32[64,512]{1,0:T(8,128)S(1)}, f32[64,512]{1,0:T(8,128)S(1)}, u32[]{:S(2)}, u32[]{:S(2)}) collective-permute-start(f32[64,512]{1,0:T(8,128)S(1)} %get-tuple-element.110), channel_id=1, source_target_pairs={{0,16},{4,20},{8,24},{12,28},{16,0},{20,4},{24,8},{28,12},{1,17},{... | collective-permute-start | bytes 393224 | tf_op jit(solution)/shard_map/ppermute | solution.py:533
  12.2 19.8 %collective-permute-start.6 = (f32[64,512]{1,0:T(8,128)S(1)}, f32[64,512]{1,0:T(8,128)S(1)}, u32[]{:S(2)}, u32[]{:S(2)}) collective-permute-start(f32[64,512]{1,0:T(8,128)S(1)} %get-tuple-element.111), channel_id=1, source_target_pairs={{0,24},{4,28},{8,0},{12,4},{16,8},{20,12},{24,16},{28,20},{1,25},{... | collective-permute-start | bytes 393224 | tf_op jit(solution)/shard_map/ppermute | solution.py:533
  20.7 11.4 %collective-permute-start.7 = (f32[128,256]{1,0:T(8,128)S(1)}, f32[128,256]{1,0:T(8,128)S(1)}, u32[]{:S(2)}, u32[]{:S(2)}) collective-permute-start(f32[128,256]{1,0:T(8,128)S(1)} %get-tuple-element.117), channel_id=1, source_target_pairs={{0,8},{4,12},{8,16},{12,20},{16,24},{20,28},{24,0},{28,4},{1,9},{5... | collective-permute-start | bytes 393224 | tf_op jit(solution)/shard_map/ppermute | solution.py:533
  27.4 13.1 %collective-permute-start.8 = (f32[128,256]{1,0:T(8,128)S(1)}, f32[128,256]{1,0:T(8,128)S(1)}, u32[]{:S(2)}, u32[]{:S(2)}) collective-permute-start(f32[128,256]{1,0:T(8,128)S(1)} %get-tuple-element.118), channel_id=1, source_target_pairs={{0,16},{4,20},{8,24},{12,28},{16,0},{20,4},{24,8},{28,12},{1,17},{... | collective-permute-start | bytes 393224 | tf_op jit(solution)/shard_map/ppermute | solution.py:533
  29.3 11.2 %collective-permute-start.9 = (f32[128,256]{1,0:T(8,128)S(1)}, f32[128,256]{1,0:T(8,128)S(1)}, u32[]{:S(2)}, u32[]{:S(2)}) collective-permute-start(f32[128,256]{1,0:T(8,128)S(1)} %get-tuple-element.119), channel_id=1, source_target_pairs={{0,24},{4,28},{8,0},{12,4},{16,8},{20,12},{24,16},{28,20},{1,25},{... | collective-permute-start | bytes 393224 | tf_op jit(solution)/shard_map/ppermute | solution.py:533
  42.3 9.2 %collective-permute-start.15 = (f32[21,32,128]{2,1,0:T(8,128)S(1)}, f32[21,32,128]{2,1,0:T(8,128)S(1)}, u32[]{:S(2)}, u32[]{:S(2)}) collective-permute-start(f32[21,32,128]{2,1,0:T(8,128)S(1)} %get-tuple-element.129), channel_id=1, source_target_pairs={{0,1},{1,0},{2,3},{3,2},{4,5},{5,4},{6,7},{7,6},{8,9},{9,8},{10,11... | collective-permute-start | bytes 1032200 | tf_op jit(solution)/shard_map/ppermute | solution.py:229
  43.6 8.8 %collective-permute-start.16 = (f32[21,32,128]{2,1,0:T(8,128)S(1)}, f32[21,32,128]{2,1,0:T(8,128)S(1)}, u32[]{:S(2)}, u32[]{:S(2)}) collective-permute-start(f32[21,32,128]{2,1,0:T(8,128)S(1)} %get-tuple-element.131), channel_id=1, source_target_pairs={{0,2},{1,3},{2,0},{3,1},{4,6},{5,7},{6,4},{7,5},{8,10},{9,11},{10,... | collective-permute-start | bytes 1032200 | tf_op jit(solution)/shard_map/ppermute | solution.py:229
  44.9 9.3 %collective-permute-start.10 = (f32[128,256]{1,0:T(8,128)S(1)}, f32[128,256]{1,0:T(8,128)S(1)}, u32[]{:S(2)}, u32[]{:S(2)}) collective-permute-start(f32[128,256]{1,0:T(8,128)S(1)} %get-tuple-element.133), channel_id=1, source_target_pairs={{0,8},{4,12},{8,16},{12,20},{16,24},{20,28},{24,0},{28,4},{1,9},{5... | collective-permute-start | bytes 393224 | tf_op jit(solution)/shard_map/ppermute | solution.py:533
  48.0 10.2 %collective-permute-start.11 = (f32[128,256]{1,0:T(8,128)S(1)}, f32[128,256]{1,0:T(8,128)S(1)}, u32[]{:S(2)}, u32[]{:S(2)}) collective-permute-start(f32[128,256]{1,0:T(8,128)S(1)} %get-tuple-element.134), channel_id=1, source_target_pairs={{0,16},{4,20},{8,24},{12,28},{16,0},{20,4},{24,8},{28,12},{1,17},{... | collective-permute-start | bytes 393224 | tf_op jit(solution)/shard_map/ppermute | solution.py:533
  48.5 9.7 %collective-permute-start.12 = (f32[128,256]{1,0:T(8,128)S(1)}, f32[128,256]{1,0:T(8,128)S(1)}, u32[]{:S(2)}, u32[]{:S(2)}) collective-permute-start(f32[128,256]{1,0:T(8,128)S(1)} %get-tuple-element.135), channel_id=1, source_target_pairs={{0,24},{4,28},{8,0},{12,4},{16,8},{20,12},{24,16},{28,20},{1,25},{... | collective-permute-start | bytes 393224 | tf_op jit(solution)/shard_map/ppermute | solution.py:533
  52.5 7.9 %collective-permute-start.17 = (f32[21,32,128]{2,1,0:T(8,128)S(1)}, f32[21,32,128]{2,1,0:T(8,128)S(1)}, u32[]{:S(2)}, u32[]{:S(2)}) collective-permute-start(f32[21,32,128]{2,1,0:T(8,128)S(1)} %add.38), channel_id=1, source_target_pairs={{0,2},{1,3},{2,0},{3,1},{4,6},{5,7},{6,4},{7,5},{8,10},{9,11},{10,... | collective-permute-start | bytes 1032200 | tf_op jit(solution)/shard_map/ppermute | solution.py:229
  53.7 7.5 %collective-permute-start.18 = (f32[21,32,128]{2,1,0:T(8,128)S(1)}, f32[21,32,128]{2,1,0:T(8,128)S(1)}, u32[]{:S(2)}, u32[]{:S(2)}) collective-permute-start(f32[21,32,128]{2,1,0:T(8,128)S(1)} %add.39), channel_id=1, source_target_pairs={{0,1},{1,0},{2,3},{3,2},{4,5},{5,4},{6,7},{7,6},{8,9},{9,8},{10,11... | collective-permute-start | bytes 1032200 | tf_op jit(solution)/shard_map/ppermute | solution.py:229
  59.4 8.1 %collective-permute-start.13 = (f32[15,32,128]{2,1,0:T(8,128)S(1)}, f32[15,32,128]{2,1,0:T(8,128)S(1)}, u32[]{:S(2)}, u32[]{:S(2)}) collective-permute-start(f32[15,32,128]{2,1,0:T(8,128)S(1)} %get-tuple-element.137), channel_id=1, source_target_pairs={{0,1},{1,0},{2,3},{3,2},{4,5},{5,4},{6,7},{7,6},{8,9},{9,8},{10,11... | collective-permute-start | bytes 737288 | tf_op jit(solution)/shard_map/ppermute | solution.py:229
  59.7 7.8 %collective-permute-start.14 = (f32[15,32,128]{2,1,0:T(8,128)S(1)}, f32[15,32,128]{2,1,0:T(8,128)S(1)}, u32[]{:S(2)}, u32[]{:S(2)}) collective-permute-start(f32[15,32,128]{2,1,0:T(8,128)S(1)} %get-tuple-element.139), channel_id=1, source_target_pairs={{0,2},{1,3},{2,0},{3,1},{4,6},{5,7},{6,4},{7,5},{8,10},{9,11},{10,... | collective-permute-start | bytes 737288 | tf_op jit(solution)/shard_map/ppermute | solution.py:229
  61.3 18.9 %collective-permute-start.21 = (f32[21,32,128]{2,1,0:T(8,128)S(1)}, f32[21,32,128]{2,1,0:T(8,128)S(1)}, u32[]{:S(2)}, u32[]{:S(2)}) collective-permute-start(f32[21,32,128]{2,1,0:T(8,128)S(1)} %add.40.refs_0_), channel_id=1, source_target_pairs={{0,1},{1,0},{2,3},{3,2},{4,5},{5,4},{6,7},{7,6},{8,9},{9,8},{10,11... | collective-permute-start | bytes 1032200 | tf_op jit(solution)/shard_map/ppermute | solution.py:229
  61.9 18.3 %collective-permute-start.22 = (f32[21,32,128]{2,1,0:T(8,128)S(1)}, f32[21,32,128]{2,1,0:T(8,128)S(1)}, u32[]{:S(2)}, u32[]{:S(2)}) collective-permute-start(f32[21,32,128]{2,1,0:T(8,128)S(1)} %add.41.refs_2_), channel_id=1, source_target_pairs={{0,2},{1,3},{2,0},{3,1},{4,6},{5,7},{6,4},{7,5},{8,10},{9,11},{10,... | collective-permute-start | bytes 1032200 | tf_op jit(solution)/shard_map/ppermute | solution.py:229
  67.6 10.8 %collective-permute-start.19 = (f32[15,32,128]{2,1,0:T(8,128)S(1)}, f32[15,32,128]{2,1,0:T(8,128)S(1)}, u32[]{:S(2)}, u32[]{:S(2)}) collective-permute-start(f32[15,32,128]{2,1,0:T(8,128)S(1)} %add.36), channel_id=1, source_target_pairs={{0,2},{1,3},{2,0},{3,1},{4,6},{5,7},{6,4},{7,5},{8,10},{9,11},{10,... | collective-permute-start | bytes 737288 | tf_op jit(solution)/shard_map/ppermute | solution.py:229
  68.1 12.1 %collective-permute-start.20 = (f32[15,32,128]{2,1,0:T(8,128)S(1)}, f32[15,32,128]{2,1,0:T(8,128)S(1)}, u32[]{:S(2)}, u32[]{:S(2)}) collective-permute-start(f32[15,32,128]{2,1,0:T(8,128)S(1)} %add.37), channel_id=1, source_target_pairs={{0,1},{1,0},{2,3},{3,2},{4,5},{5,4},{6,7},{7,6},{8,9},{9,8},{10,11... | collective-permute-start | bytes 737288 | tf_op jit(solution)/shard_map/ppermute | solution.py:229
  101.9 22.0 %collective-permute-start.25 = (f32[512,512]{1,0:T(8,128)S(1)}, f32[512,512]{1,0:T(8,128)S(1)}, u32[]{:S(2)}, u32[]{:S(2)}) collective-permute-start(f32[512,512]{1,0:T(8,128)S(1)} %get-tuple-element.155), channel_id=1, source_target_pairs={{0,4},{4,0},{8,12},{12,8},{16,20},{20,16},{24,28},{28,24},{1,5},{5... | collective-permute-start | bytes 3145736 | tf_op jit(solution)/shard_map/ppermute | solution.py:256
  105.1 18.7 %collective-permute-start.26 = (f32[512,512]{1,0:T(8,128)S(1)}, f32[512,512]{1,0:T(8,128)S(1)}, u32[]{:S(2)}, u32[]{:S(2)}) collective-permute-start(f32[512,512]{1,0:T(8,128)S(1)} %get-tuple-element.156), channel_id=1, source_target_pairs={{0,0},{28,28},{4,8},{8,4},{12,16},{16,12},{20,24},{24,20},{1,1},{2... | collective-permute-start | bytes 3145736 | tf_op jit(solution)/shard_map/ppermute | solution.py:261
  125.1 7.4 %collective-permute-start.27 = (f32[16,32,128]{2,1,0:T(8,128)S(1)}, f32[16,32,128]{2,1,0:T(8,128)S(1)}, u32[]{:S(2)}, u32[]{:S(2)}) collective-permute-start(f32[16,32,128]{2,1,0:T(8,128)S(1)} %get-tuple-element.171), channel_id=1, source_target_pairs={{0,1},{1,0},{2,3},{3,2},{4,5},{5,4},{6,7},{7,6},{8,9},{9,8},{10,11... | collective-permute-start | bytes 786440 | tf_op jit(solution)/shard_map/ppermute | solution.py:229
  126.3 6.3 %collective-permute-start.28 = (f32[16,32,128]{2,1,0:T(8,128)S(1)}, f32[16,32,128]{2,1,0:T(8,128)S(1)}, u32[]{:S(2)}, u32[]{:S(2)}) collective-permute-start(f32[16,32,128]{2,1,0:T(8,128)S(1)} %get-tuple-element.173), channel_id=1, source_target_pairs={{0,2},{1,3},{2,0},{3,1},{4,6},{5,7},{6,4},{7,5},{8,10},{9,11},{10,... | collective-permute-start | bytes 786440 | tf_op jit(solution)/shard_map/ppermute | solution.py:229
  129.5 12.3 %collective-permute-start.34 = (f32[10,128,128]{2,1,0:T(8,128)S(1)}, f32[10,128,128]{2,1,0:T(8,128)S(1)}, u32[]{:S(2)}, u32[]{:S(2)}) collective-permute-start(f32[10,128,128]{2,1,0:T(8,128)S(1)} %get-tuple-element.187), channel_id=1, source_target_pairs={{0,0},{28,28},{4,8},{8,4},{12,16},{16,12},{20,24},{24,20},{1,1},{2... | collective-permute-start | bytes 1966088 | tf_op jit(solution)/shard_map/ppermute | solution.py:261
  132.5 10.7 %collective-permute-start.33 = (f32[10,128,128]{2,1,0:T(8,128)S(1)}, f32[10,128,128]{2,1,0:T(8,128)S(1)}, u32[]{:S(2)}, u32[]{:S(2)}) collective-permute-start(f32[10,128,128]{2,1,0:T(8,128)S(1)} %get-tuple-element.181), channel_id=1, source_target_pairs={{0,4},{4,0},{8,12},{12,8},{16,20},{20,16},{24,28},{28,24},{1,5},{5... | collective-permute-start | bytes 1966088 | tf_op jit(solution)/shard_map/ppermute | solution.py:256
  132.7 7.5 %collective-permute-start.29 = (f32[16,32,128]{2,1,0:T(8,128)S(1)}, f32[16,32,128]{2,1,0:T(8,128)S(1)}, u32[]{:S(2)}, u32[]{:S(2)}) collective-permute-start(f32[16,32,128]{2,1,0:T(8,128)S(1)} %add.44), channel_id=1, source_target_pairs={{0,2},{1,3},{2,0},{3,1},{4,6},{5,7},{6,4},{7,5},{8,10},{9,11},{10,... | collective-permute-start | bytes 786440 | tf_op jit(solution)/shard_map/ppermute | solution.py:229
  133.8 7.1 %collective-permute-start.31 = (f32[16,32,128]{2,1,0:T(8,128)S(1)}, f32[16,32,128]{2,1,0:T(8,128)S(1)}, u32[]{:S(2)}, u32[]{:S(2)}) collective-permute-start(f32[16,32,128]{2,1,0:T(8,128)S(1)} %add.45), channel_id=1, source_target_pairs={{0,1},{1,0},{2,3},{3,2},{4,5},{5,4},{6,7},{7,6},{8,9},{9,8},{10,11... | collective-permute-start | bytes 786440 | tf_op jit(solution)/shard_map/ppermute | solution.py:229
  140.2 6.5 %collective-permute-start.30 = (f32[16,32,128]{2,1,0:T(8,128)S(1)}, f32[16,32,128]{2,1,0:T(8,128)S(1)}, u32[]{:S(2)}, u32[]{:S(2)}) collective-permute-start(f32[16,32,128]{2,1,0:T(8,128)S(1)} %add.46.refs_0_), channel_id=1, source_target_pairs={{0,1},{1,0},{2,3},{3,2},{4,5},{5,4},{6,7},{7,6},{8,9},{9,8},{10,11... | collective-permute-start | bytes 786440 | tf_op jit(solution)/shard_map/ppermute | solution.py:229
  163.2 16.1 %collective-permute-start.35 = (f32[512,512]{1,0:T(8,128)S(1)}, f32[512,512]{1,0:T(8,128)S(1)}, u32[]{:S(2)}, u32[]{:S(2)}) collective-permute-start(f32[512,512]{1,0:T(8,128)S(1)} %get-tuple-element.197), channel_id=1, source_target_pairs={{0,0},{28,28},{4,8},{8,4},{12,16},{16,12},{20,24},{24,20},{1,1},{2... | collective-permute-start | bytes 3145736 | tf_op jit(solution)/shard_map/ppermute | solution.py:261
  (7 other events, 30.9 us)

commit v2 on v1

--- a/solution.py
+++ b/solution.py
@@ -147,18 +147,36 @@
     return [x, 1 - x, 2 + y, 3 - y]
 
 
-def part_shapes(n, groups):
-    return [shape((n, TILE // groups, TILE))] * groups
-
-
-def spread_tiles(packed, outs, groups):
+def slots(tiles):
+    diagonal = [key for key in tiles if key[0] == key[1]]
+    both = [tuple(diagonal[i : i + 2]) for i in range(0, len(diagonal), 2)]
+    return [(key,) for key in tiles if key[0] != key[1]] + both
+
+
+def part_shapes(tiles, groups):
+    kept = slots(tiles)
+    extra = 8 if any(len(keys) == 2 for keys in kept) else 0
+    return [shape((len(kept) * (TILE // groups) + extra, TILE))] * groups
+
+
+def square_iotas():
+    dims = (TILE, TILE)
+    return lax.broadcasted_iota(jnp.int32, dims, 0), lax.broadcasted_iota(jnp.int32, dims, 1)
+
+
+def spread_tiles(packed, extra, outs, groups):
     size = TILE // groups
+    count = packed.shape[0] * size
     for out, k in zip(outs, paths(groups)):
-        out[...] = packed[:, pl.ds(pl.multiple_of(k * size, size), size), :]
+        value = packed[:, pl.ds(pl.multiple_of(k * size, size), size), :]
+        out[:count, :] = value.reshape(count, TILE)
+        if out.shape[0] > count:
+            out[count:, :] = extra[...]
 
 
 def gram_kernel(pairs, index, groups, counts, *refs):
     refs = list(refs)
+    extra = refs.pop()
     packed = refs.pop()
     n_prev, n_new = ROUNDS[index][0], len(ROUNDS[index])
     split = [tuple(refs[2 * k : 2 * k + 2]) for k in range(n_prev)]
@@ -186,7 +204,11 @@
     for both in split:
         blocks += [(both, j, first + j) for j in range(0, both[0].shape[1], SPAN)]
         first += both[0].shape[1]
-    place = {t: k for k, t in enumerate(round_tiles(index))}
+    kept = slots(round_tiles(index))
+    singles = sum(len(keys) == 1 for keys in kept)
+    place = {key: (k, keys.index(key)) for k, keys in enumerate(kept) for key in keys}
+    down, along = square_iotas()
+    extra[...] = jnp.zeros_like(extra)
     base = sum(w for _, _, w in CHUNKS[:n_prev])
     for (th, tl), i, row in blocks:
         if row < base:
@@ -199,24 +221,32 @@
             for a in range(0, SPAN, TILE):
                 for b in range(0, SPAN, TILE):
                     key = ((row + a) // TILE, (col + b) // TILE)
-                    if key in place:
-                        packed[place[key]] = full[a : a + TILE, b : b + TILE]
-    spread_tiles(packed, outs, groups)
+                    if key not in place:
+                        continue
+                    slot, turn = place[key]
+                    tile = full[a : a + TILE, b : b + TILE]
+                    if turn:
+                        own = jnp.sum(jnp.where(down == along, tile, 0.0), axis=0, keepdims=True)
+                        extra[slot - singles : slot - singles + 1, :] = own
+                        tile = jnp.where(down >= along, packed[slot], tile)
+                    packed[slot] = tile
+    spread_tiles(packed, extra, outs, groups)
 
 
 def gram(arrays, prev, index, pairs):
     widths = [pieces[0].shape[1] for pieces in arrays]
     rows = arrays[0][0].shape[0] * len(arrays[0])
-    n = len(round_tiles(index))
+    tiles = round_tiles(index)
+    n = len(slots(tiles))
     groups = lax.axis_size("rows")
     flat = [h for both in prev for h in both] + [p for pieces in arrays for p in pieces]
-    outs = [shape((rows, w), bf16) for w in widths for _ in (0, 1)] + part_shapes(n, groups)
+    outs = [shape((rows, w), bf16) for w in widths for _ in (0, 1)] + part_shapes(tiles, groups)
     out = pl.pallas_call(
         functools.partial(gram_kernel, pairs, index, groups, [len(pieces) for pieces in arrays]),
         out_shape=outs,
         in_specs=[VMEM] * len(flat),
         out_specs=[VMEM] * len(outs),
-        scratch_shapes=[pltpu.VMEM((n, TILE, TILE), f32)],
+        scratch_shapes=[pltpu.VMEM((n, TILE, TILE), f32), pltpu.VMEM((8, TILE), f32)],
         compiler_params=params(20),
         cost_estimate=cost(10000 * n * TILE * TILE * rows, 8 * rows * sum(widths)),
         name="gram" + str(index),
@@ -261,20 +291,39 @@
     return lax.ppermute(x, "pair", ends + [(i, ((i + 1) ^ 1) - 1) for i in range(1, pairs - 1)])
 
 
-def load_tile(parts, t, tile_ref):
-    groups = len(parts)
-    if groups == 1:
-        return parts[0][t]
-    if groups != 4:
-        for part, place in zip(parts, paths(groups)):
-            size = part.shape[1]
-            tile_ref[pl.ds(pl.multiple_of(place * size, size), size), :] = part[t]
+def load_slot(parts, t, tile_ref):
+    size = TILE // len(parts)
+    pieces = [part[t * size : (t + 1) * size, :] for part in parts]
+    if len(parts) != 4:
+        for piece, place in zip(pieces, paths(len(parts))):
+            tile_ref[pl.ds(pl.multiple_of(place * size, size), size), :] = piece
         return tile_ref[...]
     row = lax.axis_index("rows")
     x_flip, y_flip = lax.rem(row, 2) == 1, lax.div(row, 2) == 1
-    a, b, c, d = (part[t] for part in parts)
+    a, b, c, d = pieces
     pieces = [jnp.where(x_flip, b, a), jnp.where(x_flip, a, b), jnp.where(y_flip, d, c), jnp.where(y_flip, c, d)]
     return jnp.concatenate(pieces, axis=0)
+
+
+def tile_reader(tiles, parts, tile_ref):
+    if len(parts) == 1:
+        return lambda key: parts[0][tiles.index(key)]
+    kept = slots(tiles)
+    singles = sum(len(keys) == 1 for keys in kept)
+    place = {key: (k, keys.index(key)) for k, keys in enumerate(kept) for key in keys}
+
+    def read(key):
+        slot, turn = place[key]
+        value = load_slot(parts, slot, tile_ref)
+        if len(kept[slot]) == 1:
+            return value
+        down, along = square_iotas()
+        if not turn:
+            return jnp.where(down >= along, value, value.T)
+        at = len(kept) * (TILE // len(parts)) + slot - singles
+        return jnp.where(down == along, parts[0][at : at + 1, :], jnp.where(down < along, value, value.T))
+
+    return read
 
 
 def diagonal_of(value):
@@ -288,11 +337,11 @@
     return [jnp.sum(part, axis=1, keepdims=True) for part in parts]
 
 
-def normalize_tiles(tiles, parts, tile_ref, s_row, s_col, n_hi, n_lo):
+def normalize_tiles(tiles, read, s_row, s_col, n_hi, n_lo):
     square = jnp.zeros((TILE, TILE), f32)
-    for t, (i, j) in enumerate(tiles):
+    for i, j in tiles:
         at, to = slice(i * TILE, (i + 1) * TILE), slice(j * TILE, (j + 1) * TILE)
-        normed = load_tile(parts, t, tile_ref) * s_col[i] * s_row[:, to]
+        normed = read((i, j)) * s_col[i] * s_row[:, to]
         n_hi[at, to], n_lo[at, to] = halves(normed)
         if i == j:
             square = square + normed * normed
@@ -305,13 +354,11 @@
 def early_kernel(tiles, n_parts, *refs):
     parts, (n_hi, n_lo, own, d_ref, square_ref, tile_ref) = refs[:n_parts], refs[n_parts:]
     width = n_hi.shape[0]
-    place = {key: t for t, key in enumerate(tiles)}
-    d_row = jnp.concatenate(
-        [diagonal_of(load_tile(parts, place[i, i], tile_ref)) for i in range(width // TILE)], axis=1
-    )
+    read = tile_reader(tiles, parts, tile_ref)
+    d_row = jnp.concatenate([diagonal_of(read((i, i))) for i in range(width // TILE)], axis=1)
     d_ref[...] = d_row
     s_row = lax.rsqrt(d_row)
-    square_ref[...] = normalize_tiles(tiles, parts, tile_ref, s_row, flip_line(s_row), n_hi, n_lo)
+    square_ref[...] = normalize_tiles(tiles, read, s_row, flip_line(s_row), n_hi, n_lo)
     for i in range(0, width, SPAN):
         band = slice(i, i + SPAN)
         own[band, :] = three(dot, (n_hi[band, :], n_lo[band, :]), (n_hi[...], n_lo[...]))
@@ -361,14 +408,14 @@
     if not last:
         d_out, f_out, tile_ref = refs
     width = n_hi.shape[0]
-    place = {key: t for t, key in enumerate(tiles)}
+    read = tile_reader(tiles, parts, tile_ref)
 
     d_parts = [block[3][...] for block in known]
     for i in range(blocks[-1][1] // TILE, width // TILE):
-        d_parts.append(diagonal_of(load_tile(parts, place[i, i], tile_ref)))
+        d_parts.append(diagonal_of(read((i, i))))
     d_row = jnp.concatenate(d_parts, axis=1)
     s_row = lax.rsqrt(d_row)
-    square = normalize_tiles(tiles, parts, tile_ref, s_row, flip_line(s_row), n_hi, n_lo)
+    square = normalize_tiles(tiles, read, s_row, flip_line(s_row), n_hi, n_lo)
     for (lo, hi), block in zip(blocks, known):
         n_hi[lo:hi, lo:hi] = block[0][...]
         n_lo[lo:hi, lo:hi] = block[1][...]
@@ -508,14 +555,20 @@
         for a in range(0, SPAN, TILE):
             for b in range(0, BLK, TILE):
                 packed[(i + a) // TILE * count + b // TILE] = full[a : a + TILE, b : b + TILE]
-    spread_tiles(packed, outs, groups)
+    spread_tiles(packed, None, outs, groups)
+
+
+def cross_tiles():
+    count = BLK // TILE
+    return [(count + i, j) for i in range(count) for j in range(count)]
 
 
 def cross(near, far):
     rows = near.shape[0]
-    n = (BLK // TILE) ** 2
+    tiles = cross_tiles()
+    n = len(tiles)
     groups = lax.axis_size("rows")
-    outs = [shape((rows, BLK), bf16)] * 4 + part_shapes(n, groups)
+    outs = [shape((rows, BLK), bf16)] * 4 + part_shapes(tiles, groups)
     out = pl.pallas_call(
         functools.partial(cross_kernel, groups),
         out_shape=outs,
@@ -598,7 +651,7 @@
     summed = sum_rows(parts)
     count = BLK // TILE
     known = [early(triangle(0, count), [tiles], BLK) for tiles in (near_gram, far_gram)]
-    crossing = [(count + i, j) for i in range(count) for j in range(count)]
+    crossing = cross_tiles()
     columns = [near_pair, far_pair]
     out_s, out_q = newton(crossing, summed, [(0, BLK), (BLK, 2 * BLK)], known, columns, True)
     far, near = swap_far(out_s, pairs), swap_near(out_q, pairs)

time: 184 us -> 181 us (0.984)
  waiting for transfers between devices: 64 us -> 57.3 us
  starting transfers between devices: 53.4 us -> 57.6 us
    ppermute x18, waiting for transfers between devices: 30.3 us -> 23.1 us  [flip_rows(): lax.ppermute(x, 'rows', [(i, i ^ mask) for i in range(lax.axis_size('rows...]
    ppermute x18, starting transfers between devices: 11.7 us -> 15.7 us  [flip_rows(): lax.ppermute(x, 'rows', [(i, i ^ mask) for i in range(lax.axis_size('rows...]
  transfers between devices with their start and end apart: 37 -> 37, of which waited for: 20 -> 16; matrix products, arithmetic and copies ran while one was open for 0% -> 0% of each run, Pallas kernels for 14% -> 14%
where the time goes in v2:
time: 181 us; the launch traced here: 178 us
  Pallas kernels  60.1 us (33%)
  starting transfers between devices  57.6 us (32%)
  waiting for transfers between devices  57.3 us (32%)
  local copies, waits for them, and re-layouts  2.25 us (1%)
    pallas_call x2, Pallas kernels, newton(): pl.pallas_call(functools.partial(newton_kernel, tiles, len(parts), blocks...  29.6 us
    ppermute x12, starting transfers between devices, around(): lax.ppermute(x, 'pair', [(i, (i + 2 * hop) % pairs) for i in range(pairs)])  25 us
    ppermute x18, waiting for transfers between devices, flip_rows(): lax.ppermute(x, 'rows', [(i, i ^ mask) for i in range(lax.axis_size('rows...  23.1 us
    ppermute x12, waiting for transfers between devices, around(): lax.ppermute(x, 'pair', [(i, (i + 2 * hop) % pairs) for i in range(pairs)])  22.2 us
    ppermute x18, starting transfers between devices, flip_rows(): lax.ppermute(x, 'rows', [(i, i ^ mask) for i in range(lax.axis_size('rows...  15.7 us
    pallas_call x1, Pallas kernels, powers(): pl.pallas_call(power_kernel, out_shape=[shape((width, width), bf16)] * 4,...  13.7 us
    ppermute x3, waiting for transfers between devices, swap_far(): lax.ppermute(x, 'pair', ends + [(i, (i + 1 ^ 1) - 1) for i in range(1, pa...  12 us
    ppermute x3, starting transfers between devices, swap_far(): lax.ppermute(x, 'pair', ends + [(i, (i + 1 ^ 1) - 1) for i in range(1, pa...  11 us
  transfers between devices with their start and end apart: 37, of which 16 were waited for; matrix products, arithmetic and copies ran while one was open for 0% of the time, Pallas kernels for 14%

profile of v2, /device:TPU:1, one launch (start us, length us, event | category | flops | bytes accessed | tf_op | source)
XLA Modules:
  0.0 178.1 jit_solution(16104026220099294059)
XLA Ops:
  0.0 1.6 copy-done
  3.6 2.7 %collective-permute-start = (f32[64,512]{1,0:T(8,128)S(1)}, f32[64,512]{1,0:T(8,128)S(1)}, u32[]{:S(2)}, u32[]{:S(2)}) collective-permute-start(f32[64,512]{1,0:T(8,128)S(1)} %get-tuple-element.103), channel_id=1, source_target_pairs={{0,8},{4,12},{8,16},{12,20},{16,24},{20,28},{24,0},{28,4},{1,9},{5... | collective-permute-start | bytes 393224 | tf_op jit(solution)/shard_map/ppermute | solution.py:586
  6.3 2.3 %collective-permute-start.1 = (f32[64,512]{1,0:T(8,128)S(1)}, f32[64,512]{1,0:T(8,128)S(1)}, u32[]{:S(2)}, u32[]{:S(2)}) collective-permute-start(f32[64,512]{1,0:T(8,128)S(1)} %get-tuple-element.104), channel_id=1, source_target_pairs={{0,16},{4,20},{8,24},{12,28},{16,0},{20,4},{24,8},{28,12},{1,17},{... | collective-permute-start | bytes 393224 | tf_op jit(solution)/shard_map/ppermute | solution.py:586
  13.4 4.7 %collective-permute-done.1.refs_2_ = f32[64,512]{1,0:T(8,128)S(1)} collective-permute-done((f32[64,512]{1,0:T(8,128)S(1)}, f32[64,512]{1,0:T(8,128)S(1)}, u32[]{:S(2)}, u32[]{:S(2)}) %collective-permute-start.1) | collective-permute-done | bytes 131104 | tf_op jit(solution)/shard_map/ppermute | solution.py:586
  18.2 2.5 %collective-permute-done.4.refs_5_ = f32[64,512]{1,0:T(8,128)S(1)} collective-permute-done((f32[64,512]{1,0:T(8,128)S(1)}, f32[64,512]{1,0:T(8,128)S(1)}, u32[]{:S(2)}, u32[]{:S(2)}) %collective-permute-start.4) | collective-permute-done | bytes 131104 | tf_op jit(solution)/shard_map/ppermute | solution.py:586
  20.7 6.7 %collective-permute-start.7 = (f32[128,256]{1,0:T(8,128)S(1)}, f32[128,256]{1,0:T(8,128)S(1)}, u32[]{:S(2)}, u32[]{:S(2)}) collective-permute-start(f32[128,256]{1,0:T(8,128)S(1)} %get-tuple-element.117), channel_id=1, source_target_pairs={{0,8},{4,12},{8,16},{12,20},{16,24},{20,28},{24,0},{28,4},{1,9},{5... | collective-permute-start | bytes 393224 | tf_op jit(solution)/shard_map/ppermute | solution.py:586
  27.4 1.9 %collective-permute-start.8 = (f32[128,256]{1,0:T(8,128)S(1)}, f32[128,256]{1,0:T(8,128)S(1)}, u32[]{:S(2)}, u32[]{:S(2)}) collective-permute-start(f32[128,256]{1,0:T(8,128)S(1)} %get-tuple-element.118), channel_id=1, source_target_pairs={{0,16},{4,20},{8,24},{12,28},{16,0},{20,4},{24,8},{28,12},{1,17},{... | collective-permute-start | bytes 393224 | tf_op jit(solution)/shard_map/ppermute | solution.py:586
  29.3 2.4 %collective-permute-start.9 = (f32[128,256]{1,0:T(8,128)S(1)}, f32[128,256]{1,0:T(8,128)S(1)}, u32[]{:S(2)}, u32[]{:S(2)}) collective-permute-start(f32[128,256]{1,0:T(8,128)S(1)} %get-tuple-element.119), channel_id=1, source_target_pairs={{0,24},{4,28},{8,0},{12,4},{16,8},{20,12},{24,16},{28,20},{1,25},{... | collective-permute-start | bytes 393224 | tf_op jit(solution)/shard_map/ppermute | solution.py:586
  32.0 8.4 %collective-permute-done.8.refs_10_ = f32[128,256]{1,0:T(8,128)S(1)} collective-permute-done((f32[128,256]{1,0:T(8,128)S(1)}, f32[128,256]{1,0:T(8,128)S(1)}, u32[]{:S(2)}, u32[]{:S(2)}) %collective-permute-start.8) | collective-permute-done | bytes 131104 | tf_op jit(solution)/shard_map/ppermute | solution.py:586
  40.5 1.9 %gram0.1 = (bf16[512,512]{1,0:T(8,128)(2,1)S(1)}, bf16[512,512]{1,0:T(8,128)(2,1)S(1)}, bf16[512,256]{1,0:T(8,128)(2,1)S(1)}, bf16[512,256]{1,0:T(8,128)(2,1)S(1...) custom-call(f32[64,512]{1,0:T(8,128)S(1)} %get-tuple-element.102.refs_0_, ...), custom_call_target="tpu_custom_call" | custom-call | flops 23592960000 | bytes 49152 | tf_op jit(solution)/shard_map/gram0/pallas_call | solution.py:244
  44.9 3.1 %collective-permute-start.10 = (f32[128,256]{1,0:T(8,128)S(1)}, f32[128,256]{1,0:T(8,128)S(1)}, u32[]{:S(2)}, u32[]{:S(2)}) collective-permute-start(f32[128,256]{1,0:T(8,128)S(1)} %get-tuple-element.133), channel_id=1, source_target_pairs={{0,8},{4,12},{8,16},{12,20},{16,24},{20,28},{24,0},{28,4},{1,9},{5... | collective-permute-start | bytes 393224 | tf_op jit(solution)/shard_map/ppermute | solution.py:586
  48.5 1.7 collective-permute-start.12
  51.4 1.3 collective-permute-start.17
  53.1 5.1 %collective-permute-done.11.refs_6_ = f32[128,256]{1,0:T(8,128)S(1)} collective-permute-done((f32[128,256]{1,0:T(8,128)S(1)}, f32[128,256]{1,0:T(8,128)S(1)}, u32[]{:S(2)}, u32[]{:S(2)}) %collective-permute-start.11) | collective-permute-done | bytes 131104 | tf_op jit(solution)/shard_map/ppermute | solution.py:586
  62.6 3.5 %collective-permute-done.13 = f32[456,128]{1,0:T(8,128)S(1)} collective-permute-done((f32[456,128]{1,0:T(8,128)S(1)}, f32[456,128]{1,0:T(8,128)S(1)}, u32[]{:S(2)}, u32[]{:S(2)}) %collective-permute-start.13) | collective-permute-done | bytes 233504 | tf_op jit(solution)/shard_map/ppermute | solution.py:259
  67.5 9.9 %collective-permute-done.19 = f32[456,128]{1,0:T(8,128)S(1)} collective-permute-done((f32[456,128]{1,0:T(8,128)S(1)}, f32[456,128]{1,0:T(8,128)S(1)}, u32[]{:S(2)}, u32[]{:S(2)}) %collective-permute-start.19) | collective-permute-done | bytes 233504 | tf_op jit(solution)/shard_map/ppermute | solution.py:259
  79.0 3.6 %early.3 = (bf16[768,768]{1,0:T(8,128)(2,1)S(1)}, bf16[768,768]{1,0:T(8,128)(2,1)S(1)}, f32[768,768]{1,0:T(8,128)S(1)}, f32[1,768]{1,0:T(1,128)S(1)}, f32[1,128]{1,0:T(1,128)S(1)}) custom-call(f32[584,128]{1,0:T(8,128)S(1)} %add.40.refs_0_, f32[584,128]{1,0:T(8,128)S(1)} %collective-permute-done.21.refs_1_, f32[584,128]{1,0:T(8,128)S(1)} %add.41.refs_2_, ...), custom_call_target="tpu_custom_call" | custom-call | flops 707788800 | bytes 73728 | tf_op jit(solution)/shard_map/early/pallas_call | solution.py:368
  84.0 16.2 %newton.2 = (f32[512,512]{1,0:T(8,128)S(1)}, f32[512,512]{1,0:T(8,128)S(1)}, bf16[1024,1024]{1,0:T(8,128)(2,1)S(1)}, bf16[1024,1024]{1,0:T(8,128)(2,1)S(1)}, bf1...) custom-call(f32[456,128]{1,0:T(8,128)S(1)} %add.42.refs_0_, ...), custom_call_target="tpu_custom_call" | custom-call | flops 100663296 | bytes 262144 | tf_op jit(solution)/shard_map/newton/pallas_call | solution.py:478
  100.2 3.1 %collective-permute-start.25 = (f32[512,512]{1,0:T(8,128)S(1)}, f32[512,512]{1,0:T(8,128)S(1)}, u32[]{:S(2)}, u32[]{:S(2)}) collective-permute-start(f32[512,512]{1,0:T(8,128)S(1)} %get-tuple-element.155), channel_id=1, source_target_pairs={{0,4},{4,0},{8,12},{12,8},{16,20},{20,16},{24,28},{28,24},{1,5},{5... | collective-permute-start | bytes 3145736 | tf_op jit(solution)/shard_map/ppermute | solution.py:286
  103.2 5.0 %collective-permute-start.26 = (f32[512,512]{1,0:T(8,128)S(1)}, f32[512,512]{1,0:T(8,128)S(1)}, u32[]{:S(2)}, u32[]{:S(2)}) collective-permute-start(f32[512,512]{1,0:T(8,128)S(1)} %get-tuple-element.156), channel_id=1, source_target_pairs={{0,0},{28,28},{4,8},{8,4},{12,16},{16,12},{20,24},{24,20},{1,1},{2... | collective-permute-start | bytes 3145736 | tf_op jit(solution)/shard_map/ppermute | solution.py:291
  108.2 13.7 %powers.1 = (bf16[1024,1024]{1,0:T(8,128)(2,1)S(1)}, bf16[1024,1024]{1,0:T(8,128)(2,1)S(1)}, bf16[1024,1024]{1,0:T(8,128)(2,1)S(1)}, bf16[1024,1024]{1,0:T(8,128)(2,1)S(1)}) custom-call(bf16[1024,1024]{1,0:T(8,128)(2,1)S(1)} %get-tuple-element.157.n_hi, bf16[1024,1024]{1,0:T(8,128)(2,1)S(1)} %get-tuple-element.158.n_lo, ...), custom_call_target="tpu_custom_call" | custom-call | flops 100663296 | bytes 262144 | tf_op jit(solution)/shard_map/powers/pallas_call | solution.py:507
  123.8 2.8 %next_grams.1 = (f32[10,128,128]{2,1,0:T(8,128)S(1)}, f32[10,128,128]{2,1,0:T(8,128)S(1)}) custom-call(bf16[1024,1024]{1,0:T(8,128)(2,1)S(1)} %get-tuple-element.176.p_hi, bf16[1024,1024]{1,0:T(8,128)(2,1)S(1)} %get-tuple-element.177.p_lo, bf16[1024,1024]{1,0:T(8,128)(2,1)S(1)} %get-tuple-element.178.t_hi, bf16[1024,1024]{1,0:T(8,128)(2,1)S(1)} %get-tuple-element.179.t_lo, ...), custom_call_target="tpu_custom_call" | custom-call | flops 25165824 | bytes 131072 | tf_op jit(solution)/shard_map/next_grams/pallas_call | solution.py:536
  126.6 3.0 %collective-permute-start.34 = (f32[10,128,128]{2,1,0:T(8,128)S(1)}, f32[10,128,128]{2,1,0:T(8,128)S(1)}, u32[]{:S(2)}, u32[]{:S(2)}) collective-permute-start(f32[10,128,128]{2,1,0:T(8,128)S(1)} %get-tuple-element.187), channel_id=1, source_target_pairs={{0,0},{28,28},{4,8},{8,4},{12,16},{16,12},{20,24},{24,20},{1,1},{2... | collective-permute-start | bytes 1966088 | tf_op jit(solution)/shard_map/ppermute | solution.py:291
  129.8 1.3 collective-permute-start.29
  132.2 5.0 %collective-permute-done.29 = f32[512,128]{1,0:T(8,128)S(1)} collective-permute-done((f32[512,128]{1,0:T(8,128)S(1)}, f32[512,128]{1,0:T(8,128)S(1)}, u32[]{:S(2)}, u32[]{:S(2)}) %collective-permute-start.29) | collective-permute-done | bytes 262176 | tf_op jit(solution)/shard_map/ppermute | solution.py:259
  138.5 1.3 collective-permute-start.32
  139.8 1.4 early.5
  141.2 1.4 early.4
  144.8 13.4 %newton.3 = (f32[512,512]{1,0:T(8,128)S(1)}, f32[512,512]{1,0:T(8,128)S(1)}) custom-call(f32[512,128]{1,0:T(8,128)S(1)} %add.46.refs_0_, f32[512,128]{1,0:T(8,128)S(1)} %collective-permute-done.30.refs_1_, f32[512,128]{1,0:T(8,128)S(1)} %add.47.refs_2_, f32[512,128]{1,0:T(8,128)S(1)} %collective-permute-done.32.refs_3_, ...), custom_call_target="tpu_custom_call" | custom-call | flops 100663296 | bytes 262144 | tf_op jit(solution)/shard_map/newton/pallas_call | solution.py:478
  158.2 2.6 %collective-permute-start.36 = (f32[512,512]{1,0:T(8,128)S(1)}, f32[512,512]{1,0:T(8,128)S(1)}, u32[]{:S(2)}, u32[]{:S(2)}) collective-permute-start(f32[512,512]{1,0:T(8,128)S(1)} %get-tuple-element.198), channel_id=1, source_target_pairs={{0,4},{4,0},{8,12},{12,8},{16,20},{20,16},{24,28},{28,24},{1,5},{5... | collective-permute-start | bytes 3145736 | tf_op jit(solution)/shard_map/ppermute | solution.py:286
  160.8 3.1 %collective-permute-start.35 = (f32[512,512]{1,0:T(8,128)S(1)}, f32[512,512]{1,0:T(8,128)S(1)}, u32[]{:S(2)}, u32[]{:S(2)}) collective-permute-start(f32[512,512]{1,0:T(8,128)S(1)} %get-tuple-element.197), channel_id=1, source_target_pairs={{0,0},{28,28},{4,8},{8,4},{12,16},{16,12},{20,24},{24,20},{1,1},{2... | collective-permute-start | bytes 3145736 | tf_op jit(solution)/shard_map/ppermute | solution.py:291
  164.9 12.0 %collective-permute-done.35.block = f32[512,512]{1,0:T(8,128)S(1)} collective-permute-done((f32[512,512]{1,0:T(8,128)S(1)}, f32[512,512]{1,0:T(8,128)S(1)}, u32[]{:S(2)}, u32[]{:S(2)}) %collective-permute-start.35) | collective-permute-done | bytes 1048608 | tf_op jit(solution)/shard_map/ppermute | solution.py:291
  (72 shorter events, 29.3 us)
Async XLA Ops:
  3.6 8.6 %collective-permute-start = (f32[64,512]{1,0:T(8,128)S(1)}, f32[64,512]{1,0:T(8,128)S(1)}, u32[]{:S(2)}, u32[]{:S(2)}) collective-permute-start(f32[64,512]{1,0:T(8,128)S(1)} %get-tuple-element.103), channel_id=1, source_target_pairs={{0,8},{4,12},{8,16},{12,20},{16,24},{20,28},{24,0},{28,4},{1,9},{5... | collective-permute-start | bytes 393224 | tf_op jit(solution)/shard_map/ppermute | solution.py:586
  6.3 11.8 %collective-permute-start.1 = (f32[64,512]{1,0:T(8,128)S(1)}, f32[64,512]{1,0:T(8,128)S(1)}, u32[]{:S(2)}, u32[]{:S(2)}) collective-permute-start(f32[64,512]{1,0:T(8,128)S(1)} %get-tuple-element.104), channel_id=1, source_target_pairs={{0,16},{4,20},{8,24},{12,28},{16,0},{20,4},{24,8},{28,12},{1,17},{... | collective-permute-start | bytes 393224 | tf_op jit(solution)/shard_map/ppermute | solution.py:586
  8.6 9.5 %collective-permute-start.2 = (f32[64,512]{1,0:T(8,128)S(1)}, f32[64,512]{1,0:T(8,128)S(1)}, u32[]{:S(2)}, u32[]{:S(2)}) collective-permute-start(f32[64,512]{1,0:T(8,128)S(1)} %get-tuple-element.105), channel_id=1, source_target_pairs={{0,24},{4,28},{8,0},{12,4},{16,8},{20,12},{24,16},{28,20},{1,25},{... | collective-permute-start | bytes 393224 | tf_op jit(solution)/shard_map/ppermute | solution.py:586
  9.8 10.8 %collective-permute-start.4 = (f32[64,512]{1,0:T(8,128)S(1)}, f32[64,512]{1,0:T(8,128)S(1)}, u32[]{:S(2)}, u32[]{:S(2)}) collective-permute-start(f32[64,512]{1,0:T(8,128)S(1)} %get-tuple-element.109), channel_id=1, source_target_pairs={{0,8},{4,12},{8,16},{12,20},{16,24},{20,28},{24,0},{28,4},{1,9},{5... | collective-permute-start | bytes 393224 | tf_op jit(solution)/shard_map/ppermute | solution.py:586
  10.3 21.8 %collective-permute-start.5 = (f32[64,512]{1,0:T(8,128)S(1)}, f32[64,512]{1,0:T(8,128)S(1)}, u32[]{:S(2)}, u32[]{:S(2)}) collective-permute-start(f32[64,512]{1,0:T(8,128)S(1)} %get-tuple-element.110), channel_id=1, source_target_pairs={{0,16},{4,20},{8,24},{12,28},{16,0},{20,4},{24,8},{28,12},{1,17},{... | collective-permute-start | bytes 393224 | tf_op jit(solution)/shard_map/ppermute | solution.py:586
  12.2 19.8 %collective-permute-start.6 = (f32[64,512]{1,0:T(8,128)S(1)}, f32[64,512]{1,0:T(8,128)S(1)}, u32[]{:S(2)}, u32[]{:S(2)}) collective-permute-start(f32[64,512]{1,0:T(8,128)S(1)} %get-tuple-element.111), channel_id=1, source_target_pairs={{0,24},{4,28},{8,0},{12,4},{16,8},{20,12},{24,16},{28,20},{1,25},{... | collective-permute-start | bytes 393224 | tf_op jit(solution)/shard_map/ppermute | solution.py:586
  20.7 11.4 %collective-permute-start.7 = (f32[128,256]{1,0:T(8,128)S(1)}, f32[128,256]{1,0:T(8,128)S(1)}, u32[]{:S(2)}, u32[]{:S(2)}) collective-permute-start(f32[128,256]{1,0:T(8,128)S(1)} %get-tuple-element.117), channel_id=1, source_target_pairs={{0,8},{4,12},{8,16},{12,20},{16,24},{20,28},{24,0},{28,4},{1,9},{5... | collective-permute-start | bytes 393224 | tf_op jit(solution)/shard_map/ppermute | solution.py:586
  27.4 13.1 %collective-permute-start.8 = (f32[128,256]{1,0:T(8,128)S(1)}, f32[128,256]{1,0:T(8,128)S(1)}, u32[]{:S(2)}, u32[]{:S(2)}) collective-permute-start(f32[128,256]{1,0:T(8,128)S(1)} %get-tuple-element.118), channel_id=1, source_target_pairs={{0,16},{4,20},{8,24},{12,28},{16,0},{20,4},{24,8},{28,12},{1,17},{... | collective-permute-start | bytes 393224 | tf_op jit(solution)/shard_map/ppermute | solution.py:586
  29.3 11.2 %collective-permute-start.9 = (f32[128,256]{1,0:T(8,128)S(1)}, f32[128,256]{1,0:T(8,128)S(1)}, u32[]{:S(2)}, u32[]{:S(2)}) collective-permute-start(f32[128,256]{1,0:T(8,128)S(1)} %get-tuple-element.119), channel_id=1, source_target_pairs={{0,24},{4,28},{8,0},{12,4},{16,8},{20,12},{24,16},{28,20},{1,25},{... | collective-permute-start | bytes 393224 | tf_op jit(solution)/shard_map/ppermute | solution.py:586
  42.3 8.2 %collective-permute-start.15 = (f32[584,128]{1,0:T(8,128)S(1)}, f32[584,128]{1,0:T(8,128)S(1)}, u32[]{:S(2)}, u32[]{:S(2)}) collective-permute-start(f32[584,128]{1,0:T(8,128)S(1)} %get-tuple-element.129), channel_id=1, source_target_pairs={{0,1},{1,0},{2,3},{3,2},{4,5},{5,4},{6,7},{7,6},{8,9},{9,8},{10,11... | collective-permute-start | bytes 897032 | tf_op jit(solution)/shard_map/ppermute | solution.py:259
  43.6 7.8 %collective-permute-start.16 = (f32[584,128]{1,0:T(8,128)S(1)}, f32[584,128]{1,0:T(8,128)S(1)}, u32[]{:S(2)}, u32[]{:S(2)}) collective-permute-start(f32[584,128]{1,0:T(8,128)S(1)} %get-tuple-element.131), channel_id=1, source_target_pairs={{0,2},{1,3},{2,0},{3,1},{4,6},{5,7},{6,4},{7,5},{8,10},{9,11},{10,... | collective-permute-start | bytes 897032 | tf_op jit(solution)/shard_map/ppermute | solution.py:259
  44.9 8.3 %collective-permute-start.10 = (f32[128,256]{1,0:T(8,128)S(1)}, f32[128,256]{1,0:T(8,128)S(1)}, u32[]{:S(2)}, u32[]{:S(2)}) collective-permute-start(f32[128,256]{1,0:T(8,128)S(1)} %get-tuple-element.133), channel_id=1, source_target_pairs={{0,8},{4,12},{8,16},{12,20},{16,24},{20,28},{24,0},{28,4},{1,9},{5... | collective-permute-start | bytes 393224 | tf_op jit(solution)/shard_map/ppermute | solution.py:586
  47.9 10.2 %collective-permute-start.11 = (f32[128,256]{1,0:T(8,128)S(1)}, f32[128,256]{1,0:T(8,128)S(1)}, u32[]{:S(2)}, u32[]{:S(2)}) collective-permute-start(f32[128,256]{1,0:T(8,128)S(1)} %get-tuple-element.134), channel_id=1, source_target_pairs={{0,16},{4,20},{8,24},{12,28},{16,0},{20,4},{24,8},{28,12},{1,17},{... | collective-permute-start | bytes 393224 | tf_op jit(solution)/shard_map/ppermute | solution.py:586
  48.5 9.7 %collective-permute-start.12 = (f32[128,256]{1,0:T(8,128)S(1)}, f32[128,256]{1,0:T(8,128)S(1)}, u32[]{:S(2)}, u32[]{:S(2)}) collective-permute-start(f32[128,256]{1,0:T(8,128)S(1)} %get-tuple-element.135), channel_id=1, source_target_pairs={{0,24},{4,28},{8,0},{12,4},{16,8},{20,12},{24,16},{28,20},{1,25},{... | collective-permute-start | bytes 393224 | tf_op jit(solution)/shard_map/ppermute | solution.py:586
  51.4 8.5 %collective-permute-start.17 = (f32[584,128]{1,0:T(8,128)S(1)}, f32[584,128]{1,0:T(8,128)S(1)}, u32[]{:S(2)}, u32[]{:S(2)}) collective-permute-start(f32[584,128]{1,0:T(8,128)S(1)} %add.38), channel_id=1, source_target_pairs={{0,2},{1,3},{2,0},{3,1},{4,6},{5,7},{6,4},{7,5},{8,10},{9,11},{10,... | collective-permute-start | bytes 897032 | tf_op jit(solution)/shard_map/ppermute | solution.py:259
  52.8 7.2 %collective-permute-start.18 = (f32[584,128]{1,0:T(8,128)S(1)}, f32[584,128]{1,0:T(8,128)S(1)}, u32[]{:S(2)}, u32[]{:S(2)}) collective-permute-start(f32[584,128]{1,0:T(8,128)S(1)} %add.39), channel_id=1, source_target_pairs={{0,1},{1,0},{2,3},{3,2},{4,5},{5,4},{6,7},{7,6},{8,9},{9,8},{10,11... | collective-permute-start | bytes 897032 | tf_op jit(solution)/shard_map/ppermute | solution.py:259
  59.4 6.6 %collective-permute-start.13 = (f32[456,128]{1,0:T(8,128)S(1)}, f32[456,128]{1,0:T(8,128)S(1)}, u32[]{:S(2)}, u32[]{:S(2)}) collective-permute-start(f32[456,128]{1,0:T(8,128)S(1)} %get-tuple-element.137), channel_id=1, source_target_pairs={{0,1},{1,0},{2,3},{3,2},{4,5},{5,4},{6,7},{7,6},{8,9},{9,8},{10,11... | collective-permute-start | bytes 700424 | tf_op jit(solution)/shard_map/ppermute | solution.py:259
  59.7 6.3 %collective-permute-start.14 = (f32[456,128]{1,0:T(8,128)S(1)}, f32[456,128]{1,0:T(8,128)S(1)}, u32[]{:S(2)}, u32[]{:S(2)}) collective-permute-start(f32[456,128]{1,0:T(8,128)S(1)} %get-tuple-element.139), channel_id=1, source_target_pairs={{0,2},{1,3},{2,0},{3,1},{4,6},{5,7},{6,4},{7,5},{8,10},{9,11},{10,... | collective-permute-start | bytes 700424 | tf_op jit(solution)/shard_map/ppermute | solution.py:259
  60.1 17.4 %collective-permute-start.21 = (f32[584,128]{1,0:T(8,128)S(1)}, f32[584,128]{1,0:T(8,128)S(1)}, u32[]{:S(2)}, u32[]{:S(2)}) collective-permute-start(f32[584,128]{1,0:T(8,128)S(1)} %add.40.refs_0_), channel_id=1, source_target_pairs={{0,1},{1,0},{2,3},{3,2},{4,5},{5,4},{6,7},{7,6},{8,9},{9,8},{10,11... | collective-permute-start | bytes 897032 | tf_op jit(solution)/shard_map/ppermute | solution.py:259
  61.3 16.2 %collective-permute-start.22 = (f32[584,128]{1,0:T(8,128)S(1)}, f32[584,128]{1,0:T(8,128)S(1)}, u32[]{:S(2)}, u32[]{:S(2)}) collective-permute-start(f32[584,128]{1,0:T(8,128)S(1)} %add.41.refs_2_), channel_id=1, source_target_pairs={{0,2},{1,3},{2,0},{3,1},{4,6},{5,7},{6,4},{7,5},{8,10},{9,11},{10,... | collective-permute-start | bytes 897032 | tf_op jit(solution)/shard_map/ppermute | solution.py:259
  66.1 11.3 %collective-permute-start.19 = (f32[456,128]{1,0:T(8,128)S(1)}, f32[456,128]{1,0:T(8,128)S(1)}, u32[]{:S(2)}, u32[]{:S(2)}) collective-permute-start(f32[456,128]{1,0:T(8,128)S(1)} %add.36), channel_id=1, source_target_pairs={{0,2},{1,3},{2,0},{3,1},{4,6},{5,7},{6,4},{7,5},{8,10},{9,11},{10,... | collective-permute-start | bytes 700424 | tf_op jit(solution)/shard_map/ppermute | solution.py:259
  66.4 11.0 %collective-permute-start.20 = (f32[456,128]{1,0:T(8,128)S(1)}, f32[456,128]{1,0:T(8,128)S(1)}, u32[]{:S(2)}, u32[]{:S(2)}) collective-permute-start(f32[456,128]{1,0:T(8,128)S(1)} %add.37), channel_id=1, source_target_pairs={{0,1},{1,0},{2,3},{3,2},{4,5},{5,4},{6,7},{7,6},{8,9},{9,8},{10,11... | collective-permute-start | bytes 700424 | tf_op jit(solution)/shard_map/ppermute | solution.py:259
  100.2 21.7 %collective-permute-start.25 = (f32[512,512]{1,0:T(8,128)S(1)}, f32[512,512]{1,0:T(8,128)S(1)}, u32[]{:S(2)}, u32[]{:S(2)}) collective-permute-start(f32[512,512]{1,0:T(8,128)S(1)} %get-tuple-element.155), channel_id=1, source_target_pairs={{0,4},{4,0},{8,12},{12,8},{16,20},{20,16},{24,28},{28,24},{1,5},{5... | collective-permute-start | bytes 3145736 | tf_op jit(solution)/shard_map/ppermute | solution.py:286
  103.2 18.6 %collective-permute-start.26 = (f32[512,512]{1,0:T(8,128)S(1)}, f32[512,512]{1,0:T(8,128)S(1)}, u32[]{:S(2)}, u32[]{:S(2)}) collective-permute-start(f32[512,512]{1,0:T(8,128)S(1)} %get-tuple-element.156), channel_id=1, source_target_pairs={{0,0},{28,28},{4,8},{8,4},{12,16},{16,12},{20,24},{24,20},{1,1},{2... | collective-permute-start | bytes 3145736 | tf_op jit(solution)/shard_map/ppermute | solution.py:291
  123.2 6.5 %collective-permute-start.27 = (f32[512,128]{1,0:T(8,128)S(1)}, f32[512,128]{1,0:T(8,128)S(1)}, u32[]{:S(2)}, u32[]{:S(2)}) collective-permute-start(f32[512,128]{1,0:T(8,128)S(1)} %get-tuple-element.171), channel_id=1, source_target_pairs={{0,1},{1,0},{2,3},{3,2},{4,5},{5,4},{6,7},{7,6},{8,9},{9,8},{10,11... | collective-permute-start | bytes 786440 | tf_op jit(solution)/shard_map/ppermute | solution.py:259
  126.6 13.2 %collective-permute-start.34 = (f32[10,128,128]{2,1,0:T(8,128)S(1)}, f32[10,128,128]{2,1,0:T(8,128)S(1)}, u32[]{:S(2)}, u32[]{:S(2)}) collective-permute-start(f32[10,128,128]{2,1,0:T(8,128)S(1)} %get-tuple-element.187), channel_id=1, source_target_pairs={{0,0},{28,28},{4,8},{8,4},{12,16},{16,12},{20,24},{24,20},{1,1},{2... | collective-permute-start | bytes 1966088 | tf_op jit(solution)/shard_map/ppermute | solution.py:291
  129.6 11.6 %collective-permute-start.33 = (f32[10,128,128]{2,1,0:T(8,128)S(1)}, f32[10,128,128]{2,1,0:T(8,128)S(1)}, u32[]{:S(2)}, u32[]{:S(2)}) collective-permute-start(f32[10,128,128]{2,1,0:T(8,128)S(1)} %get-tuple-element.181), channel_id=1, source_target_pairs={{0,4},{4,0},{8,12},{12,8},{16,20},{20,16},{24,28},{28,24},{1,5},{5... | collective-permute-start | bytes 1966088 | tf_op jit(solution)/shard_map/ppermute | solution.py:286
  129.8 7.5 %collective-permute-start.29 = (f32[512,128]{1,0:T(8,128)S(1)}, f32[512,128]{1,0:T(8,128)S(1)}, u32[]{:S(2)}, u32[]{:S(2)}) collective-permute-start(f32[512,128]{1,0:T(8,128)S(1)} %add.44), channel_id=1, source_target_pairs={{0,2},{1,3},{2,0},{3,1},{4,6},{5,7},{6,4},{7,5},{8,10},{9,11},{10,... | collective-permute-start | bytes 786440 | tf_op jit(solution)/shard_map/ppermute | solution.py:259
  131.1 7.4 %collective-permute-start.31 = (f32[512,128]{1,0:T(8,128)S(1)}, f32[512,128]{1,0:T(8,128)S(1)}, u32[]{:S(2)}, u32[]{:S(2)}) collective-permute-start(f32[512,128]{1,0:T(8,128)S(1)} %add.45), channel_id=1, source_target_pairs={{0,1},{1,0},{2,3},{3,2},{4,5},{5,4},{6,7},{7,6},{8,9},{9,8},{10,11... | collective-permute-start | bytes 786440 | tf_op jit(solution)/shard_map/ppermute | solution.py:259
  137.2 6.5 %collective-permute-start.30 = (f32[512,128]{1,0:T(8,128)S(1)}, f32[512,128]{1,0:T(8,128)S(1)}, u32[]{:S(2)}, u32[]{:S(2)}) collective-permute-start(f32[512,128]{1,0:T(8,128)S(1)} %add.46.refs_0_), channel_id=1, source_target_pairs={{0,1},{1,0},{2,3},{3,2},{4,5},{5,4},{6,7},{7,6},{8,9},{9,8},{10,11... | collective-permute-start | bytes 786440 | tf_op jit(solution)/shard_map/ppermute | solution.py:259
  138.5 6.3 %collective-permute-start.32 = (f32[512,128]{1,0:T(8,128)S(1)}, f32[512,128]{1,0:T(8,128)S(1)}, u32[]{:S(2)}, u32[]{:S(2)}) collective-permute-start(f32[512,128]{1,0:T(8,128)S(1)} %add.47.refs_2_), channel_id=1, source_target_pairs={{0,2},{1,3},{2,0},{3,1},{4,6},{5,7},{6,4},{7,5},{8,10},{9,11},{10,... | collective-permute-start | bytes 786440 | tf_op jit(solution)/shard_map/ppermute | solution.py:259
  160.8 16.1 %collective-permute-start.35 = (f32[512,512]{1,0:T(8,128)S(1)}, f32[512,512]{1,0:T(8,128)S(1)}, u32[]{:S(2)}, u32[]{:S(2)}) collective-permute-start(f32[512,512]{1,0:T(8,128)S(1)} %get-tuple-element.197), channel_id=1, source_target_pairs={{0,0},{28,28},{4,8},{8,4},{12,16},{16,12},{20,24},{24,20},{1,1},{2... | collective-permute-start | bytes 3145736 | tf_op jit(solution)/shard_map/ppermute | solution.py:291
  (7 other events, 31.0 us)

commit v3 on v2

--- a/solution.py
+++ b/solution.py
@@ -10,6 +10,7 @@
 BLK = 512
 TILE = 128
 SPAN = 256
+BAND = 512
 
 epsilon = 1e-06
 f32 = jnp.float32
@@ -449,8 +450,8 @@
         b_hi[band, :], b_lo[band, :] = halves(product - 6.0 * scaled + jnp.where(here, 5.0, 0.0))
     swapped = lax.axis_index("pair") == 0
     s_at, q_at = ends(last)
-    for i in range(0, out_s.shape[0], SPAN):
-        band = slice(i, i + SPAN)
+    for i in range(0, out_s.shape[0], BAND):
+        band = slice(i, i + BAND)
         high, low = columns_band(columns, band)
         w = halves(three(dot, (high, low), (a_hi[...], a_lo[...])))
         plain = (high.astype(f32) + low.astype(f32)) * scale
@@ -490,14 +491,14 @@
 def power_kernel(n_hi, n_lo, a_hi, a_lo, b_hi, b_lo, d_ref, p_hi, p_lo, t_hi, t_lo):
     width = n_hi.shape[0]
     d_col = flip_line(d_ref[...])
-    for i in range(0, width, SPAN):
-        band = slice(i, i + SPAN)
-        here = lax.broadcasted_iota(jnp.int32, (SPAN, width), 0) + i == lax.broadcasted_iota(jnp.int32, (SPAN, width), 1)
-        root = jnp.sqrt(jnp.concatenate(d_col[i // TILE : (i + SPAN) // TILE], axis=0))
+    for i in range(0, width, BAND):
+        band = slice(i, i + BAND)
+        here = lax.broadcasted_iota(jnp.int32, (BAND, width), 0) + i == lax.broadcasted_iota(jnp.int32, (BAND, width), 1)
+        root = jnp.sqrt(jnp.concatenate(d_col[i // TILE : (i + BAND) // TILE], axis=0))
         value = three(dot, (a_hi[band, :], a_lo[band, :]), (b_hi[...], b_lo[...]))
         p_hi[band, :], p_lo[band, :] = halves(value * (0.125 * root) + jnp.where(here, 2.0, 0.0))
-    for i in range(0, width, SPAN):
-        band = slice(i, i + SPAN)
+    for i in range(0, width, BAND):
+        band = slice(i, i + BAND)
         value = three(dot, (n_hi[band, :], n_lo[band, :]), (p_hi[...], p_lo[...]))
         t_hi[band, :], t_lo[band, :] = halves(value)
 

time: 181 us -> 178 us (0.983)
  Pallas kernels: 60.1 us -> 56.2 us
    pallas_call x2, Pallas kernels: 29.6 us -> 26 us  [newton(): pl.pallas_call(functools.partial(newton_kernel, tiles, len(parts), blocks...]
  transfers between devices with their start and end apart: 37 -> 37, of which waited for: 16 -> 17; matrix products, arithmetic and copies ran while one was open for 0% -> 0% of each run, Pallas kernels for 14% -> 14%
where the time goes in v3:
time: 178 us; the launch traced here: 175 us
  starting transfers between devices  57.8 us (32%)
  waiting for transfers between devices  57.4 us (32%)
  Pallas kernels  56.2 us (32%)
  local copies, waits for them, and re-layouts  2.25 us (1%)
    pallas_call x2, Pallas kernels, newton(): pl.pallas_call(functools.partial(newton_kernel, tiles, len(parts), blocks...  26 us
    ppermute x12, starting transfers between devices, around(): lax.ppermute(x, 'pair', [(i, (i + 2 * hop) % pairs) for i in range(pairs)])  24.9 us
    ppermute x18, waiting for transfers between devices, flip_rows(): lax.ppermute(x, 'rows', [(i, i ^ mask) for i in range(lax.axis_size('rows...  23.2 us
    ppermute x12, waiting for transfers between devices, around(): lax.ppermute(x, 'pair', [(i, (i + 2 * hop) % pairs) for i in range(pairs)])  22.2 us
    ppermute x18, starting transfers between devices, flip_rows(): lax.ppermute(x, 'rows', [(i, i ^ mask) for i in range(lax.axis_size('rows...  15.8 us
    pallas_call x1, Pallas kernels, powers(): pl.pallas_call(power_kernel, out_shape=[shape((width, width), bf16)] * 4,...  13.5 us
    ppermute x3, waiting for transfers between devices, swap_far(): lax.ppermute(x, 'pair', ends + [(i, (i + 1 ^ 1) - 1) for i in range(1, pa...  12 us
    ppermute x3, starting transfers between devices, swap_far(): lax.ppermute(x, 'pair', ends + [(i, (i + 1 ^ 1) - 1) for i in range(1, pa...  11.3 us
  transfers between devices with their start and end apart: 37, of which 17 were waited for; matrix products, arithmetic and copies ran while one was open for 0% of the time, Pallas kernels for 14%

profile of v3, /device:TPU:1, one launch (start us, length us, event | category | flops | bytes accessed | tf_op | source)
XLA Modules:
  0.0 174.6 jit_solution(18126157205238101958)
XLA Ops:
  0.0 1.6 copy-done
  3.6 2.7 %collective-permute-start = (f32[64,512]{1,0:T(8,128)S(1)}, f32[64,512]{1,0:T(8,128)S(1)}, u32[]{:S(2)}, u32[]{:S(2)}) collective-permute-start(f32[64,512]{1,0:T(8,128)S(1)} %get-tuple-element.103), channel_id=1, source_target_pairs={{0,8},{4,12},{8,16},{12,20},{16,24},{20,28},{24,0},{28,4},{1,9},{5... | collective-permute-start | bytes 393224 | tf_op jit(solution)/shard_map/ppermute | solution.py:587
  6.3 2.3 %collective-permute-start.1 = (f32[64,512]{1,0:T(8,128)S(1)}, f32[64,512]{1,0:T(8,128)S(1)}, u32[]{:S(2)}, u32[]{:S(2)}) collective-permute-start(f32[64,512]{1,0:T(8,128)S(1)} %get-tuple-element.104), channel_id=1, source_target_pairs={{0,16},{4,20},{8,24},{12,28},{16,0},{20,4},{24,8},{28,12},{1,17},{... | collective-permute-start | bytes 393224 | tf_op jit(solution)/shard_map/ppermute | solution.py:587
  13.4 4.7 %collective-permute-done.1.refs_2_ = f32[64,512]{1,0:T(8,128)S(1)} collective-permute-done((f32[64,512]{1,0:T(8,128)S(1)}, f32[64,512]{1,0:T(8,128)S(1)}, u32[]{:S(2)}, u32[]{:S(2)}) %collective-permute-start.1) | collective-permute-done | bytes 131104 | tf_op jit(solution)/shard_map/ppermute | solution.py:587
  18.2 2.5 %collective-permute-done.4.refs_5_ = f32[64,512]{1,0:T(8,128)S(1)} collective-permute-done((f32[64,512]{1,0:T(8,128)S(1)}, f32[64,512]{1,0:T(8,128)S(1)}, u32[]{:S(2)}, u32[]{:S(2)}) %collective-permute-start.4) | collective-permute-done | bytes 131104 | tf_op jit(solution)/shard_map/ppermute | solution.py:587
  20.7 6.7 %collective-permute-start.7 = (f32[128,256]{1,0:T(8,128)S(1)}, f32[128,256]{1,0:T(8,128)S(1)}, u32[]{:S(2)}, u32[]{:S(2)}) collective-permute-start(f32[128,256]{1,0:T(8,128)S(1)} %get-tuple-element.117), channel_id=1, source_target_pairs={{0,8},{4,12},{8,16},{12,20},{16,24},{20,28},{24,0},{28,4},{1,9},{5... | collective-permute-start | bytes 393224 | tf_op jit(solution)/shard_map/ppermute | solution.py:587
  27.4 1.9 %collective-permute-start.8 = (f32[128,256]{1,0:T(8,128)S(1)}, f32[128,256]{1,0:T(8,128)S(1)}, u32[]{:S(2)}, u32[]{:S(2)}) collective-permute-start(f32[128,256]{1,0:T(8,128)S(1)} %get-tuple-element.118), channel_id=1, source_target_pairs={{0,16},{4,20},{8,24},{12,28},{16,0},{20,4},{24,8},{28,12},{1,17},{... | collective-permute-start | bytes 393224 | tf_op jit(solution)/shard_map/ppermute | solution.py:587
  29.3 2.4 %collective-permute-start.9 = (f32[128,256]{1,0:T(8,128)S(1)}, f32[128,256]{1,0:T(8,128)S(1)}, u32[]{:S(2)}, u32[]{:S(2)}) collective-permute-start(f32[128,256]{1,0:T(8,128)S(1)} %get-tuple-element.119), channel_id=1, source_target_pairs={{0,24},{4,28},{8,0},{12,4},{16,8},{20,12},{24,16},{28,20},{1,25},{... | collective-permute-start | bytes 393224 | tf_op jit(solution)/shard_map/ppermute | solution.py:587
  32.0 8.4 %collective-permute-done.8.refs_10_ = f32[128,256]{1,0:T(8,128)S(1)} collective-permute-done((f32[128,256]{1,0:T(8,128)S(1)}, f32[128,256]{1,0:T(8,128)S(1)}, u32[]{:S(2)}, u32[]{:S(2)}) %collective-permute-start.8) | collective-permute-done | bytes 131104 | tf_op jit(solution)/shard_map/ppermute | solution.py:587
  40.5 1.9 %gram0.1 = (bf16[512,512]{1,0:T(8,128)(2,1)S(1)}, bf16[512,512]{1,0:T(8,128)(2,1)S(1)}, bf16[512,256]{1,0:T(8,128)(2,1)S(1)}, bf16[512,256]{1,0:T(8,128)(2,1)S(1...) custom-call(f32[64,512]{1,0:T(8,128)S(1)} %get-tuple-element.102.refs_0_, ...), custom_call_target="tpu_custom_call" | custom-call | flops 23592960000 | bytes 49152 | tf_op jit(solution)/shard_map/gram0/pallas_call | solution.py:245
  44.9 3.1 %collective-permute-start.10 = (f32[128,256]{1,0:T(8,128)S(1)}, f32[128,256]{1,0:T(8,128)S(1)}, u32[]{:S(2)}, u32[]{:S(2)}) collective-permute-start(f32[128,256]{1,0:T(8,128)S(1)} %get-tuple-element.133), channel_id=1, source_target_pairs={{0,8},{4,12},{8,16},{12,20},{16,24},{20,28},{24,0},{28,4},{1,9},{5... | collective-permute-start | bytes 393224 | tf_op jit(solution)/shard_map/ppermute | solution.py:587
  48.5 1.6 collective-permute-start.12
  51.4 1.3 collective-permute-start.17
  53.1 5.1 %collective-permute-done.11.refs_6_ = f32[128,256]{1,0:T(8,128)S(1)} collective-permute-done((f32[128,256]{1,0:T(8,128)S(1)}, f32[128,256]{1,0:T(8,128)S(1)}, u32[]{:S(2)}, u32[]{:S(2)}) %collective-permute-start.11) | collective-permute-done | bytes 131104 | tf_op jit(solution)/shard_map/ppermute | solution.py:587
  60.1 1.3 collective-permute-start.21
  62.6 3.5 %collective-permute-done.13 = f32[456,128]{1,0:T(8,128)S(1)} collective-permute-done((f32[456,128]{1,0:T(8,128)S(1)}, f32[456,128]{1,0:T(8,128)S(1)}, u32[]{:S(2)}, u32[]{:S(2)}) %collective-permute-start.13) | collective-permute-done | bytes 233504 | tf_op jit(solution)/shard_map/ppermute | solution.py:260
  67.6 9.8 %collective-permute-done.19 = f32[456,128]{1,0:T(8,128)S(1)} collective-permute-done((f32[456,128]{1,0:T(8,128)S(1)}, f32[456,128]{1,0:T(8,128)S(1)}, u32[]{:S(2)}, u32[]{:S(2)}) %collective-permute-start.19) | collective-permute-done | bytes 233504 | tf_op jit(solution)/shard_map/ppermute | solution.py:260
  79.1 3.6 %early.3 = (bf16[768,768]{1,0:T(8,128)(2,1)S(1)}, bf16[768,768]{1,0:T(8,128)(2,1)S(1)}, f32[768,768]{1,0:T(8,128)S(1)}, f32[1,768]{1,0:T(1,128)S(1)}, f32[1,128]{1,0:T(1,128)S(1)}) custom-call(f32[584,128]{1,0:T(8,128)S(1)} %add.40.refs_0_, f32[584,128]{1,0:T(8,128)S(1)} %collective-permute-done.21.refs_1_, f32[584,128]{1,0:T(8,128)S(1)} %add.41.refs_2_, ...), custom_call_target="tpu_custom_call" | custom-call | flops 707788800 | bytes 73728 | tf_op jit(solution)/shard_map/early/pallas_call | solution.py:369
  84.0 12.9 %newton.2 = (f32[512,512]{1,0:T(8,128)S(1)}, f32[512,512]{1,0:T(8,128)S(1)}, bf16[1024,1024]{1,0:T(8,128)(2,1)S(1)}, bf16[1024,1024]{1,0:T(8,128)(2,1)S(1)}, bf1...) custom-call(f32[456,128]{1,0:T(8,128)S(1)} %add.42.refs_0_, ...), custom_call_target="tpu_custom_call" | custom-call | flops 100663296 | bytes 262144 | tf_op jit(solution)/shard_map/newton/pallas_call | solution.py:479
  96.9 3.0 %collective-permute-start.25 = (f32[512,512]{1,0:T(8,128)S(1)}, f32[512,512]{1,0:T(8,128)S(1)}, u32[]{:S(2)}, u32[]{:S(2)}) collective-permute-start(f32[512,512]{1,0:T(8,128)S(1)} %get-tuple-element.155), channel_id=1, source_target_pairs={{0,4},{4,0},{8,12},{12,8},{16,20},{20,16},{24,28},{28,24},{1,5},{5... | collective-permute-start | bytes 3145736 | tf_op jit(solution)/shard_map/ppermute | solution.py:287
  99.9 5.0 %collective-permute-start.26 = (f32[512,512]{1,0:T(8,128)S(1)}, f32[512,512]{1,0:T(8,128)S(1)}, u32[]{:S(2)}, u32[]{:S(2)}) collective-permute-start(f32[512,512]{1,0:T(8,128)S(1)} %get-tuple-element.156), channel_id=1, source_target_pairs={{0,0},{28,28},{4,8},{8,4},{12,16},{16,12},{20,24},{24,20},{1,1},{2... | collective-permute-start | bytes 3145736 | tf_op jit(solution)/shard_map/ppermute | solution.py:292
  104.9 13.5 %powers.1 = (bf16[1024,1024]{1,0:T(8,128)(2,1)S(1)}, bf16[1024,1024]{1,0:T(8,128)(2,1)S(1)}, bf16[1024,1024]{1,0:T(8,128)(2,1)S(1)}, bf16[1024,1024]{1,0:T(8,128)(2,1)S(1)}) custom-call(bf16[1024,1024]{1,0:T(8,128)(2,1)S(1)} %get-tuple-element.157.n_hi, bf16[1024,1024]{1,0:T(8,128)(2,1)S(1)} %get-tuple-element.158.n_lo, ...), custom_call_target="tpu_custom_call" | custom-call | flops 100663296 | bytes 262144 | tf_op jit(solution)/shard_map/powers/pallas_call | solution.py:508
  120.3 2.6 %next_grams.1 = (f32[10,128,128]{2,1,0:T(8,128)S(1)}, f32[10,128,128]{2,1,0:T(8,128)S(1)}) custom-call(bf16[1024,1024]{1,0:T(8,128)(2,1)S(1)} %get-tuple-element.176.p_hi, bf16[1024,1024]{1,0:T(8,128)(2,1)S(1)} %get-tuple-element.177.p_lo, bf16[1024,1024]{1,0:T(8,128)(2,1)S(1)} %get-tuple-element.178.t_hi, bf16[1024,1024]{1,0:T(8,128)(2,1)S(1)} %get-tuple-element.179.t_lo, ...), custom_call_target="tpu_custom_call" | custom-call | flops 25165824 | bytes 131072 | tf_op jit(solution)/shard_map/next_grams/pallas_call | solution.py:537
  123.0 3.3 %collective-permute-start.34 = (f32[10,128,128]{2,1,0:T(8,128)S(1)}, f32[10,128,128]{2,1,0:T(8,128)S(1)}, u32[]{:S(2)}, u32[]{:S(2)}) collective-permute-start(f32[10,128,128]{2,1,0:T(8,128)S(1)} %get-tuple-element.187), channel_id=1, source_target_pairs={{0,0},{28,28},{4,8},{8,4},{12,16},{16,12},{20,24},{24,20},{1,1},{2... | collective-permute-start | bytes 1966088 | tf_op jit(solution)/shard_map/ppermute | solution.py:292
  126.5 1.3 collective-permute-start.29
  128.9 5.0 %collective-permute-done.29 = f32[512,128]{1,0:T(8,128)S(1)} collective-permute-done((f32[512,128]{1,0:T(8,128)S(1)}, f32[512,128]{1,0:T(8,128)S(1)}, u32[]{:S(2)}, u32[]{:S(2)}) %collective-permute-start.29) | collective-permute-done | bytes 262176 | tf_op jit(solution)/shard_map/ppermute | solution.py:260
  136.5 1.4 early.5
  137.9 1.4 early.4
  141.5 13.2 %newton.3 = (f32[512,512]{1,0:T(8,128)S(1)}, f32[512,512]{1,0:T(8,128)S(1)}) custom-call(f32[512,128]{1,0:T(8,128)S(1)} %add.46.refs_0_, f32[512,128]{1,0:T(8,128)S(1)} %collective-permute-done.30.refs_1_, f32[512,128]{1,0:T(8,128)S(1)} %add.47.refs_2_, f32[512,128]{1,0:T(8,128)S(1)} %collective-permute-done.32.refs_3_, ...), custom_call_target="tpu_custom_call" | custom-call | flops 100663296 | bytes 262144 | tf_op jit(solution)/shard_map/newton/pallas_call | solution.py:479
  154.7 2.6 %collective-permute-start.36 = (f32[512,512]{1,0:T(8,128)S(1)}, f32[512,512]{1,0:T(8,128)S(1)}, u32[]{:S(2)}, u32[]{:S(2)}) collective-permute-start(f32[512,512]{1,0:T(8,128)S(1)} %get-tuple-element.198), channel_id=1, source_target_pairs={{0,4},{4,0},{8,12},{12,8},{16,20},{20,16},{24,28},{28,24},{1,5},{5... | collective-permute-start | bytes 3145736 | tf_op jit(solution)/shard_map/ppermute | solution.py:287
  157.3 3.1 %collective-permute-start.35 = (f32[512,512]{1,0:T(8,128)S(1)}, f32[512,512]{1,0:T(8,128)S(1)}, u32[]{:S(2)}, u32[]{:S(2)}) collective-permute-start(f32[512,512]{1,0:T(8,128)S(1)} %get-tuple-element.197), channel_id=1, source_target_pairs={{0,0},{28,28},{4,8},{8,4},{12,16},{16,12},{20,24},{24,20},{1,1},{2... | collective-permute-start | bytes 3145736 | tf_op jit(solution)/shard_map/ppermute | solution.py:292
  161.4 12.0 %collective-permute-done.35.block = f32[512,512]{1,0:T(8,128)S(1)} collective-permute-done((f32[512,512]{1,0:T(8,128)S(1)}, f32[512,512]{1,0:T(8,128)S(1)}, u32[]{:S(2)}, u32[]{:S(2)}) %collective-permute-start.35) | collective-permute-done | bytes 1048608 | tf_op jit(solution)/shard_map/ppermute | solution.py:292
  (72 shorter events, 29.4 us)
Async XLA Ops:
  3.6 8.6 %collective-permute-start = (f32[64,512]{1,0:T(8,128)S(1)}, f32[64,512]{1,0:T(8,128)S(1)}, u32[]{:S(2)}, u32[]{:S(2)}) collective-permute-start(f32[64,512]{1,0:T(8,128)S(1)} %get-tuple-element.103), channel_id=1, source_target_pairs={{0,8},{4,12},{8,16},{12,20},{16,24},{20,28},{24,0},{28,4},{1,9},{5... | collective-permute-start | bytes 393224 | tf_op jit(solution)/shard_map/ppermute | solution.py:587
  6.3 11.8 %collective-permute-start.1 = (f32[64,512]{1,0:T(8,128)S(1)}, f32[64,512]{1,0:T(8,128)S(1)}, u32[]{:S(2)}, u32[]{:S(2)}) collective-permute-start(f32[64,512]{1,0:T(8,128)S(1)} %get-tuple-element.104), channel_id=1, source_target_pairs={{0,16},{4,20},{8,24},{12,28},{16,0},{20,4},{24,8},{28,12},{1,17},{... | collective-permute-start | bytes 393224 | tf_op jit(solution)/shard_map/ppermute | solution.py:587
  8.6 9.5 %collective-permute-start.2 = (f32[64,512]{1,0:T(8,128)S(1)}, f32[64,512]{1,0:T(8,128)S(1)}, u32[]{:S(2)}, u32[]{:S(2)}) collective-permute-start(f32[64,512]{1,0:T(8,128)S(1)} %get-tuple-element.105), channel_id=1, source_target_pairs={{0,24},{4,28},{8,0},{12,4},{16,8},{20,12},{24,16},{28,20},{1,25},{... | collective-permute-start | bytes 393224 | tf_op jit(solution)/shard_map/ppermute | solution.py:587
  9.8 10.8 %collective-permute-start.4 = (f32[64,512]{1,0:T(8,128)S(1)}, f32[64,512]{1,0:T(8,128)S(1)}, u32[]{:S(2)}, u32[]{:S(2)}) collective-permute-start(f32[64,512]{1,0:T(8,128)S(1)} %get-tuple-element.109), channel_id=1, source_target_pairs={{0,8},{4,12},{8,16},{12,20},{16,24},{20,28},{24,0},{28,4},{1,9},{5... | collective-permute-start | bytes 393224 | tf_op jit(solution)/shard_map/ppermute | solution.py:587
  10.3 21.8 %collective-permute-start.5 = (f32[64,512]{1,0:T(8,128)S(1)}, f32[64,512]{1,0:T(8,128)S(1)}, u32[]{:S(2)}, u32[]{:S(2)}) collective-permute-start(f32[64,512]{1,0:T(8,128)S(1)} %get-tuple-element.110), channel_id=1, source_target_pairs={{0,16},{4,20},{8,24},{12,28},{16,0},{20,4},{24,8},{28,12},{1,17},{... | collective-permute-start | bytes 393224 | tf_op jit(solution)/shard_map/ppermute | solution.py:587
  12.2 19.8 %collective-permute-start.6 = (f32[64,512]{1,0:T(8,128)S(1)}, f32[64,512]{1,0:T(8,128)S(1)}, u32[]{:S(2)}, u32[]{:S(2)}) collective-permute-start(f32[64,512]{1,0:T(8,128)S(1)} %get-tuple-element.111), channel_id=1, source_target_pairs={{0,24},{4,28},{8,0},{12,4},{16,8},{20,12},{24,16},{28,20},{1,25},{... | collective-permute-start | bytes 393224 | tf_op jit(solution)/shard_map/ppermute | solution.py:587
  20.7 11.4 %collective-permute-start.7 = (f32[128,256]{1,0:T(8,128)S(1)}, f32[128,256]{1,0:T(8,128)S(1)}, u32[]{:S(2)}, u32[]{:S(2)}) collective-permute-start(f32[128,256]{1,0:T(8,128)S(1)} %get-tuple-element.117), channel_id=1, source_target_pairs={{0,8},{4,12},{8,16},{12,20},{16,24},{20,28},{24,0},{28,4},{1,9},{5... | collective-permute-start | bytes 393224 | tf_op jit(solution)/shard_map/ppermute | solution.py:587
  27.4 13.1 %collective-permute-start.8 = (f32[128,256]{1,0:T(8,128)S(1)}, f32[128,256]{1,0:T(8,128)S(1)}, u32[]{:S(2)}, u32[]{:S(2)}) collective-permute-start(f32[128,256]{1,0:T(8,128)S(1)} %get-tuple-element.118), channel_id=1, source_target_pairs={{0,16},{4,20},{8,24},{12,28},{16,0},{20,4},{24,8},{28,12},{1,17},{... | collective-permute-start | bytes 393224 | tf_op jit(solution)/shard_map/ppermute | solution.py:587
  29.3 11.2 %collective-permute-start.9 = (f32[128,256]{1,0:T(8,128)S(1)}, f32[128,256]{1,0:T(8,128)S(1)}, u32[]{:S(2)}, u32[]{:S(2)}) collective-permute-start(f32[128,256]{1,0:T(8,128)S(1)} %get-tuple-element.119), channel_id=1, source_target_pairs={{0,24},{4,28},{8,0},{12,4},{16,8},{20,12},{24,16},{28,20},{1,25},{... | collective-permute-start | bytes 393224 | tf_op jit(solution)/shard_map/ppermute | solution.py:587
  42.3 8.2 %collective-permute-start.15 = (f32[584,128]{1,0:T(8,128)S(1)}, f32[584,128]{1,0:T(8,128)S(1)}, u32[]{:S(2)}, u32[]{:S(2)}) collective-permute-start(f32[584,128]{1,0:T(8,128)S(1)} %get-tuple-element.129), channel_id=1, source_target_pairs={{0,1},{1,0},{2,3},{3,2},{4,5},{5,4},{6,7},{7,6},{8,9},{9,8},{10,11... | collective-permute-start | bytes 897032 | tf_op jit(solution)/shard_map/ppermute | solution.py:260
  43.6 7.8 %collective-permute-start.16 = (f32[584,128]{1,0:T(8,128)S(1)}, f32[584,128]{1,0:T(8,128)S(1)}, u32[]{:S(2)}, u32[]{:S(2)}) collective-permute-start(f32[584,128]{1,0:T(8,128)S(1)} %get-tuple-element.131), channel_id=1, source_target_pairs={{0,2},{1,3},{2,0},{3,1},{4,6},{5,7},{6,4},{7,5},{8,10},{9,11},{10,... | collective-permute-start | bytes 897032 | tf_op jit(solution)/shard_map/ppermute | solution.py:260
  44.9 8.3 %collective-permute-start.10 = (f32[128,256]{1,0:T(8,128)S(1)}, f32[128,256]{1,0:T(8,128)S(1)}, u32[]{:S(2)}, u32[]{:S(2)}) collective-permute-start(f32[128,256]{1,0:T(8,128)S(1)} %get-tuple-element.133), channel_id=1, source_target_pairs={{0,8},{4,12},{8,16},{12,20},{16,24},{20,28},{24,0},{28,4},{1,9},{5... | collective-permute-start | bytes 393224 | tf_op jit(solution)/shard_map/ppermute | solution.py:587
  47.9 10.2 %collective-permute-start.11 = (f32[128,256]{1,0:T(8,128)S(1)}, f32[128,256]{1,0:T(8,128)S(1)}, u32[]{:S(2)}, u32[]{:S(2)}) collective-permute-start(f32[128,256]{1,0:T(8,128)S(1)} %get-tuple-element.134), channel_id=1, source_target_pairs={{0,16},{4,20},{8,24},{12,28},{16,0},{20,4},{24,8},{28,12},{1,17},{... | collective-permute-start | bytes 393224 | tf_op jit(solution)/shard_map/ppermute | solution.py:587
  48.5 9.7 %collective-permute-start.12 = (f32[128,256]{1,0:T(8,128)S(1)}, f32[128,256]{1,0:T(8,128)S(1)}, u32[]{:S(2)}, u32[]{:S(2)}) collective-permute-start(f32[128,256]{1,0:T(8,128)S(1)} %get-tuple-element.135), channel_id=1, source_target_pairs={{0,24},{4,28},{8,0},{12,4},{16,8},{20,12},{24,16},{28,20},{1,25},{... | collective-permute-start | bytes 393224 | tf_op jit(solution)/shard_map/ppermute | solution.py:587
  51.4 8.5 %collective-permute-start.17 = (f32[584,128]{1,0:T(8,128)S(1)}, f32[584,128]{1,0:T(8,128)S(1)}, u32[]{:S(2)}, u32[]{:S(2)}) collective-permute-start(f32[584,128]{1,0:T(8,128)S(1)} %add.38), channel_id=1, source_target_pairs={{0,2},{1,3},{2,0},{3,1},{4,6},{5,7},{6,4},{7,5},{8,10},{9,11},{10,... | collective-permute-start | bytes 897032 | tf_op jit(solution)/shard_map/ppermute | solution.py:260
  52.8 7.3 %collective-permute-start.18 = (f32[584,128]{1,0:T(8,128)S(1)}, f32[584,128]{1,0:T(8,128)S(1)}, u32[]{:S(2)}, u32[]{:S(2)}) collective-permute-start(f32[584,128]{1,0:T(8,128)S(1)} %add.39), channel_id=1, source_target_pairs={{0,1},{1,0},{2,3},{3,2},{4,5},{5,4},{6,7},{7,6},{8,9},{9,8},{10,11... | collective-permute-start | bytes 897032 | tf_op jit(solution)/shard_map/ppermute | solution.py:260
  59.4 6.7 %collective-permute-start.13 = (f32[456,128]{1,0:T(8,128)S(1)}, f32[456,128]{1,0:T(8,128)S(1)}, u32[]{:S(2)}, u32[]{:S(2)}) collective-permute-start(f32[456,128]{1,0:T(8,128)S(1)} %get-tuple-element.137), channel_id=1, source_target_pairs={{0,1},{1,0},{2,3},{3,2},{4,5},{5,4},{6,7},{7,6},{8,9},{9,8},{10,11... | collective-permute-start | bytes 700424 | tf_op jit(solution)/shard_map/ppermute | solution.py:260
  59.7 6.4 %collective-permute-start.14 = (f32[456,128]{1,0:T(8,128)S(1)}, f32[456,128]{1,0:T(8,128)S(1)}, u32[]{:S(2)}, u32[]{:S(2)}) collective-permute-start(f32[456,128]{1,0:T(8,128)S(1)} %get-tuple-element.139), channel_id=1, source_target_pairs={{0,2},{1,3},{2,0},{3,1},{4,6},{5,7},{6,4},{7,5},{8,10},{9,11},{10,... | collective-permute-start | bytes 700424 | tf_op jit(solution)/shard_map/ppermute | solution.py:260
  60.1 17.5 %collective-permute-start.21 = (f32[584,128]{1,0:T(8,128)S(1)}, f32[584,128]{1,0:T(8,128)S(1)}, u32[]{:S(2)}, u32[]{:S(2)}) collective-permute-start(f32[584,128]{1,0:T(8,128)S(1)} %add.40.refs_0_), channel_id=1, source_target_pairs={{0,1},{1,0},{2,3},{3,2},{4,5},{5,4},{6,7},{7,6},{8,9},{9,8},{10,11... | collective-permute-start | bytes 897032 | tf_op jit(solution)/shard_map/ppermute | solution.py:260
  61.3 16.2 %collective-permute-start.22 = (f32[584,128]{1,0:T(8,128)S(1)}, f32[584,128]{1,0:T(8,128)S(1)}, u32[]{:S(2)}, u32[]{:S(2)}) collective-permute-start(f32[584,128]{1,0:T(8,128)S(1)} %add.41.refs_2_), channel_id=1, source_target_pairs={{0,2},{1,3},{2,0},{3,1},{4,6},{5,7},{6,4},{7,5},{8,10},{9,11},{10,... | collective-permute-start | bytes 897032 | tf_op jit(solution)/shard_map/ppermute | solution.py:260
  66.2 11.2 %collective-permute-start.19 = (f32[456,128]{1,0:T(8,128)S(1)}, f32[456,128]{1,0:T(8,128)S(1)}, u32[]{:S(2)}, u32[]{:S(2)}) collective-permute-start(f32[456,128]{1,0:T(8,128)S(1)} %add.36), channel_id=1, source_target_pairs={{0,2},{1,3},{2,0},{3,1},{4,6},{5,7},{6,4},{7,5},{8,10},{9,11},{10,... | collective-permute-start | bytes 700424 | tf_op jit(solution)/shard_map/ppermute | solution.py:260
  66.5 11.0 %collective-permute-start.20 = (f32[456,128]{1,0:T(8,128)S(1)}, f32[456,128]{1,0:T(8,128)S(1)}, u32[]{:S(2)}, u32[]{:S(2)}) collective-permute-start(f32[456,128]{1,0:T(8,128)S(1)} %add.37), channel_id=1, source_target_pairs={{0,1},{1,0},{2,3},{3,2},{4,5},{5,4},{6,7},{7,6},{8,9},{9,8},{10,11... | collective-permute-start | bytes 700424 | tf_op jit(solution)/shard_map/ppermute | solution.py:260
  96.9 21.5 %collective-permute-start.25 = (f32[512,512]{1,0:T(8,128)S(1)}, f32[512,512]{1,0:T(8,128)S(1)}, u32[]{:S(2)}, u32[]{:S(2)}) collective-permute-start(f32[512,512]{1,0:T(8,128)S(1)} %get-tuple-element.155), channel_id=1, source_target_pairs={{0,4},{4,0},{8,12},{12,8},{16,20},{20,16},{24,28},{28,24},{1,5},{5... | collective-permute-start | bytes 3145736 | tf_op jit(solution)/shard_map/ppermute | solution.py:287
  99.9 18.5 %collective-permute-start.26 = (f32[512,512]{1,0:T(8,128)S(1)}, f32[512,512]{1,0:T(8,128)S(1)}, u32[]{:S(2)}, u32[]{:S(2)}) collective-permute-start(f32[512,512]{1,0:T(8,128)S(1)} %get-tuple-element.156), channel_id=1, source_target_pairs={{0,0},{28,28},{4,8},{8,4},{12,16},{16,12},{20,24},{24,20},{1,1},{2... | collective-permute-start | bytes 3145736 | tf_op jit(solution)/shard_map/ppermute | solution.py:292
  119.7 6.7 %collective-permute-start.27 = (f32[512,128]{1,0:T(8,128)S(1)}, f32[512,128]{1,0:T(8,128)S(1)}, u32[]{:S(2)}, u32[]{:S(2)}) collective-permute-start(f32[512,128]{1,0:T(8,128)S(1)} %get-tuple-element.171), channel_id=1, source_target_pairs={{0,1},{1,0},{2,3},{3,2},{4,5},{5,4},{6,7},{7,6},{8,9},{9,8},{10,11... | collective-permute-start | bytes 786440 | tf_op jit(solution)/shard_map/ppermute | solution.py:260
  120.1 6.3 %collective-permute-start.28 = (f32[512,128]{1,0:T(8,128)S(1)}, f32[512,128]{1,0:T(8,128)S(1)}, u32[]{:S(2)}, u32[]{:S(2)}) collective-permute-start(f32[512,128]{1,0:T(8,128)S(1)} %get-tuple-element.173), channel_id=1, source_target_pairs={{0,2},{1,3},{2,0},{3,1},{4,6},{5,7},{6,4},{7,5},{8,10},{9,11},{10,... | collective-permute-start | bytes 786440 | tf_op jit(solution)/shard_map/ppermute | solution.py:260
  123.0 13.5 %collective-permute-start.34 = (f32[10,128,128]{2,1,0:T(8,128)S(1)}, f32[10,128,128]{2,1,0:T(8,128)S(1)}, u32[]{:S(2)}, u32[]{:S(2)}) collective-permute-start(f32[10,128,128]{2,1,0:T(8,128)S(1)} %get-tuple-element.187), channel_id=1, source_target_pairs={{0,0},{28,28},{4,8},{8,4},{12,16},{16,12},{20,24},{24,20},{1,1},{2... | collective-permute-start | bytes 1966088 | tf_op jit(solution)/shard_map/ppermute | solution.py:292
  126.3 11.6 %collective-permute-start.33 = (f32[10,128,128]{2,1,0:T(8,128)S(1)}, f32[10,128,128]{2,1,0:T(8,128)S(1)}, u32[]{:S(2)}, u32[]{:S(2)}) collective-permute-start(f32[10,128,128]{2,1,0:T(8,128)S(1)} %get-tuple-element.181), channel_id=1, source_target_pairs={{0,4},{4,0},{8,12},{12,8},{16,20},{20,16},{24,28},{28,24},{1,5},{5... | collective-permute-start | bytes 1966088 | tf_op jit(solution)/shard_map/ppermute | solution.py:287
  126.5 7.5 %collective-permute-start.29 = (f32[512,128]{1,0:T(8,128)S(1)}, f32[512,128]{1,0:T(8,128)S(1)}, u32[]{:S(2)}, u32[]{:S(2)}) collective-permute-start(f32[512,128]{1,0:T(8,128)S(1)} %add.44), channel_id=1, source_target_pairs={{0,2},{1,3},{2,0},{3,1},{4,6},{5,7},{6,4},{7,5},{8,10},{9,11},{10,... | collective-permute-start | bytes 786440 | tf_op jit(solution)/shard_map/ppermute | solution.py:260
  127.8 7.4 %collective-permute-start.31 = (f32[512,128]{1,0:T(8,128)S(1)}, f32[512,128]{1,0:T(8,128)S(1)}, u32[]{:S(2)}, u32[]{:S(2)}) collective-permute-start(f32[512,128]{1,0:T(8,128)S(1)} %add.45), channel_id=1, source_target_pairs={{0,1},{1,0},{2,3},{3,2},{4,5},{5,4},{6,7},{7,6},{8,9},{9,8},{10,11... | collective-permute-start | bytes 786440 | tf_op jit(solution)/shard_map/ppermute | solution.py:260
  134.0 6.5 %collective-permute-start.30 = (f32[512,128]{1,0:T(8,128)S(1)}, f32[512,128]{1,0:T(8,128)S(1)}, u32[]{:S(2)}, u32[]{:S(2)}) collective-permute-start(f32[512,128]{1,0:T(8,128)S(1)} %add.46.refs_0_), channel_id=1, source_target_pairs={{0,1},{1,0},{2,3},{3,2},{4,5},{5,4},{6,7},{7,6},{8,9},{9,8},{10,11... | collective-permute-start | bytes 786440 | tf_op jit(solution)/shard_map/ppermute | solution.py:260
  157.3 16.1 %collective-permute-start.35 = (f32[512,512]{1,0:T(8,128)S(1)}, f32[512,512]{1,0:T(8,128)S(1)}, u32[]{:S(2)}, u32[]{:S(2)}) collective-permute-start(f32[512,512]{1,0:T(8,128)S(1)} %get-tuple-element.197), channel_id=1, source_target_pairs={{0,0},{28,28},{4,8},{8,4},{12,16},{16,12},{20,24},{24,20},{1,1},{2... | collective-permute-start | bytes 3145736 | tf_op jit(solution)/shard_map/ppermute | solution.py:292
  (7 other events, 31.1 us)
